TPU v7x, 32 devices: a whole 2x2x4 slice. The times are simulated.
32 devices in a mesh: pole: 2 (over y), prow: 4 (over z), pcol: 4 (over x, core).
Axes of the slice: x: 2, y: 2, z: 4, core: 2. Of those that a mesh axis runs over, the one named last changes fastest.
Arguments:
- known: float32 [8192, 4096], P(('pole', 'prow'), 'pcol'), parts along dimension 0, may hold values from -0.09375 to 0.09375
- lower_two: float32 [8192, 256], P(('pole', 'prow', 'pcol')), parts along dimension 0, may hold values from -0.5 to 0.5
- lower_one: float32 [8192, 256], P(('pole', 'prow', 'pcol')), parts along dimension 0, may hold values from -0.5 to 0.5
- top_one: float32 [512, 256], P('pole'), parts along dimension 0, may hold values from -0.375 to 0.375
- inner_two: float32 [512, 256], P('pole'), parts along dimension 0, may hold values from -6 to 6
- inner_one: float32 [512, 256], P('pole'), parts along dimension 0, may hold values from -6 to 6
- heights: int32 [16], replicated, may hold values from 128 to 256, as said below
- pattern_two: int32 [16], replicated, may hold values 0 or 1
- pattern_one: int32 [16], replicated, may hold values 0 or 1
Outputs:
- column_two: float32 [8192, 256], P(('pole', 'prow', 'pcol')), parts along dimension 0
- diag_two: float32 [512, 256], P('pole'), parts along dimension 0
- column_one: float32 [8192, 256], P(('pole', 'prow', 'pcol')), parts along dimension 0
- cross_block: float32 [512, 256], P('pole'), parts along dimension 0
- diag_one: float32 [512, 256], P('pole'), parts along dimension 0
There are 2 independent parts, one for each index of `pole`. A program takes and returns all parts, laid end to end along the dimension named above; an argument that names none is the same for every part. Nothing has to cross between parts.
Inputs may be any that keep to these rules, and one draw needn't show every extreme that they name: `heights`: live rows of each block; some block has all 256 rows live.
All inputs are finite; a program needn't handle non-finite values.
Results may differ from a plain program's by a relative error of at most 0.000071.
Values sent between devices are 32-bit elements; how exact they have to be, the bound alone decides.
No kernel may reach another device: no remote copies, remote signals or barrier semaphores. Data moves between devices by JAX's collectives and lax.ppermute only.
A program may use at most 64 MiB of HBM per device.

v0:
```python
import jax
import jax.numpy as jnp
from jax import lax
from jax.sharding import PartitionSpec as P


def spread_2(array, axis, root):
    mine = lax.axis_index(axis) == root
    return lax.psum(jnp.where(mine, array, jnp.zeros_like(array)), axis)


def product(left, right):
    return jnp.dot(left, right, precision=lax.Precision.HIGHEST, preferred_element_type=jnp.float32)


def contract(left, right):
    return lax.dot_general(
        left,
        right,
        (((0,), (0,)), ((), ())),
        precision=lax.Precision.HIGHEST,
        preferred_element_type=jnp.float32,
    )


def per_device(
    known, lower_two, lower_one, top_one, inner_two, inner_one, heights, pattern_two, pattern_one
):
    width = top_one.shape[0]
    piece = lower_two.shape[0]
    n_col = lax.axis_size("pcol")
    ratio = lax.axis_size("prow") // n_col
    row_index = lax.axis_index("prow")
    col_index = lax.axis_index("pcol")
    live = (jnp.arange(width)[None, :] < heights[:, None]).astype(jnp.float32).reshape(-1)
    own_start = (row_index * n_col + col_index) * piece
    own_live = lax.dynamic_slice_in_dim(live, own_start, piece)

    def mask_own(lower, pattern):
        keep = live * jnp.repeat(pattern.astype(jnp.float32), width)
        return lower * lax.dynamic_slice_in_dim(keep, own_start, piece)[:, None]

    def spread(own_rows):
        band = lax.all_gather(own_rows, "pcol", axis=0, tiled=True)
        needed = jnp.concatenate(
            [spread_2(band, "prow", col_index * ratio + offset) for offset in range(ratio)], axis=0
        )
        return (band, needed)

    def total_rows(partial_value):
        return lax.psum_scatter(partial_value, "pcol", scatter_dimension=0, tiled=True)

    def total_terms(terms):
        return lax.psum(terms, ("prow", "pcol"))

    own_two = mask_own(lower_two, pattern_two)
    own_one = mask_own(lower_one, pattern_one)
    band_two, needed_two = spread(own_two)
    band_one, needed_one = spread(own_one)
    partial_two = product(known, needed_two)
    partial_one = product(known, needed_one)
    lows_two, lows_one = (own_two, own_one)
    column_two = -(own_live[:, None] * total_rows(partial_two))
    first_term, second_term = total_terms(
        (contract(lows_two, column_two), contract(column_two, lows_one))
    )
    diag_two = inner_two - first_term
    cross_block = -(second_term + product(diag_two, top_one))
    column_one = -(own_live[:, None] * (total_rows(partial_one) + product(column_two, top_one)))
    (third_term,) = total_terms((contract(lows_one, column_one),))
    diag_one = inner_one - third_term - contract(top_one, cross_block)
    return (column_two, diag_two, column_one, cross_block, diag_one)


def solution(mesh):
    return jax.shard_map(
        per_device,
        mesh=mesh,
        in_specs=(
            P(("pole", "prow"), "pcol"),
            P(("pole", "prow", "pcol"), None),
            P(("pole", "prow", "pcol"), None),
            P("pole", None),
            P("pole", None),
            P("pole", None),
            P(),
            P(),
            P(),
        ),
        out_specs=(
            P(("pole", "prow", "pcol"), None),
            P("pole", None),
            P(("pole", "prow", "pcol"), None),
            P("pole", None),
            P("pole", None),
        ),
        check_vma=False,
    )
```

profile of v0, /device:TPU:0, one launch (start us, length us, event | category | flops | bytes accessed | tf_op | source)
XLA Modules:
  0.0 309.8 jit_solution(9019047215438995695)
XLA Ops:
  7.2 0.7 convert_element_type.15
  7.9 0.7 convert_element_type.16
  8.6 0.7 select_bitcast_fusion
  9.3 0.1 dynamic_slice.11
  9.4 1.8 broadcast_multiply_fusion
  11.2 0.0 all-gather.3.cloned.1.call-start
  11.2 0.1 dynamic_slice.10
  11.3 1.8 broadcast_multiply_fusion.1
  13.2 17.6 %all-gather.5.cloned.1.call-done = f32[1024,256]{1,0:T(8,128)} async-done(((f32[256,256]{1,0:T(8,128)}), f32[1024,256]{1,0:T(8,128)}) %all-gather.5.cloned.1.call-update) | async-done | bytes 1048592 | tf_op jit(solution)/shard_map/all_gather | solution.py:44
  30.8 2.3 broadcast_select_fusion
  33.0 16.6 %all-gather.3.cloned.1.call-done = f32[1024,256]{1,0:T(8,128)} async-done(((f32[256,256]{1,0:T(8,128)}), f32[1024,256]{1,0:T(8,128)}) %all-gather.3.cloned.1.call-update) | async-done | bytes 1048592 | tf_op jit(solution)/shard_map/all_gather | solution.py:44
  49.6 2.3 broadcast_select_fusion.1
  52.0 0.0 reduce-scatter.3.cloned.1.call-start
  52.0 87.1 %all-reduce.7.cloned.1.call-done = (f32[1024,256]{1,0:T(8,128)}, f32[1024,256]{1,0:T(8,128)}) async-done(((f32[1024,256]{1,0:T(8,128)}, f32[1024,256]{1,0:T(8,128)}), (f32[1024,256]{1,0:T(8,128)}, f32[1024,256]{1,0:T(8,128)})) %all-reduce.7.cloned.1.call-update) | async-done | bytes 2097168 | tf_op jit(solution)/shard_map/psum | solution.py:9
  139.2 10.4 %convolution_bitcast_fusion.1 = f32[1024,256]{0,1:T(8,128)} fusion(f32[1024,256]{1,0:T(8,128)} %get-tuple-element.13, f32[1024,1024]{1,0:T(8,128)} %param.9), kind=kOutput, calls=%fused_computation.1 | convolution fusion | flops 3221225472 | bytes 6291456 | tf_op jit(solution)/shard_map/dot_general | solution.py:13
  149.6 0.2 reduce-scatter.5.cloned.1.call-start
  149.8 10.0 %convolution_bitcast_fusion = f32[1024,256]{0,1:T(8,128)} fusion(f32[1024,256]{1,0:T(8,128)S(1)} %copy-done.5, f32[1024,1024]{1,0:T(8,128)} %param.9), kind=kOutput, calls=%fused_computation | convolution fusion | flops 3221225472 | bytes 6291456 | tf_op jit(solution)/shard_map/dot_general | solution.py:13
  159.9 0.1 convert_bitcast_fusion
  160.0 0.1 dynamic_slice.9
  160.1 13.5 %reduce-scatter.3.cloned.1.call-done = f32[256,256]{0,1:T(8,128)} async-done(((f32[1024,256]{0,1:T(8,128)}), f32[256,256]{0,1:T(8,128)}) %reduce-scatter.3.cloned.1.call-update) | async-done | bytes 262160 | tf_op jit(solution)/shard_map/reduce_scatter | solution.py:51
  173.6 1.0 multiply_negate_fusion
  174.5 1.1 fusion.5
  175.6 1.3 fusion.4
  176.9 23.9 %reduce-scatter.5.cloned.1.call-done = f32[256,256]{0,1:T(8,128)} async-done(((f32[1024,256]{0,1:T(8,128)}), f32[256,256]{0,1:T(8,128)}) %reduce-scatter.5.cloned.1.call-update) | async-done | bytes 262160 | tf_op jit(solution)/shard_map/reduce_scatter | solution.py:51
  200.9 1.5 fusion.3
  202.4 1.3 fusion.6
  203.7 0.8 copy.17
  204.6 0.8 copy.16
  205.4 92.7 %all-reduce.5.cloned.1.call-done = (f32[256,256]{1,0:T(8,128)}, f32[256,256]{1,0:T(8,128)}, f32[256,256]{1,0:T(8,128)}) async-done(((f32[256,256]{1,0:T(8,128)}, f32[256,256]{1,0:T(8,128)}, f32[256,256]{1,0:T(8,128)}), (f32[256,256]{1,0:T(8,128)}, f32[256,256]{1,0:T(8,128)}, f32[256,256]{1,0:T(8,128)})) %all-reduce.5.cloned.1.call-update) | async-done | bytes 786448 | tf_op jit(solution)/shard_map/psum | solution.py:54
  298.1 1.0 sub.9
  299.1 1.4 fusion.1
  300.6 2.3 fusion
  (30 shorter events, 0.3 us)
Async XLA Ops:
  7.2 193.7 %copy-start = (f32[256,256]{1,0:T(8,128)S(1)}, f32[256,256]{1,0:T(8,128)}, u32[]{:S(2)}) copy-start(f32[256,256]{1,0:T(8,128)} %param.12) | copy-start | bytes 786436
  7.2 23.6 %all-gather.5.cloned.1.call-start = ((), (), s32[]{:S(2)}) async-start(), calls=%async_computation.4 | async-start | bytes 1310720 | tf_op jit(solution)/shard_map/all_gather | solution.py:44
  11.2 38.5 %all-gather.3.cloned.1.call-start = ((), (), s32[]{:S(2)}) async-start(), calls=%async_computation.2 | async-start | bytes 1310720 | tf_op jit(solution)/shard_map/all_gather | solution.py:44
  13.1 126.0 %all-reduce.7.cloned.1.call-start = ((), (), s32[]{:S(2)}) async-start(), calls=%async_computation.7 | async-start | bytes 4194304 | tf_op jit(solution)/shard_map/psum | solution.py:9
  52.0 121.6 %reduce-scatter.3.cloned.1.call-start = ((), (), s32[]{:S(2)}) async-start(), calls=%async_computation.3 | async-start | bytes 1310720 | tf_op jit(solution)/shard_map/reduce_scatter | solution.py:51
  139.2 10.6 %copy-start.5 = (f32[1024,256]{1,0:T(8,128)S(1)}, f32[1024,256]{1,0:T(8,128)}, u32[]{:S(2)}) copy-start(f32[1024,256]{1,0:T(8,128)} %get-tuple-element.14) | copy-start | bytes 3145732
  149.5 10.4 %copy-start.8 = (s32[16]{0:T(128)S(1)}, s32[16]{0:T(128)}, u32[]{:S(2)}) copy-start(s32[16]{0:T(128)} %param.15) | copy-start | bytes 196
  149.6 25.0 %copy-start.1 = (f32[256,256]{1,0:T(8,128)S(1)}, f32[256,256]{1,0:T(8,128)}, u32[]{:S(2)}) copy-start(f32[256,256]{1,0:T(8,128)} %broadcast_multiply_fusion) | copy-start | bytes 786436
  149.6 51.3 %reduce-scatter.5.cloned.1.call-start = ((), (), s32[]{:S(2)}) async-start(), calls=%async_computation.5 | async-start | bytes 1310720 | tf_op jit(solution)/shard_map/reduce_scatter | solution.py:51
  149.8 25.8 %copy-start.2 = (f32[256,256]{1,0:T(8,128)S(1)}, f32[256,256]{1,0:T(8,128)}, u32[]{:S(2)}) copy-start(f32[256,256]{1,0:T(8,128)} %broadcast_multiply_fusion.1) | copy-start | bytes 786436
  159.8 138.3 %copy-start.6 = (f32[256,256]{1,0:T(8,128)S(1)}, f32[256,256]{1,0:T(8,128)}, u32[]{:S(2)}) copy-start(f32[256,256]{1,0:T(8,128)} %param.13) | copy-start | bytes 786436
  159.8 140.7 %copy-start.7 = (f32[256,256]{1,0:T(8,128)S(1)}, f32[256,256]{1,0:T(8,128)}, u32[]{:S(2)}) copy-start(f32[256,256]{1,0:T(8,128)} %param.14) | copy-start | bytes 786436
  159.9 138.3 %all-reduce.5.cloned.1.call-start = ((), (), s32[]{:S(2)}) async-start(), calls=%async_computation.6 | async-start | bytes 1572864 | tf_op jit(solution)/shard_map/psum | solution.py:54
  299.1 3.8 %copy-start.3 = (f32[256,256]{1,0:T(8,128)}, f32[256,256]{1,0:T(8,128)S(1)}, u32[]{:S(2)}) copy-start(f32[256,256]{1,0:T(8,128)S(1)} %sub.9) | copy-start | bytes 786436
  300.6 2.4 copy-start.4
Sparse Core Ops, SparseCore 0:
  11.3 19.4 all-gather.4
  32.9 16.7 all-gather.2
  52.1 87.0 all-reduce.6
  149.7 23.8 reduce-scatter.2
  175.9 24.8 reduce-scatter.4
  205.5 92.6 all-reduce.4
where the time goes:
time: 310 us
  waiting for transfers between devices  252 us (81%)
  matrix products  29.4 us (9%)
  between operations  14.2 us (5%)
  other arithmetic  12.2 us (4%)
    psum x1, waiting for transfers between devices, total_terms(): return lax.psum(terms, ('prow', 'pcol'))  92.7 us
    psum x1, waiting for transfers between devices, spread_2(): return lax.psum(jnp.where(mine, array, jnp.zeros_like(array)), axis)  87.1 us
    reduce_scatter x2, waiting for transfers between devices, total_rows(): lax.psum_scatter(partial_value, 'pcol', scatter_dimension=0, tiled=True)  37.4 us
    all_gather x2, waiting for transfers between devices, spread(): band = lax.all_gather(own_rows, 'pcol', axis=0, tiled=True)  34.2 us
    dot_general x4, matrix products, product(): jnp.dot(left, right, precision=lax.Precision.HIGHEST, preferred_element_t...  23.4 us
  transfers between devices with their start and end apart: 6, of which 6 were waited for; matrix products, arithmetic and copies ran while one was open for 6% of the time, Pallas kernels for 0%

commit v1 on v0

v1 whole, which is shorter than its diff:
```python
import functools

import jax
import jax.numpy as jnp
from jax import lax
from jax.experimental import pallas as pl
from jax.experimental.pallas import tpu as pltpu
from jax.sharding import PartitionSpec as P

F32 = jnp.float32
BF16 = jnp.bfloat16
SMEM = pl.BlockSpec(memory_space=pltpu.SMEM)
VMEM = pl.BlockSpec(memory_space=pltpu.VMEM)
ANY = pl.BlockSpec(memory_space=pl.ANY)


def product(left, right):
    return jnp.dot(left, right, precision=lax.Precision.HIGHEST, preferred_element_type=F32)


def contract(left, right):
    return lax.dot_general(
        left, right, (((0,), (0,)), ((), ())), precision=lax.Precision.HIGHEST, preferred_element_type=F32
    )


def spread_2(array, axis, root):
    mine = lax.axis_index(axis) == root
    return lax.psum(jnp.where(mine, array, jnp.zeros_like(array)), axis)


def any_mesh(
    known, lower_two, lower_one, top_one, inner_two, inner_one, heights, pattern_two, pattern_one
):
    width = top_one.shape[0]
    piece = lower_two.shape[0]
    n_col = lax.axis_size("pcol")
    ratio = lax.axis_size("prow") // n_col
    row_index = lax.axis_index("prow")
    col_index = lax.axis_index("pcol")
    live = (jnp.arange(width)[None, :] < heights[:, None]).astype(F32).reshape(-1)
    own_start = (row_index * n_col + col_index) * piece
    own_live = lax.dynamic_slice_in_dim(live, own_start, piece)

    def mask_own(lower, pattern):
        keep = live * jnp.repeat(pattern.astype(F32), width)
        return lower * lax.dynamic_slice_in_dim(keep, own_start, piece)[:, None]

    def spread(own_rows):
        band = lax.all_gather(own_rows, "pcol", axis=0, tiled=True)
        return jnp.concatenate(
            [spread_2(band, "prow", col_index * ratio + offset) for offset in range(ratio)], axis=0
        )

    def total_rows(partial_value):
        return lax.psum_scatter(partial_value, "pcol", scatter_dimension=0, tiled=True)

    own_two = mask_own(lower_two, pattern_two)
    own_one = mask_own(lower_one, pattern_one)
    partial_two = product(known, spread(own_two))
    partial_one = product(known, spread(own_one))
    column_two = -(own_live[:, None] * total_rows(partial_two))
    first_term, second_term = lax.psum(
        (contract(own_two, column_two), contract(column_two, own_one)), ("prow", "pcol")
    )
    diag_two = inner_two - first_term
    cross_block = -(second_term + product(diag_two, top_one))
    column_one = -(own_live[:, None] * (total_rows(partial_one) + product(column_two, top_one)))
    third_term = lax.psum(contract(own_one, column_one), ("prow", "pcol"))
    diag_one = inner_one - third_term - contract(top_one, cross_block)
    return (column_two, diag_two, column_one, cross_block, diag_one)


def halves(value):
    high = value.astype(BF16)
    return high, (value - high.astype(F32)).astype(BF16)


def dot3(left, right, dims):
    (lh, ll), (rh, rl) = left, right
    dot = lambda a, b: lax.dot_general(a, b, (dims, ((), ())), preferred_element_type=F32)
    return dot(lh, rh) + (dot(lh, rl) + dot(ll, rh))


ROWS_BY_COLUMNS = ((1,), (0,))
ROWS_BY_ROWS = ((0,), (0,))


def keep_rows(block, limit):
    row = lax.broadcasted_iota(jnp.int32, block.shape, 0)
    return jnp.where(row < limit, block, 0.0)


def band_kernel(n, sides, at, heights, *refs):
    patterns, refs = refs[:sides], refs[sides:]
    known = refs[0]
    gathered, plane = refs[1 : 1 + n], refs[1 + n : 1 + 2 * n]
    keep, send, sums = refs[1 + 2 * n : 4 + 2 * n]
    tiles, high, low, total, sems = refs[4 + 2 * n :]
    row, col = at[0], at[1]
    width = total.shape[-1]
    copies = [
        pltpu.make_async_copy(
            known.at[pl.ds(pl.multiple_of((a ^ col) * width, width), width)], tiles.at[a], sems.at[a]
        )
        for a in range(n)
    ]
    for copy in copies:
        copy.start()
    own = patterns[0]
    for k in range(n):
        block = row ^ k
        which = col * n + block
        h, l = halves(keep_rows(gathered[k][...], heights[which] * own[which]))
        where = pl.ds(pl.multiple_of(block * width, width), width)
        high[where] = h
        low[where] = l
    right = (high[...], low[...])
    for a in range(n):
        copies[a].wait()
        tile = dot3(halves(tiles[a]), right, ROWS_BY_COLUMNS)
        (send if a & 1 else keep)[a >> 1] = tile
        tile = halves(tile)
        which = row * n + (a ^ col)
        for s in range(sides):
            offset = plane[a].shape[0] - sides * width + s * width
            rows = plane[a][offset : offset + width]
            rows = halves(keep_rows(rows, heights[which] * patterns[s][which]))
            term = dot3(rows, tile, ROWS_BY_ROWS) if s == 0 else dot3(tile, rows, ROWS_BY_ROWS)
            total[s] = term if a == 0 else total[s] + term
    quarter = width // n
    for s in range(sides):
        for e in range(n):
            sums[e, s] = total[s, pl.ds(pl.multiple_of((e ^ col) * quarter, quarter), quarter)]


def band(at, heights, patterns, known, gathered, plane):
    n, sides = len(gathered), len(patterns)
    width = gathered[0].shape[0]
    span = known.shape[1]
    flops = 2 * 3 * (known.shape[0] * span * width + sides * known.shape[0] * width * width)
    return pl.pallas_call(
        functools.partial(band_kernel, n, sides),
        out_shape=(
            jax.ShapeDtypeStruct((n // 2, width, width), F32),
            jax.ShapeDtypeStruct((n // 2, width, width), F32),
            jax.ShapeDtypeStruct((n, sides, width // n, width), F32),
        ),
        in_specs=[SMEM] * (2 + sides) + [ANY] + [VMEM] * (2 * n),
        out_specs=(VMEM, VMEM, VMEM),
        scratch_shapes=[
            pltpu.VMEM((n, width, span), F32),
            pltpu.VMEM((span, width), BF16),
            pltpu.VMEM((span, width), BF16),
            pltpu.VMEM((sides, width, width), F32),
            pltpu.SemaphoreType.DMA((n,)),
        ],
        compiler_params=pltpu.CompilerParams(vmem_limit_bytes=40 * 2**20),
        cost_estimate=pl.CostEstimate(flops=flops, bytes_accessed=8 * 2**20, transcendentals=0),
        name="band_product",
    )(at, heights, *patterns, known, *gathered, *plane)


def blocks_kernel(n, at, top, inner_two, inner_one, *refs):
    parts, (diag_two, cross, rest, whole) = refs[:n], refs[n:]
    col = at[1]
    quarter = parts[0].shape[1]
    for e in range(n):
        for s in range(2):
            whole[s, pl.ds(pl.multiple_of((e ^ col) * quarter, quarter), quarter)] = parts[e][s]
    t = halves(top[...])
    d = inner_two[...] + whole[0]
    diag_two[...] = d
    c = whole[1] - dot3(halves(d), t, ROWS_BY_COLUMNS)
    cross[...] = c
    rest[...] = (
        inner_one[...]
        - dot3(halves(whole[1]), t, ROWS_BY_ROWS)
        - dot3(t, halves(c), ROWS_BY_ROWS)
    )


def blocks(at, top, inner_two, inner_one, parts):
    shape = jax.ShapeDtypeStruct(top.shape, F32)
    return pl.pallas_call(
        functools.partial(blocks_kernel, len(parts)),
        out_shape=(shape, shape, shape),
        in_specs=[SMEM] + [VMEM] * (3 + len(parts)),
        out_specs=(VMEM,) * 3,
        scratch_shapes=[pltpu.VMEM((2,) + top.shape, F32)],
        name="small_blocks",
    )(at, top, inner_two, inner_one, *parts)


def last_kernel(n, at, rest, *refs):
    parts, out = refs[:n], refs[n]
    col = at[1]
    quarter = parts[0].shape[1]
    for e in range(n):
        where = pl.ds(pl.multiple_of((e ^ col) * quarter, quarter), quarter)
        out[where] = rest[where] + parts[e][0]


def last(at, rest, parts):
    return pl.pallas_call(
        functools.partial(last_kernel, len(parts)),
        out_shape=jax.ShapeDtypeStruct(rest.shape, F32),
        in_specs=[SMEM] + [VMEM] * (1 + len(parts)),
        out_specs=VMEM,
        name="last_block",
    )(at, rest, *parts)


def column_kernel(at, heights, mine, other, *refs):
    n = heights.shape[0]
    limit = heights[at[0] * 4 + at[1]]
    total = mine[...] + other[...]
    if len(refs) == 1:
        refs[0][...] = keep_rows(-total, limit)
    else:
        before, top, out = refs
        total = total + dot3(halves(before[...]), halves(top[...]), ROWS_BY_COLUMNS)
        out[...] = keep_rows(-total, limit)


def column(at, heights, mine, other, *more):
    return pl.pallas_call(
        column_kernel,
        out_shape=jax.ShapeDtypeStruct(mine.shape, F32),
        in_specs=[SMEM, SMEM] + [VMEM] * (2 + len(more)),
        out_specs=VMEM,
        name="column_rows",
    )(at, heights, mine, other, *more)


def square_mesh(
    known, lower_two, lower_one, top_one, inner_two, inner_one, heights, pattern_two, pattern_one
):
    n = lax.axis_size("pcol")
    at = jnp.stack([lax.axis_index("prow"), lax.axis_index("pcol")]).astype(jnp.int32)

    def along(axis, k, array):
        return lax.ppermute(array, axis, [(i, i ^ k) for i in range(n)])

    core = functools.partial(along, "pcol", 1)
    across = functools.partial(along, "pcol", 2)

    def gather(rows):
        return [
            lax.ppermute(
                rows, ("prow", "pcol"), [(z * n + j, (j ^ k) * n + z) for z in range(n) for j in range(n)]
            )
            for k in range(n)
        ]

    def total_over_mesh(sums):
        got = core(sums[1::2])
        mine, theirs = sums[0] + got[0], sums[2] + got[1]
        mine = mine + across(theirs)
        mine = mine + along("prow", 1, mine)
        mine = mine + along("prow", 2, mine)
        other = across(mine)
        return (mine, core(mine), other, core(other))

    def total_over_row(keep, send):
        got = core(send)
        return keep[0] + got[0], across(keep[1] + got[1])

    rows_two = gather(lower_two)
    pair = jnp.concatenate([lower_two, lower_one], axis=0)
    pair_x = across(pair)
    plane = [pair, core(pair), pair_x, core(pair_x)]
    rows_one = gather(lower_one)

    keep_two, send_two, sums_two = band(
        at, heights, (pattern_two, pattern_one), known, rows_two, plane
    )
    parts_two = total_over_mesh(sums_two)
    column_two = column(at, heights, *total_over_row(keep_two, send_two))
    diag_two, cross_block, rest = blocks(at, top_one, inner_two, inner_one, parts_two)
    keep_one, send_one, sums_one = band(at, heights, (pattern_one,), known, rows_one, plane)
    parts_one = total_over_mesh(sums_one)
    column_one = column(at, heights, *total_over_row(keep_one, send_one), column_two, top_one)
    diag_one = last(at, rest, parts_one)
    return (column_two, diag_two, column_one, cross_block, diag_one)


def per_device(known, lower_two, lower_one, top_one, *rest):
    square = lax.axis_size("prow") == 4 and lax.axis_size("pcol") == 4
    body = square_mesh if square and lower_two.shape == top_one.shape else any_mesh
    return body(known, lower_two, lower_one, top_one, *rest)


def solution(mesh):
    return jax.shard_map(
        per_device,
        mesh=mesh,
        in_specs=(
            P(("pole", "prow"), "pcol"),
            P(("pole", "prow", "pcol"), None),
            P(("pole", "prow", "pcol"), None),
            P("pole", None),
            P("pole", None),
            P("pole", None),
            P(),
            P(),
            P(),
        ),
        out_specs=(
            P(("pole", "prow", "pcol"), None),
            P("pole", None),
            P(("pole", "prow", "pcol"), None),
            P("pole", None),
            P("pole", None),
        ),
        check_vma=False,
    )
```

time: 310 us -> 126 us (0.41)
  waiting for transfers between devices: 252 us -> 38.9 us
  starting transfers between devices: 0.43 us -> 54.4 us
  matrix products: 29.4 us -> 0 us
  Pallas kernels: 0 us -> 21.2 us
  between operations: 14.2 us -> 0.9 us
  other arithmetic: 12.2 us -> 1.74 us
  local copies, waits for them, and re-layouts: 2 us -> 8.3 us
    psum x2 -> x0, waiting for transfers between devices: 180 us -> none  [the longest x1 92.7 us: total_terms(): return lax.psum(terms, ('prow', 'pcol'))]
    ppermute x0 -> x29, starting transfers between devices: none -> 54.4 us  [the longest x8 31.5 us: gather(): lax.ppermute(rows, ('prow', 'pcol'), [(z * n + j, (j ^ k) * n + z) for z...]
    ppermute x0 -> x29, waiting for transfers between devices: none -> 38.9 us  [the longest x21 28.8 us: along(): return lax.ppermute(array, axis, [(i, i ^ k) for i in range(n)])]
    reduce_scatter x2 -> x0, waiting for transfers between devices: 37.4 us -> none  [total_rows(): lax.psum_scatter(partial_value, 'pcol', scatter_dimension=0, tiled=True)]
    all_gather x2 -> x0, waiting for transfers between devices: 34.2 us -> none  [spread(): band = lax.all_gather(own_rows, 'pcol', axis=0, tiled=True)]
    dot_general x8 -> x0, matrix products: 29.4 us -> none  [the longest x4 23.4 us: product(): jnp.dot(left, right, precision=lax.Precision.HIGHEST, preferred_element_t...]
    pallas_call x0 -> x6, Pallas kernels: none -> 21.2 us  [the longest x2 12.8 us: band(): pl.pallas_call(functools.partial(band_kernel, n, sides), out_shape=(jax.S...]
    unnamed x23 -> x33, local copies, waits for them, and re-layouts: 1.76 us -> 7.29 us
  transfers between devices with their start and end apart: 6 -> 29, of which waited for: 6 -> 9; matrix products, arithmetic and copies ran while one was open for 6% -> 1% of each run, Pallas kernels for 0% -> 15%
where the time goes in v1:
time: 126 us; the launch traced here: 125 us
  starting transfers between devices  54.4 us (43%)
  waiting for transfers between devices  38.9 us (31%)
  Pallas kernels  21.2 us (17%)
  local copies, waits for them, and re-layouts  8.3 us (7%)
  other arithmetic  1.74 us (1%)
    ppermute x8, starting transfers between devices, gather(): lax.ppermute(rows, ('prow', 'pcol'), [(z * n + j, (j ^ k) * n + z) for z...  31.5 us
    ppermute x21, waiting for transfers between devices, along(): return lax.ppermute(array, axis, [(i, i ^ k) for i in range(n)])  28.8 us
    ppermute x21, starting transfers between devices, along(): return lax.ppermute(array, axis, [(i, i ^ k) for i in range(n)])  22.9 us
    pallas_call x2, Pallas kernels, band(): pl.pallas_call(functools.partial(band_kernel, n, sides), out_shape=(jax.S...  12.8 us
    ppermute x8, waiting for transfers between devices, gather(): lax.ppermute(rows, ('prow', 'pcol'), [(z * n + j, (j ^ k) * n + z) for z...  10 us
    unnamed x33, local copies, waits for them, and re-layouts  7.29 us
    pallas_call x2, Pallas kernels, column(): pl.pallas_call(column_kernel, out_shape=jax.ShapeDtypeStruct(mine.shape,...  3.95 us
    pallas_call x1, Pallas kernels, blocks(): pl.pallas_call(functools.partial(blocks_kernel, len(parts)), out_shape=(s...  2.64 us
  transfers between devices with their start and end apart: 29, of which 9 were waited for; matrix products, arithmetic and copies ran while one was open for 1% of the time, Pallas kernels for 15%

profile of v1, /device:TPU:0, one launch (start us, length us, event | category | flops | bytes accessed | tf_op | source)
XLA Modules:
  0.0 125.3 jit_solution(15569443451962866109)
XLA Ops:
  1.6 1.0 constant_dynamic-update-slice_fusion.refs_7_.refs_6_
  2.6 3.0 %collective-permute-start.5 = (f32[512,256]{1,0:T(8,128)S(1)}, f32[512,256]{1,0:T(8,128)S(1)}, u32[]{:S(2)}, u32[]{:S(2)}) collective-permute-start(f32[512,256]{1,0:T(8,128)S(1)} %constant_dynamic-update-slice_fusion.refs_7_.refs_6_), channel_id=1, source_target_pairs={{0,2},{1,3},{2,0},{3,1},{4,6},{5,7},{6,4},{7,5},{8,10},{9,11},{10,... | collective-permute-start | bytes 1572872 | tf_op jit(solution)/shard_map/ppermute | solution.py:243
  5.6 1.6 %collective-permute-start.16 = (f32[256,256]{1,0:T(8,128)}, f32[256,256]{1,0:T(8,128)S(1)}, u32[]{:S(2)}, u32[]{:S(2)}) collective-permute-start(f32[256,256]{1,0:T(8,128)} %param.11), channel_id=1, source_target_pairs={{0,0},{1,4},{2,8},{3,12},{4,1},{5,5},{6,9},{7,13},{8,2},{9,6},{10,... | collective-permute-start | bytes 786440 | tf_op jit(solution)/shard_map/ppermute | solution.py:250
  7.2 2.1 %collective-permute-start.4 = (f32[512,256]{1,0:T(8,128)S(1)}, f32[512,256]{1,0:T(8,128)S(1)}, u32[]{:S(2)}, u32[]{:S(2)}) collective-permute-start(f32[512,256]{1,0:T(8,128)S(1)} %constant_dynamic-update-slice_fusion.refs_7_.refs_6_), channel_id=1, source_target_pairs={{0,1},{1,0},{2,3},{3,2},{4,5},{5,4},{6,7},{7,6},{8,9},{9,8},{10,11... | collective-permute-start | bytes 1572872 | tf_op jit(solution)/shard_map/ppermute | solution.py:243
  9.3 13.2 %collective-permute-done.5.refs_9_.refs_8_ = f32[512,256]{1,0:T(8,128)S(1)} collective-permute-done((f32[512,256]{1,0:T(8,128)S(1)}, f32[512,256]{1,0:T(8,128)S(1)}, u32[]{:S(2)}, u32[]{:S(2)}) %collective-permute-start.5) | collective-permute-done | bytes 524320 | tf_op jit(solution)/shard_map/ppermute | solution.py:243
  22.4 1.5 %collective-permute-start.17 = (f32[256,256]{1,0:T(8,128)}, f32[256,256]{1,0:T(8,128)S(1)}, u32[]{:S(2)}, u32[]{:S(2)}) collective-permute-start(f32[256,256]{1,0:T(8,128)} %param.11), channel_id=1, source_target_pairs={{0,4},{1,0},{2,12},{3,8},{4,5},{5,1},{6,13},{7,9},{8,6},{9,2},{10,... | collective-permute-start | bytes 786440 | tf_op jit(solution)/shard_map/ppermute | solution.py:250
  24.0 3.4 %collective-permute-start.18 = (f32[256,256]{1,0:T(8,128)}, f32[256,256]{1,0:T(8,128)S(1)}, u32[]{:S(2)}, u32[]{:S(2)}) collective-permute-start(f32[256,256]{1,0:T(8,128)} %param.11), channel_id=1, source_target_pairs={{0,8},{1,12},{2,0},{3,4},{4,9},{5,13},{6,1},{7,5},{8,10},{9,14},{1... | collective-permute-start | bytes 786440 | tf_op jit(solution)/shard_map/ppermute | solution.py:250
  27.4 1.0 collective-permute-start.19
  28.4 1.6 %collective-permute-start = (f32[256,256]{1,0:T(8,128)}, f32[256,256]{1,0:T(8,128)S(1)}, u32[]{:S(2)}, u32[]{:S(2)}) collective-permute-start(f32[256,256]{1,0:T(8,128)} %param.10), channel_id=1, source_target_pairs={{0,0},{1,4},{2,8},{3,12},{4,1},{5,5},{6,9},{7,13},{8,2},{9,6},{10,... | collective-permute-start | bytes 786440 | tf_op jit(solution)/shard_map/ppermute | solution.py:250
  30.0 10.0 %collective-permute-done.18.refs_4_ = f32[256,256]{1,0:T(8,128)S(1)} collective-permute-done((f32[256,256]{1,0:T(8,128)}, f32[256,256]{1,0:T(8,128)S(1)}, u32[]{:S(2)}, u32[]{:S(2)}) %collective-permute-start.18) | collective-permute-done | bytes 262176 | tf_op jit(solution)/shard_map/ppermute | solution.py:250
  40.0 5.4 %collective-permute-start.1 = (f32[256,256]{1,0:T(8,128)}, f32[256,256]{1,0:T(8,128)S(1)}, u32[]{:S(2)}, u32[]{:S(2)}) collective-permute-start(f32[256,256]{1,0:T(8,128)} %param.10), channel_id=1, source_target_pairs={{0,4},{1,0},{2,12},{3,8},{4,5},{5,1},{6,13},{7,9},{8,6},{9,2},{10,... | collective-permute-start | bytes 786440 | tf_op jit(solution)/shard_map/ppermute | solution.py:250
  45.4 4.2 %collective-permute-start.2 = (f32[256,256]{1,0:T(8,128)}, f32[256,256]{1,0:T(8,128)S(1)}, u32[]{:S(2)}, u32[]{:S(2)}) collective-permute-start(f32[256,256]{1,0:T(8,128)} %param.10), channel_id=1, source_target_pairs={{0,8},{1,12},{2,0},{3,4},{4,9},{5,13},{6,1},{7,5},{8,10},{9,14},{1... | collective-permute-start | bytes 786440 | tf_op jit(solution)/shard_map/ppermute | solution.py:250
  49.6 12.7 %collective-permute-start.3 = (f32[256,256]{1,0:T(8,128)}, f32[256,256]{1,0:T(8,128)S(1)}, u32[]{:S(2)}, u32[]{:S(2)}) collective-permute-start(f32[256,256]{1,0:T(8,128)} %param.10), channel_id=1, source_target_pairs={{0,12},{1,8},{2,4},{3,0},{4,13},{5,9},{6,5},{7,1},{8,14},{9,10},{1... | collective-permute-start | bytes 786440 | tf_op jit(solution)/shard_map/ppermute | solution.py:250
  63.1 2.2 %copy-done.2 = f32[1024,1024]{1,0:T(8,128)S(1)} copy-done((f32[1024,1024]{1,0:T(8,128)S(1)}, f32[1024,1024]{1,0:T(8,128)}, u32[]{:S(2)}) %copy-start.2) | copy-done | bytes 4194328
  65.9 5.9 %band_product.3 = (f32[2,256,256]{2,1,0:T(8,128)S(1)}, f32[2,256,256]{2,1,0:T(8,128)S(1)}, f32[4,1,64,256]{3,2,1,0:T(8,128)S(1)}) custom-call(s32[2]{0:T(128)S(1)} %pad_add_fusion.at, s32[16]{0:T(128)S(1)} %copy-done.1, s32[16]{0:T(128)S(1)} %copy-done.5, f32[1024,1024]{1,0:T(8,128)S(1)} %copy-done.2, f32[256,256]{1,0:T(8,128)S(1)} %collective-permute-done.16.refs_2_, ...), custom_call_target="tpu_custom_call" | custom-call | flops 2013265920 | bytes 8388608 | tf_op jit(solution)/shard_map/band_product/pallas_call | solution.py:142
  72.0 6.9 %band_product.2 = (f32[2,256,256]{2,1,0:T(8,128)S(1)}, f32[2,256,256]{2,1,0:T(8,128)S(1)}, f32[4,2,64,256]{3,2,1,0:T(8,128)S(1)}) custom-call(s32[2]{0:T(128)S(1)} %pad_add_fusion.at, s32[16]{0:T(128)S(1)} %copy-done.1, s32[16]{0:T(128)S(1)} %copy-done.4, s32[16]{0:T(128)S(1)} %copy-done.5, f32[1024,1024]{1,0:T(8,128)S(1)} %copy-done.3, ...), custom_call_target="tpu_custom_call" | custom-call | flops 2415919104 | bytes 8388608 | tf_op jit(solution)/shard_map/band_product/pallas_call | solution.py:142
  80.0 3.0 %collective-permute-start.23 = (f32[1,64,256]{2,1,0:T(8,128)S(1)}, f32[1,64,256]{2,1,0:T(8,128)S(1)}, u32[]{:S(2)}, u32[]{:S(2)}) collective-permute-start(f32[1,64,256]{2,1,0:T(8,128)S(1)} %fusion.7), channel_id=1, source_target_pairs={{0,2},{1,3},{2,0},{3,1},{4,6},{5,7},{6,4},{7,5},{8,10},{9,11},{10,... | collective-permute-start | bytes 196616 | tf_op jit(solution)/shard_map/ppermute | solution.py:243
  83.9 1.7 %collective-permute-done.23 = f32[1,64,256]{2,1,0:T(8,128)S(1)} collective-permute-done((f32[1,64,256]{2,1,0:T(8,128)S(1)}, f32[1,64,256]{2,1,0:T(8,128)S(1)}, u32[]{:S(2)}, u32[]{:S(2)}) %collective-permute-start.23) | collective-permute-done | bytes 65568 | tf_op jit(solution)/shard_map/ppermute | solution.py:243
  85.7 2.1 %collective-permute-start.24 = (f32[1,64,256]{2,1,0:T(8,128)S(1)}, f32[1,64,256]{2,1,0:T(8,128)S(1)}, u32[]{:S(2)}, u32[]{:S(2)}) collective-permute-start(f32[1,64,256]{2,1,0:T(8,128)S(1)} %fusion.9), channel_id=1, source_target_pairs={{0,4},{4,0},{8,12},{12,8},{1,5},{5,1},{9,13},{13,9},{2,6},{6,2},{1... | collective-permute-start | bytes 196616 | tf_op jit(solution)/shard_map/ppermute | solution.py:243
  88.7 2.1 %collective-permute-start.11 = (f32[2,64,256]{2,1,0:T(8,128)S(1)}, f32[2,64,256]{2,1,0:T(8,128)S(1)}, u32[]{:S(2)}, u32[]{:S(2)}) collective-permute-start(f32[2,64,256]{2,1,0:T(8,128)S(1)} %fusion.6), channel_id=1, source_target_pairs={{0,4},{4,0},{8,12},{12,8},{1,5},{5,1},{9,13},{13,9},{2,6},{6,2},{1... | collective-permute-start | bytes 393224 | tf_op jit(solution)/shard_map/ppermute | solution.py:243
  91.5 1.6 %collective-permute-start.8 = (f32[256,256]{1,0:T(8,128)S(1)}, f32[256,256]{1,0:T(8,128)S(1)}, u32[]{:S(2)}, u32[]{:S(2)}) collective-permute-start(f32[256,256]{1,0:T(8,128)S(1)} %get-tuple-element.25), channel_id=1, source_target_pairs={{0,2},{1,3},{2,0},{3,1},{4,6},{5,7},{6,4},{7,5},{8,10},{9,11},{10,... | collective-permute-start | bytes 786440 | tf_op jit(solution)/shard_map/ppermute | solution.py:243
  93.7 2.1 %collective-permute-start.12 = (f32[2,64,256]{2,1,0:T(8,128)S(1)}, f32[2,64,256]{2,1,0:T(8,128)S(1)}, u32[]{:S(2)}, u32[]{:S(2)}) collective-permute-start(f32[2,64,256]{2,1,0:T(8,128)S(1)} %add.89), channel_id=1, source_target_pairs={{0,8},{4,12},{8,0},{12,4},{1,9},{5,13},{9,1},{13,5},{2,10},{6,14},... | collective-permute-start | bytes 393224 | tf_op jit(solution)/shard_map/ppermute | solution.py:243
  96.6 1.3 %collective-permute-start.21 = (f32[256,256]{1,0:T(8,128)S(1)}, f32[256,256]{1,0:T(8,128)S(1)}, u32[]{:S(2)}, u32[]{:S(2)}) collective-permute-start(f32[256,256]{1,0:T(8,128)S(1)} %get-tuple-element.23), channel_id=1, source_target_pairs={{0,2},{1,3},{2,0},{3,1},{4,6},{5,7},{6,4},{7,5},{8,10},{9,11},{10,... | collective-permute-start | bytes 786440 | tf_op jit(solution)/shard_map/ppermute | solution.py:243
  97.9 3.5 %collective-permute-done.12 = f32[2,64,256]{2,1,0:T(8,128)S(1)} collective-permute-done((f32[2,64,256]{2,1,0:T(8,128)S(1)}, f32[2,64,256]{2,1,0:T(8,128)S(1)}, u32[]{:S(2)}, u32[]{:S(2)}) %collective-permute-start.12) | collective-permute-done | bytes 131104 | tf_op jit(solution)/shard_map/ppermute | solution.py:243
  101.4 2.6 %collective-permute-start.14 = (f32[2,64,256]{2,1,0:T(8,128)S(1)}, f32[2,64,256]{2,1,0:T(8,128)S(1)}, u32[]{:S(2)}, u32[]{:S(2)}) collective-permute-start(f32[2,64,256]{2,1,0:T(8,128)S(1)} %add.90.refs_0_), channel_id=1, source_target_pairs={{0,2},{1,3},{2,0},{3,1},{4,6},{5,7},{6,4},{7,5},{8,10},{9,11},{10,... | collective-permute-start | bytes 393224 | tf_op jit(solution)/shard_map/ppermute | solution.py:243
  104.1 3.2 %collective-permute-done.14.refs_2_ = f32[2,64,256]{2,1,0:T(8,128)S(1)} collective-permute-done((f32[2,64,256]{2,1,0:T(8,128)S(1)}, f32[2,64,256]{2,1,0:T(8,128)S(1)}, u32[]{:S(2)}, u32[]{:S(2)}) %collective-permute-start.14) | collective-permute-done | bytes 131104 | tf_op jit(solution)/shard_map/ppermute | solution.py:243
  107.4 1.9 %collective-permute-done.25 = f32[1,64,256]{2,1,0:T(8,128)S(1)} collective-permute-done((f32[1,64,256]{2,1,0:T(8,128)S(1)}, f32[1,64,256]{2,1,0:T(8,128)S(1)}, u32[]{:S(2)}, u32[]{:S(2)}) %collective-permute-start.25) | collective-permute-done | bytes 65568 | tf_op jit(solution)/shard_map/ppermute | solution.py:243
  109.8 3.8 %collective-permute-done.27.refs_2_ = f32[1,64,256]{2,1,0:T(8,128)S(1)} collective-permute-done((f32[1,64,256]{2,1,0:T(8,128)S(1)}, f32[1,64,256]{2,1,0:T(8,128)S(1)}, u32[]{:S(2)}, u32[]{:S(2)}) %collective-permute-start.27) | collective-permute-done | bytes 65568 | tf_op jit(solution)/shard_map/ppermute | solution.py:243
  114.3 1.8 %column_rows.2.refs_0_ = f32[256,256]{1,0:T(8,128)} custom-call(s32[2]{0:T(128)} %copy-done, s32[16]{0:T(128)} %heights.7, f32[256,256]{1,0:T(8,128)} %get-tuple-element.26.mine, f32[256,256]{1,0:T(8,128)} %copy-done.7), custom_call_target="tpu_custom_call" | custom-call | tf_op jit(solution)/shard_map/column_rows/pallas_call | solution.py:227
  116.8 2.2 %column_rows.3 = f32[256,256]{1,0:T(8,128)} custom-call(s32[2]{0:T(128)} %copy-done, s32[16]{0:T(128)} %heights.7, f32[256,256]{1,0:T(8,128)} %get-tuple-element.24.mine, f32[256,256]{1,0:T(8,128)} %copy-done.8, f32[256,256]{1,0:T(8,128)} %column_rows.2.refs_0_, f32[256,256]{1,0:T(8,128)} %refs_1_.5), custom_call_target="tpu_custom_call" | custom-call | tf_op jit(solution)/shard_map/column_rows/pallas_call | solution.py:227
  120.3 2.6 %small_blocks.1 = (f32[256,256]{1,0:T(8,128)}, f32[256,256]{1,0:T(8,128)}, f32[256,256]{1,0:T(8,128)}) custom-call(s32[2]{0:T(128)} %copy-done, f32[256,256]{1,0:T(8,128)} %refs_1_.5, f32[256,256]{1,0:T(8,128)} %inner_two.1, f32[256,256]{1,0:T(8,128)} %inner_one.1, f32[2,64,256]{2,1,0:T(8,128)} %copy-done.6, f32[2,64,256]{2,1,0:T(8,128)} %copy-done.11, ...), custom_call_target="tpu_custom_call" | custom-call | tf_op jit(solution)/shard_map/small_blocks/pallas_call | solution.py:185
  123.6 1.8 %last_block.1 = f32[256,256]{1,0:T(8,128)} custom-call(s32[2]{0:T(128)} %copy-done, f32[256,256]{1,0:T(8,128)} %get-tuple-element.21.rest, f32[1,64,256]{2,1,0:T(8,128)} %copy-done.9, f32[1,64,256]{2,1,0:T(8,128)} %copy-done.14, f32[1,64,256]{2,1,0:T(8,128)} %copy-done.13, f32[1,64,256]{2,1,0:T(8,128)} %copy-done.15), custom_call_target="tpu_custom_call" | custom-call | tf_op jit(solution)/shard_map/last_block/pallas_call | solution.py:205
  (79 shorter events, 11.7 us)
Async XLA Ops:
  1.6 70.4 %copy-start.4 = (s32[16]{0:T(128)S(1)}, s32[16]{0:T(128)}, u32[]{:S(2)}) copy-start(s32[16]{0:T(128)} %refs_0_.2) | copy-start | bytes 196
  2.6 19.8 %collective-permute-start.5 = (f32[512,256]{1,0:T(8,128)S(1)}, f32[512,256]{1,0:T(8,128)S(1)}, u32[]{:S(2)}, u32[]{:S(2)}) collective-permute-start(f32[512,256]{1,0:T(8,128)S(1)} %constant_dynamic-update-slice_fusion.refs_7_.refs_6_), channel_id=1, source_target_pairs={{0,2},{1,3},{2,0},{3,1},{4,6},{5,7},{6,4},{7,5},{8,10},{9,11},{10,... | collective-permute-start | bytes 1572872 | tf_op jit(solution)/shard_map/ppermute | solution.py:243
  5.6 21.8 %collective-permute-start.16 = (f32[256,256]{1,0:T(8,128)}, f32[256,256]{1,0:T(8,128)S(1)}, u32[]{:S(2)}, u32[]{:S(2)}) collective-permute-start(f32[256,256]{1,0:T(8,128)} %param.11), channel_id=1, source_target_pairs={{0,0},{1,4},{2,8},{3,12},{4,1},{5,5},{6,9},{7,13},{8,2},{9,6},{10,... | collective-permute-start | bytes 786440 | tf_op jit(solution)/shard_map/ppermute | solution.py:250
  7.2 42.5 %collective-permute-start.4 = (f32[512,256]{1,0:T(8,128)S(1)}, f32[512,256]{1,0:T(8,128)S(1)}, u32[]{:S(2)}, u32[]{:S(2)}) collective-permute-start(f32[512,256]{1,0:T(8,128)S(1)} %constant_dynamic-update-slice_fusion.refs_7_.refs_6_), channel_id=1, source_target_pairs={{0,1},{1,0},{2,3},{3,2},{4,5},{5,4},{6,7},{7,6},{8,9},{9,8},{10,11... | collective-permute-start | bytes 1572872 | tf_op jit(solution)/shard_map/ppermute | solution.py:243
  22.4 40.0 %collective-permute-start.6 = (f32[512,256]{1,0:T(8,128)S(1)}, f32[512,256]{1,0:T(8,128)S(1)}, u32[]{:S(2)}, u32[]{:S(2)}) collective-permute-start(f32[512,256]{1,0:T(8,128)S(1)} %collective-permute-done.5.refs_9_.refs_8_), channel_id=1, source_target_pairs={{0,1},{1,0},{2,3},{3,2},{4,5},{5,4},{6,7},{7,6},{8,9},{9,8},{10,11... | collective-permute-start | bytes 1572872 | tf_op jit(solution)/shard_map/ppermute | solution.py:243
  22.4 6.0 %collective-permute-start.17 = (f32[256,256]{1,0:T(8,128)}, f32[256,256]{1,0:T(8,128)S(1)}, u32[]{:S(2)}, u32[]{:S(2)}) collective-permute-start(f32[256,256]{1,0:T(8,128)} %param.11), channel_id=1, source_target_pairs={{0,4},{1,0},{2,12},{3,8},{4,5},{5,1},{6,13},{7,9},{8,6},{9,2},{10,... | collective-permute-start | bytes 786440 | tf_op jit(solution)/shard_map/ppermute | solution.py:250
  24.0 16.1 %collective-permute-start.18 = (f32[256,256]{1,0:T(8,128)}, f32[256,256]{1,0:T(8,128)S(1)}, u32[]{:S(2)}, u32[]{:S(2)}) collective-permute-start(f32[256,256]{1,0:T(8,128)} %param.11), channel_id=1, source_target_pairs={{0,8},{1,12},{2,0},{3,4},{4,9},{5,13},{6,1},{7,5},{8,10},{9,14},{1... | collective-permute-start | bytes 786440 | tf_op jit(solution)/shard_map/ppermute | solution.py:250
  27.4 18.1 %collective-permute-start.19 = (f32[256,256]{1,0:T(8,128)}, f32[256,256]{1,0:T(8,128)S(1)}, u32[]{:S(2)}, u32[]{:S(2)}) collective-permute-start(f32[256,256]{1,0:T(8,128)} %param.11), channel_id=1, source_target_pairs={{0,12},{1,8},{2,4},{3,0},{4,13},{5,9},{6,5},{7,1},{8,14},{9,10},{1... | collective-permute-start | bytes 786440 | tf_op jit(solution)/shard_map/ppermute | solution.py:250
  28.4 43.6 %collective-permute-start = (f32[256,256]{1,0:T(8,128)}, f32[256,256]{1,0:T(8,128)S(1)}, u32[]{:S(2)}, u32[]{:S(2)}) collective-permute-start(f32[256,256]{1,0:T(8,128)} %param.10), channel_id=1, source_target_pairs={{0,0},{1,4},{2,8},{3,12},{4,1},{5,5},{6,9},{7,13},{8,2},{9,6},{10,... | collective-permute-start | bytes 786440 | tf_op jit(solution)/shard_map/ppermute | solution.py:250
  40.0 31.9 %collective-permute-start.1 = (f32[256,256]{1,0:T(8,128)}, f32[256,256]{1,0:T(8,128)S(1)}, u32[]{:S(2)}, u32[]{:S(2)}) collective-permute-start(f32[256,256]{1,0:T(8,128)} %param.10), channel_id=1, source_target_pairs={{0,4},{1,0},{2,12},{3,8},{4,5},{5,1},{6,13},{7,9},{8,6},{9,2},{10,... | collective-permute-start | bytes 786440 | tf_op jit(solution)/shard_map/ppermute | solution.py:250
  45.4 26.6 %collective-permute-start.2 = (f32[256,256]{1,0:T(8,128)}, f32[256,256]{1,0:T(8,128)S(1)}, u32[]{:S(2)}, u32[]{:S(2)}) collective-permute-start(f32[256,256]{1,0:T(8,128)} %param.10), channel_id=1, source_target_pairs={{0,8},{1,12},{2,0},{3,4},{4,9},{5,13},{6,1},{7,5},{8,10},{9,14},{1... | collective-permute-start | bytes 786440 | tf_op jit(solution)/shard_map/ppermute | solution.py:250
  49.6 22.3 %collective-permute-start.3 = (f32[256,256]{1,0:T(8,128)}, f32[256,256]{1,0:T(8,128)S(1)}, u32[]{:S(2)}, u32[]{:S(2)}) collective-permute-start(f32[256,256]{1,0:T(8,128)} %param.10), channel_id=1, source_target_pairs={{0,12},{1,8},{2,4},{3,0},{4,13},{5,9},{6,5},{7,1},{8,14},{9,10},{1... | collective-permute-start | bytes 786440 | tf_op jit(solution)/shard_map/ppermute | solution.py:250
  62.4 16.5 %copy-start = (s32[2]{0:T(128)}, s32[2]{0:T(128)S(1)}, u32[]{:S(2)}) copy-start(s32[2]{0:T(128)S(1)} %pad_add_fusion.at) | copy-start | bytes 28
  71.9 8.1 %collective-permute-start.22 = (f32[2,1,64,256]{3,2,1,0:T(8,128)S(1)}, f32[2,1,64,256]{3,2,1,0:T(8,128)S(1)}, u32[]{:S(2)}, u32[]{:S(2)}) collective-permute-start(f32[2,1,64,256]{3,2,1,0:T(8,128)S(1)} %slice.68), channel_id=1, source_target_pairs={{0,1},{1,0},{2,3},{3,2},{4,5},{5,4},{6,7},{7,6},{8,9},{9,8},{10,11... | collective-permute-start | bytes 393224 | tf_op jit(solution)/shard_map/ppermute | solution.py:243
  78.9 4.0 %collective-permute-start.9 = (f32[2,2,64,256]{3,2,1,0:T(8,128)S(1)}, f32[2,2,64,256]{3,2,1,0:T(8,128)S(1)}, u32[]{:S(2)}, u32[]{:S(2)}) collective-permute-start(f32[2,2,64,256]{3,2,1,0:T(8,128)S(1)} %slice.59), channel_id=1, source_target_pairs={{0,1},{1,0},{2,3},{3,2},{4,5},{5,4},{6,7},{7,6},{8,9},{9,8},{10,11... | collective-permute-start | bytes 786440 | tf_op jit(solution)/shard_map/ppermute | solution.py:243
  79.5 11.2 %collective-permute-start.7 = (f32[2,256,256]{2,1,0:T(8,128)S(1)}, f32[2,256,256]{2,1,0:T(8,128)S(1)}, u32[]{:S(2)}, u32[]{:S(2)}) collective-permute-start(f32[2,256,256]{2,1,0:T(8,128)S(1)} %get-tuple-element.15), channel_id=1, source_target_pairs={{0,1},{1,0},{2,3},{3,2},{4,5},{5,4},{6,7},{7,6},{8,9},{9,8},{10,11... | collective-permute-start | bytes 1572872 | tf_op jit(solution)/shard_map/ppermute | solution.py:243
  79.5 16.3 %collective-permute-start.20 = (f32[2,256,256]{2,1,0:T(8,128)S(1)}, f32[2,256,256]{2,1,0:T(8,128)S(1)}, u32[]{:S(2)}, u32[]{:S(2)}) collective-permute-start(f32[2,256,256]{2,1,0:T(8,128)S(1)} %get-tuple-element.19), channel_id=1, source_target_pairs={{0,1},{1,0},{2,3},{3,2},{4,5},{5,4},{6,7},{7,6},{8,9},{9,8},{10,11... | collective-permute-start | bytes 1572872 | tf_op jit(solution)/shard_map/ppermute | solution.py:243
  80.0 5.7 %collective-permute-start.23 = (f32[1,64,256]{2,1,0:T(8,128)S(1)}, f32[1,64,256]{2,1,0:T(8,128)S(1)}, u32[]{:S(2)}, u32[]{:S(2)}) collective-permute-start(f32[1,64,256]{2,1,0:T(8,128)S(1)} %fusion.7), channel_id=1, source_target_pairs={{0,2},{1,3},{2,0},{3,1},{4,6},{5,7},{6,4},{7,5},{8,10},{9,11},{10,... | collective-permute-start | bytes 196616 | tf_op jit(solution)/shard_map/ppermute | solution.py:243
  83.0 5.6 %collective-permute-start.10 = (f32[2,64,256]{2,1,0:T(8,128)S(1)}, f32[2,64,256]{2,1,0:T(8,128)S(1)}, u32[]{:S(2)}, u32[]{:S(2)}) collective-permute-start(f32[2,64,256]{2,1,0:T(8,128)S(1)} %fusion.4), channel_id=1, source_target_pairs={{0,2},{1,3},{2,0},{3,1},{4,6},{5,7},{6,4},{7,5},{8,10},{9,11},{10,... | collective-permute-start | bytes 393224 | tf_op jit(solution)/shard_map/ppermute | solution.py:243
  85.7 18.3 %collective-permute-start.24 = (f32[1,64,256]{2,1,0:T(8,128)S(1)}, f32[1,64,256]{2,1,0:T(8,128)S(1)}, u32[]{:S(2)}, u32[]{:S(2)}) collective-permute-start(f32[1,64,256]{2,1,0:T(8,128)S(1)} %fusion.9), channel_id=1, source_target_pairs={{0,4},{4,0},{8,12},{12,8},{1,5},{5,1},{9,13},{13,9},{2,6},{6,2},{1... | collective-permute-start | bytes 196616 | tf_op jit(solution)/shard_map/ppermute | solution.py:243
  88.7 5.1 %collective-permute-start.11 = (f32[2,64,256]{2,1,0:T(8,128)S(1)}, f32[2,64,256]{2,1,0:T(8,128)S(1)}, u32[]{:S(2)}, u32[]{:S(2)}) collective-permute-start(f32[2,64,256]{2,1,0:T(8,128)S(1)} %fusion.6), channel_id=1, source_target_pairs={{0,4},{4,0},{8,12},{12,8},{1,5},{5,1},{9,13},{13,9},{2,6},{6,2},{1... | collective-permute-start | bytes 393224 | tf_op jit(solution)/shard_map/ppermute | solution.py:243
  91.5 22.1 %collective-permute-start.8 = (f32[256,256]{1,0:T(8,128)S(1)}, f32[256,256]{1,0:T(8,128)S(1)}, u32[]{:S(2)}, u32[]{:S(2)}) collective-permute-start(f32[256,256]{1,0:T(8,128)S(1)} %get-tuple-element.25), channel_id=1, source_target_pairs={{0,2},{1,3},{2,0},{3,1},{4,6},{5,7},{6,4},{7,5},{8,10},{9,11},{10,... | collective-permute-start | bytes 786440 | tf_op jit(solution)/shard_map/ppermute | solution.py:243
  93.7 7.7 %collective-permute-start.12 = (f32[2,64,256]{2,1,0:T(8,128)S(1)}, f32[2,64,256]{2,1,0:T(8,128)S(1)}, u32[]{:S(2)}, u32[]{:S(2)}) collective-permute-start(f32[2,64,256]{2,1,0:T(8,128)S(1)} %add.89), channel_id=1, source_target_pairs={{0,8},{4,12},{8,0},{12,4},{1,9},{5,13},{9,1},{13,5},{2,10},{6,14},... | collective-permute-start | bytes 393224 | tf_op jit(solution)/shard_map/ppermute | solution.py:243
  96.6 19.5 %collective-permute-start.21 = (f32[256,256]{1,0:T(8,128)S(1)}, f32[256,256]{1,0:T(8,128)S(1)}, u32[]{:S(2)}, u32[]{:S(2)}) collective-permute-start(f32[256,256]{1,0:T(8,128)S(1)} %get-tuple-element.23), channel_id=1, source_target_pairs={{0,2},{1,3},{2,0},{3,1},{4,6},{5,7},{6,4},{7,5},{8,10},{9,11},{10,... | collective-permute-start | bytes 786440 | tf_op jit(solution)/shard_map/ppermute | solution.py:243
  101.4 17.6 %copy-start.6 = (f32[2,64,256]{2,1,0:T(8,128)}, f32[2,64,256]{2,1,0:T(8,128)S(1)}, u32[]{:S(2)}) copy-start(f32[2,64,256]{2,1,0:T(8,128)S(1)} %add.90.refs_0_) | copy-start | bytes 393220
  101.4 5.9 %collective-permute-start.14 = (f32[2,64,256]{2,1,0:T(8,128)S(1)}, f32[2,64,256]{2,1,0:T(8,128)S(1)}, u32[]{:S(2)}, u32[]{:S(2)}) collective-permute-start(f32[2,64,256]{2,1,0:T(8,128)S(1)} %add.90.refs_0_), channel_id=1, source_target_pairs={{0,2},{1,3},{2,0},{3,1},{4,6},{5,7},{6,4},{7,5},{8,10},{9,11},{10,... | collective-permute-start | bytes 393224 | tf_op jit(solution)/shard_map/ppermute | solution.py:243
  104.0 5.2 %collective-permute-start.25 = (f32[1,64,256]{2,1,0:T(8,128)S(1)}, f32[1,64,256]{2,1,0:T(8,128)S(1)}, u32[]{:S(2)}, u32[]{:S(2)}) collective-permute-start(f32[1,64,256]{2,1,0:T(8,128)S(1)} %add.100), channel_id=1, source_target_pairs={{0,8},{4,12},{8,0},{12,4},{1,9},{5,13},{9,1},{13,5},{2,10},{6,14},... | collective-permute-start | bytes 196616 | tf_op jit(solution)/shard_map/ppermute | solution.py:243
  104.1 14.9 %collective-permute-start.13 = (f32[2,64,256]{2,1,0:T(8,128)S(1)}, f32[2,64,256]{2,1,0:T(8,128)S(1)}, u32[]{:S(2)}, u32[]{:S(2)}) collective-permute-start(f32[2,64,256]{2,1,0:T(8,128)S(1)} %add.90.refs_0_), channel_id=1, source_target_pairs={{0,1},{1,0},{2,3},{3,2},{4,5},{5,4},{6,7},{7,6},{8,9},{9,8},{10,11... | collective-permute-start | bytes 393224 | tf_op jit(solution)/shard_map/ppermute | solution.py:243
  107.4 11.6 %collective-permute-start.15 = (f32[2,64,256]{2,1,0:T(8,128)S(1)}, f32[2,64,256]{2,1,0:T(8,128)S(1)}, u32[]{:S(2)}, u32[]{:S(2)}) collective-permute-start(f32[2,64,256]{2,1,0:T(8,128)S(1)} %collective-permute-done.14.refs_2_), channel_id=1, source_target_pairs={{0,1},{1,0},{2,3},{3,2},{4,5},{5,4},{6,7},{7,6},{8,9},{9,8},{10,11... | collective-permute-start | bytes 393224 | tf_op jit(solution)/shard_map/ppermute | solution.py:243
  109.2 4.3 %collective-permute-start.27 = (f32[1,64,256]{2,1,0:T(8,128)S(1)}, f32[1,64,256]{2,1,0:T(8,128)S(1)}, u32[]{:S(2)}, u32[]{:S(2)}) collective-permute-start(f32[1,64,256]{2,1,0:T(8,128)S(1)} %add.101.refs_0_), channel_id=1, source_target_pairs={{0,2},{1,3},{2,0},{3,1},{4,6},{5,7},{6,4},{7,5},{8,10},{9,11},{10,... | collective-permute-start | bytes 196616 | tf_op jit(solution)/shard_map/ppermute | solution.py:243
  113.6 9.3 %collective-permute-start.26 = (f32[1,64,256]{2,1,0:T(8,128)S(1)}, f32[1,64,256]{2,1,0:T(8,128)S(1)}, u32[]{:S(2)}, u32[]{:S(2)}) collective-permute-start(f32[1,64,256]{2,1,0:T(8,128)S(1)} %add.101.refs_0_), channel_id=1, source_target_pairs={{0,1},{1,0},{2,3},{3,2},{4,5},{5,4},{6,7},{7,6},{8,9},{9,8},{10,11... | collective-permute-start | bytes 196616 | tf_op jit(solution)/shard_map/ppermute | solution.py:243
  113.6 9.3 %collective-permute-start.28 = (f32[1,64,256]{2,1,0:T(8,128)S(1)}, f32[1,64,256]{2,1,0:T(8,128)S(1)}, u32[]{:S(2)}, u32[]{:S(2)}) collective-permute-start(f32[1,64,256]{2,1,0:T(8,128)S(1)} %collective-permute-done.27.refs_2_), channel_id=1, source_target_pairs={{0,1},{1,0},{2,3},{3,2},{4,5},{5,4},{6,7},{7,6},{8,9},{9,8},{10,11... | collective-permute-start | bytes 196616 | tf_op jit(solution)/shard_map/ppermute | solution.py:243
  (13 other events, 48.3 us)

commit v2 on v0

v2 whole, which is shorter than its diff:
```python
import functools

import jax
import jax.numpy as jnp
from jax import lax
from jax.experimental import pallas as pl
from jax.experimental.pallas import tpu as pltpu
from jax.sharding import PartitionSpec as P

F32 = jnp.float32
BF16 = jnp.bfloat16
HBM = pl.BlockSpec(memory_space=pltpu.HBM)
SMEM = pl.BlockSpec(memory_space=pltpu.SMEM)
VMEM = pl.BlockSpec(memory_space=pltpu.VMEM)


def product(left, right):
    return jnp.dot(left, right, precision=lax.Precision.HIGHEST, preferred_element_type=F32)


def contract(left, right):
    return lax.dot_general(
        left, right, (((0,), (0,)), ((), ())), precision=lax.Precision.HIGHEST, preferred_element_type=F32
    )


def spread_2(array, axis, root):
    mine = lax.axis_index(axis) == root
    return lax.psum(jnp.where(mine, array, jnp.zeros_like(array)), axis)


def any_mesh(
    known, lower_two, lower_one, top_one, inner_two, inner_one, heights, pattern_two, pattern_one
):
    width = top_one.shape[0]
    piece = lower_two.shape[0]
    n_col = lax.axis_size("pcol")
    ratio = lax.axis_size("prow") // n_col
    row_index = lax.axis_index("prow")
    col_index = lax.axis_index("pcol")
    live = (jnp.arange(width)[None, :] < heights[:, None]).astype(F32).reshape(-1)
    own_start = (row_index * n_col + col_index) * piece
    own_live = lax.dynamic_slice_in_dim(live, own_start, piece)

    def mask_own(lower, pattern):
        keep = live * jnp.repeat(pattern.astype(F32), width)
        return lower * lax.dynamic_slice_in_dim(keep, own_start, piece)[:, None]

    def spread(own_rows):
        band = lax.all_gather(own_rows, "pcol", axis=0, tiled=True)
        return jnp.concatenate(
            [spread_2(band, "prow", col_index * ratio + offset) for offset in range(ratio)], axis=0
        )

    def total_rows(partial_value):
        return lax.psum_scatter(partial_value, "pcol", scatter_dimension=0, tiled=True)

    own_two = mask_own(lower_two, pattern_two)
    own_one = mask_own(lower_one, pattern_one)
    partial_two = product(known, spread(own_two))
    partial_one = product(known, spread(own_one))
    column_two = -(own_live[:, None] * total_rows(partial_two))
    first_term, second_term = lax.psum(
        (contract(own_two, column_two), contract(column_two, own_one)), ("prow", "pcol")
    )
    diag_two = inner_two - first_term
    cross_block = -(second_term + product(diag_two, top_one))
    column_one = -(own_live[:, None] * (total_rows(partial_one) + product(column_two, top_one)))
    third_term = lax.psum(contract(own_one, column_one), ("prow", "pcol"))
    diag_one = inner_one - third_term - contract(top_one, cross_block)
    return (column_two, diag_two, column_one, cross_block, diag_one)


def halves(value):
    high = value.astype(BF16)
    return high, (value - high.astype(F32)).astype(BF16)


def dot3(left, right, dims):
    (lh, ll), (rh, rl) = left, right
    dot = lambda a, b: lax.dot_general(a, b, (dims, ((), ())), preferred_element_type=F32)
    return dot(lh, rh) + (dot(lh, rl) + dot(ll, rh))


ROWS_BY_COLUMNS = ((1,), (0,))
ROWS_BY_ROWS = ((0,), (0,))


def keep_rows(block, limit):
    row = lax.broadcasted_iota(jnp.int32, block.shape, 0)
    return jnp.where(row < limit, block, 0.0)


def limits(megabytes):
    return pltpu.CompilerParams(vmem_limit_bytes=megabytes * 2**20)


def cost(flops, moved):
    return pl.CostEstimate(flops=flops, bytes_accessed=moved, transcendentals=0)


def live_rows(at, n, which):
    return at[2 + which]


def kept_rows(at, n, side, which):
    return at[2 + which] * at[2 + n * n * (1 + side) + which]


def masked(block, at, n, which):
    width = block.shape[-1]
    return jnp.concatenate(
        [
            keep_rows(block[side * width : (side + 1) * width], kept_rows(at, n, side, which))
            for side in range(2)
        ],
        axis=1,
    )


def tile_copies(n, col, known, tiles, sems):
    width = tiles.shape[1]
    copies = [
        pltpu.make_async_copy(
            known.at[pl.ds(pl.multiple_of((a ^ col) * width, width), width)], tiles.at[a], sems.at[a]
        )
        for a in range(n)
    ]
    for copy in copies:
        copy.start()
    return copies


def pair_kernel(two, one, out, sems):
    rows = two.shape[0]
    copies = [
        pltpu.make_async_copy(block, out.at[pl.ds(i * rows, rows)], sems.at[i])
        for i, block in enumerate((two, one))
    ]
    for copy in copies:
        copy.start()
    for copy in copies:
        copy.wait()


def pair_up(two, one):
    rows, width = two.shape
    return pl.pallas_call(
        pair_kernel,
        out_shape=jax.ShapeDtypeStruct((2 * rows, width), F32),
        in_specs=[HBM, HBM],
        out_specs=VMEM,
        scratch_shapes=[pltpu.SemaphoreType.DMA((2,))],
        compiler_params=limits(4),
        cost_estimate=cost(0, 16 * rows * width),
        name="pair_rows",
    )(two, one)


def left_kernel(n, at, known, *refs):
    plane, (high, low, tiles, total, sems) = refs[:2], refs[2:]
    row, col = at[0], at[1]
    height = 2 * tiles.shape[1]
    copies = tile_copies(n, col, known, tiles, sems)
    for a in range(n):
        rows = plane[a >> 1][(a & 1) * height : (a & 1) * height + height]
        rows = halves(masked(rows, at, n, row * n + (a ^ col)))
        copies[a].wait()
        term = dot3(rows, halves(tiles[a]), ROWS_BY_ROWS)
        total[...] = term if a == 0 else total[...] + term
    high[...], low[...] = halves(total[...])


def left_product(n, at, known, plane):
    rows, span = known.shape
    width = rows // n
    half = jax.ShapeDtypeStruct((2 * width, span), BF16)
    return pl.pallas_call(
        functools.partial(left_kernel, n),
        out_shape=(half, half),
        in_specs=[SMEM, HBM, VMEM, VMEM],
        out_specs=(VMEM, VMEM),
        scratch_shapes=[
            pltpu.VMEM((n, width, span), F32),
            pltpu.VMEM((2 * width, span), F32),
            pltpu.SemaphoreType.DMA((n,)),
        ],
        compiler_params=limits(24),
        cost_estimate=cost(12 * rows * span * width, 4 * rows * span),
        name="left_product",
    )(at, known, *plane)


def gathered_halves(n, at, gathered, high, low):
    row, col = at[0], at[1]
    width = gathered[0].shape[-1]
    for k in range(n):
        block = row ^ k
        h, l = halves(masked(gathered[k][...], at, n, col * n + block))
        where = pl.ds(pl.multiple_of(block * width, width), width)
        high[where] = h
        low[where] = l


def sums_kernel(n, at, left_high, left_low, *refs):
    gathered, (keep, send, high, low, total) = refs[:n], refs[n:]
    col = at[1]
    width = total.shape[-1]
    gathered_halves(n, at, gathered, high, low)
    two = (high[:, :width], low[:, :width])
    one = (high[:, width:], low[:, width:])
    total[: 2 * width] = dot3((left_high[...], left_low[...]), two, ROWS_BY_COLUMNS)
    total[2 * width :] = dot3((left_high[width:], left_low[width:]), one, ROWS_BY_COLUMNS)
    quarter = width // n
    for e in range(n):
        for s in range(3):
            start = pl.multiple_of(s * width + (e ^ col) * quarter, quarter)
            where = pl.ds(((e >> 1) * 3 + s) * quarter, quarter)
            (send if e & 1 else keep)[where] = total[pl.ds(start, quarter)]


def small_sums(n, at, left, gathered):
    span = left[0].shape[1]
    width = gathered[0].shape[-1]
    half = jax.ShapeDtypeStruct((3 * width // 2, width), F32)
    return pl.pallas_call(
        functools.partial(sums_kernel, n),
        out_shape=(half, half),
        in_specs=[SMEM] + [VMEM] * (2 + n),
        out_specs=(VMEM, VMEM),
        scratch_shapes=[
            pltpu.VMEM((span, 2 * width), BF16),
            pltpu.VMEM((span, 2 * width), BF16),
            pltpu.VMEM((3 * width, width), F32),
        ],
        compiler_params=limits(16),
        cost_estimate=cost(18 * span * width * width, 4 * span * width),
        name="small_sums",
    )(at, *left, *gathered)


def band_kernel(n, at, known, *refs):
    gathered, (keep, send, tiles, high, low, sems) = refs[:n], refs[n:]
    copies = tile_copies(n, at[1], known, tiles, sems)
    gathered_halves(n, at, gathered, high, low)
    right = (high[...], low[...])
    for a in range(n):
        copies[a].wait()
        (send if a & 1 else keep)[a >> 1] = dot3(halves(tiles[a]), right, ROWS_BY_COLUMNS)


def band_product(n, at, known, gathered):
    rows, span = known.shape
    width = rows // n
    half = jax.ShapeDtypeStruct((n // 2, width, 2 * width), F32)
    return pl.pallas_call(
        functools.partial(band_kernel, n),
        out_shape=(half, half),
        in_specs=[SMEM, HBM] + [VMEM] * n,
        out_specs=(VMEM, VMEM),
        scratch_shapes=[
            pltpu.VMEM((n, width, span), F32),
            pltpu.VMEM((span, 2 * width), BF16),
            pltpu.VMEM((span, 2 * width), BF16),
            pltpu.SemaphoreType.DMA((n,)),
        ],
        compiler_params=limits(24),
        cost_estimate=cost(12 * rows * span * width, 4 * rows * span),
        name="band_product",
    )(at, known, *gathered)


def column_kernel(n, at, keep, got, other, top, two, one):
    width = top.shape[0]
    limit = live_rows(at, n, at[0] * n + at[1])
    total = keep[0] + got[0] + other[...]
    column_two = keep_rows(-total[:, :width], limit)
    two[...] = column_two
    second = total[:, width:] + dot3(halves(column_two), halves(top[...]), ROWS_BY_COLUMNS)
    one[...] = keep_rows(-second, limit)


def columns(n, at, keep, got, other, top):
    shape = jax.ShapeDtypeStruct(top.shape, F32)
    return pl.pallas_call(
        functools.partial(column_kernel, n),
        out_shape=(shape, shape),
        in_specs=[SMEM] + [VMEM] * 4,
        out_specs=(VMEM, VMEM),
        compiler_params=limits(8),
        name="column_rows",
    )(at, keep, got, other, top)


def blocks_kernel(n, at, top, inner_two, inner_one, first, second, diag_two, cross, diag_one, sums):
    col = at[1]
    quarter = top.shape[0] // n
    for e, (part, i) in enumerate(((first, 0), (second, 0), (first, 1), (second, 1))):
        for s in range(3):
            start = (i * 3 + s) * quarter
            where = pl.ds(pl.multiple_of((e ^ col) * quarter, quarter), quarter)
            sums[s, where] = part[start : start + quarter]
    t = halves(top[...])
    d = inner_two[...] + sums[0]
    diag_two[...] = d
    c = sums[1].T - dot3(halves(d), t, ROWS_BY_COLUMNS)
    cross[...] = c
    diag_one[...] = (
        inner_one[...]
        + sums[2]
        - dot3(halves(sums[1]), t, ROWS_BY_COLUMNS)
        - dot3(t, halves(c), ROWS_BY_ROWS)
    )


def small_blocks(n, at, top, inner_two, inner_one, parts):
    shape = jax.ShapeDtypeStruct(top.shape, F32)
    return pl.pallas_call(
        functools.partial(blocks_kernel, n),
        out_shape=(shape, shape, shape),
        in_specs=[SMEM] + [VMEM] * 5,
        out_specs=(VMEM,) * 3,
        scratch_shapes=[pltpu.VMEM((3,) + top.shape, F32)],
        compiler_params=limits(8),
        name="small_blocks",
    )(at, top, inner_two, inner_one, *parts)


def after(value, *others):
    return lax.optimization_barrier((value, *others))[0]


def square_mesh(
    known, lower_two, lower_one, top_one, inner_two, inner_one, heights, pattern_two, pattern_one
):
    n = lax.axis_size("pcol")
    place = jnp.stack([lax.axis_index("prow"), lax.axis_index("pcol")]).astype(jnp.int32)
    at = jnp.concatenate([place, heights, pattern_two, pattern_one])

    def along(axis, k, array):
        return lax.ppermute(array, axis, [(i, i ^ k) for i in range(n)])

    core = functools.partial(along, "pcol", 1)
    across = functools.partial(along, "pcol", 2)

    def direct(k, rows):
        pairs = [(z * n + j, (j ^ k) * n + z) for z in range(n) for j in range(n)]
        return lax.ppermute(rows, ("prow", "pcol"), pairs)

    pair = pair_up(lower_two, lower_one)
    gathered = [direct(k, pair) for k in range(n)]
    four = pair_up(pair, core(pair))
    plane = [four, across(four)]
    left = left_product(n, at, known, plane)

    keep_sums, send_sums = small_sums(n, at, left, gathered)
    mine = keep_sums + core(send_sums)
    half = mine.shape[0] // 2
    keep, send = band_product(n, after(at, mine), known, gathered)
    mine = mine[:half] + across(mine[half:])
    got = core(after(send, mine))
    mine = mine + along("prow", 1, mine)
    other = across(after(keep[1] + got[1], mine))
    mine = mine + along("prow", 2, mine)
    column_two, column_one = columns(n, at, keep, got, other, top_one)
    both = jnp.concatenate([after(mine, column_one), across(mine)])
    both = both, core(both)
    diag_two, cross_block, diag_one = small_blocks(n, at, top_one, inner_two, inner_one, both)
    return (column_two, diag_two, column_one, cross_block, diag_one)


def per_device(known, lower_two, lower_one, top_one, *rest):
    square = lax.axis_size("prow") == 4 and lax.axis_size("pcol") == 4
    body = square_mesh if square and lower_two.shape == top_one.shape else any_mesh
    return body(known, lower_two, lower_one, top_one, *rest)


def solution(mesh):
    return jax.shard_map(
        per_device,
        mesh=mesh,
        in_specs=(
            P(("pole", "prow"), "pcol"),
            P(("pole", "prow", "pcol"), None),
            P(("pole", "prow", "pcol"), None),
            P("pole", None),
            P("pole", None),
            P("pole", None),
            P(),
            P(),
            P(),
        ),
        out_specs=(
            P(("pole", "prow", "pcol"), None),
            P("pole", None),
            P(("pole", "prow", "pcol"), None),
            P("pole", None),
            P("pole", None),
        ),
        check_vma=False,
    )
```

time: 310 us -> 104 us (0.34)
  waiting for transfers between devices: 252 us -> 54.5 us
  matrix products: 29.4 us -> 0 us
  starting transfers between devices: 0.43 us -> 25.3 us
  Pallas kernels: 0 us -> 18.4 us
  between operations: 14.2 us -> 0.83 us
  other arithmetic: 12.2 us -> 0.21 us
    psum x2 -> x0, waiting for transfers between devices: 180 us -> none  [the longest x1 92.7 us: total_terms(): return lax.psum(terms, ('prow', 'pcol'))]
    ppermute x0 -> x14, waiting for transfers between devices: none -> 54.5 us  [the longest x10 54.5 us: along(): return lax.ppermute(array, axis, [(i, i ^ k) for i in range(n)])]
    reduce_scatter x2 -> x0, waiting for transfers between devices: 37.4 us -> none  [total_rows(): lax.psum_scatter(partial_value, 'pcol', scatter_dimension=0, tiled=True)]
    all_gather x2 -> x0, waiting for transfers between devices: 34.2 us -> none  [spread(): band = lax.all_gather(own_rows, 'pcol', axis=0, tiled=True)]
    dot_general x8 -> x0, matrix products: 29.4 us -> none  [the longest x4 23.4 us: product(): jnp.dot(left, right, precision=lax.Precision.HIGHEST, preferred_element_t...]
    ppermute x0 -> x14, starting transfers between devices: none -> 25.3 us  [the longest x10 16.7 us: along(): return lax.ppermute(array, axis, [(i, i ^ k) for i in range(n)])]
    pallas_call x0 -> x7, Pallas kernels: none -> 18.4 us  [the longest x1 6.41 us: band_product(): pl.pallas_call(functools.partial(band_kernel, n), out_shape=(half, half),...]
    select_n x2 -> x0, other arithmetic: 4.56 us -> none  [spread_2(): return lax.psum(jnp.where(mine, array, jnp.zeros_like(array)), axis)]
  transfers between devices with their start and end apart: 6 -> 14, of which waited for: 6 -> 7; matrix products, arithmetic and copies ran while one was open for 6% -> 1% of each run, Pallas kernels for 0% -> 12%
where the time goes in v2:
time: 104 us
  waiting for transfers between devices  54.5 us (52%)
  starting transfers between devices  25.3 us (24%)
  Pallas kernels  18.4 us (18%)
  local copies, waits for them, and re-layouts  4.9 us (5%)
    ppermute x10, waiting for transfers between devices, along(): return lax.ppermute(array, axis, [(i, i ^ k) for i in range(n)])  54.5 us
    ppermute x10, starting transfers between devices, along(): return lax.ppermute(array, axis, [(i, i ^ k) for i in range(n)])  16.7 us
    ppermute x4, starting transfers between devices, direct(): return lax.ppermute(rows, ('prow', 'pcol'), pairs)  8.6 us
    pallas_call x1, Pallas kernels, band_product(): pl.pallas_call(functools.partial(band_kernel, n), out_shape=(half, half),...  6.41 us
    pallas_call x1, Pallas kernels, left_product(): pl.pallas_call(functools.partial(left_kernel, n), out_shape=(half, half),...  5.05 us
    unnamed x13, local copies, waits for them, and re-layouts  4.11 us
    pallas_call x1, Pallas kernels, small_sums(): pl.pallas_call(functools.partial(sums_kernel, n), out_shape=(half, half),...  3.39 us
  transfers between devices with their start and end apart: 14, of which 7 were waited for; matrix products, arithmetic and copies ran while one was open for 1% of the time, Pallas kernels for 12%

profile of v2, /device:TPU:0, one launch (start us, length us, event | category | flops | bytes accessed | tf_op | source)
XLA Modules:
  0.0 104.2 jit_solution(905197731345112456)
XLA Ops:
  0.6 0.9 copy-done.1
  1.6 0.9 copy-done.2
  2.6 0.5 collective-permute-start
  3.1 1.5 %collective-permute-done.one = f32[512,256]{1,0:T(8,128)S(1)} collective-permute-done((f32[512,256]{1,0:T(8,128)S(1)}, f32[512,256]{1,0:T(8,128)S(1)}, u32[]{:S(2)}, u32[]{:S(2)}) %collective-permute-start) | collective-permute-done | bytes 524320 | tf_op jit(solution)/shard_map/ppermute | solution.py:341
  4.7 0.1 pair_rows.3.refs_0_
  4.8 2.9 %collective-permute-start.1 = (f32[1024,256]{1,0:T(8,128)S(1)}, f32[1024,256]{1,0:T(8,128)S(1)}, u32[]{:S(2)}, u32[]{:S(2)}) collective-permute-start(f32[1024,256]{1,0:T(8,128)S(1)} %pair_rows.3.refs_0_), channel_id=1, source_target_pairs={{0,2},{1,3},{2,0},{3,1},{4,6},{5,7},{6,4},{7,5},{8,10},{9,11},{10,... | collective-permute-start | bytes 3145736 | tf_op jit(solution)/shard_map/ppermute | solution.py:341
  7.7 0.7 collective-permute-start.2
  8.4 2.9 %collective-permute-start.3 = (f32[512,256]{1,0:T(8,128)S(1)}, f32[512,256]{1,0:T(8,128)}, u32[]{:S(2)}, u32[]{:S(2)}) collective-permute-start(f32[512,256]{1,0:T(8,128)S(1)} %pair_rows.2.two), channel_id=1, source_target_pairs={{0,4},{1,0},{2,12},{3,8},{4,5},{5,1},{6,13},{7,9},{8,6},{9,2},{10,... | collective-permute-start | bytes 1572872 | tf_op jit(solution)/shard_map/ppermute | solution.py:348
  11.2 3.4 %collective-permute-start.4 = (f32[512,256]{1,0:T(8,128)S(1)}, f32[512,256]{1,0:T(8,128)}, u32[]{:S(2)}, u32[]{:S(2)}) collective-permute-start(f32[512,256]{1,0:T(8,128)S(1)} %pair_rows.2.two), channel_id=1, source_target_pairs={{0,8},{1,12},{2,0},{3,4},{4,9},{5,13},{6,1},{7,5},{8,10},{9,14},{1... | collective-permute-start | bytes 1572872 | tf_op jit(solution)/shard_map/ppermute | solution.py:348
  14.6 1.7 %collective-permute-start.5 = (f32[512,256]{1,0:T(8,128)S(1)}, f32[512,256]{1,0:T(8,128)}, u32[]{:S(2)}, u32[]{:S(2)}) collective-permute-start(f32[512,256]{1,0:T(8,128)S(1)} %pair_rows.2.two), channel_id=1, source_target_pairs={{0,12},{1,8},{2,4},{3,0},{4,13},{5,9},{6,5},{7,1},{8,14},{9,10},{1... | collective-permute-start | bytes 1572872 | tf_op jit(solution)/shard_map/ppermute | solution.py:348
  16.3 0.8 concatenate.6.at
  17.0 31.2 %collective-permute-done.1.refs_1_ = f32[1024,256]{1,0:T(8,128)S(1)} collective-permute-done((f32[1024,256]{1,0:T(8,128)S(1)}, f32[1024,256]{1,0:T(8,128)S(1)}, u32[]{:S(2)}, u32[]{:S(2)}) %collective-permute-start.1) | collective-permute-done | bytes 1048608 | tf_op jit(solution)/shard_map/ppermute | solution.py:341
  48.3 2.2 %copy-done.5 = f32[1024,1024]{1,0:T(8,128)S(1)} copy-done((f32[1024,1024]{1,0:T(8,128)S(1)}, f32[1024,1024]{1,0:T(8,128)}, u32[]{:S(2)}) %copy-start.5) | copy-done | bytes 4194328
  50.5 5.1 %left_product.1 = (bf16[512,1024]{1,0:T(8,128)(2,1)S(1)}, bf16[512,1024]{1,0:T(8,128)(2,1)S(1)}) custom-call(s32[50]{0:T(128)S(1)} %concatenate.6.at, f32[1024,1024]{1,0:T(8,128)S(1)} %copy-done.5, f32[1024,256]{1,0:T(8,128)S(1)} %pair_rows.3.refs_0_, f32[1024,256]{1,0:T(8,128)S(1)} %collective-permute-done.1.refs_1_), custom_call_target="tpu_custom_call" | custom-call | flops 3221225472 | bytes 4194304 | tf_op jit(solution)/shard_map/left_product/pallas_call | solution.py:178
  55.6 3.4 %small_sums.1 = (f32[384,256]{1,0:T(8,128)S(1)}, f32[384,256]{1,0:T(8,128)S(1)}) custom-call(s32[50]{0:T(128)S(1)} %concatenate.6.at, bf16[512,1024]{1,0:T(8,128)(2,1)S(1)} %get-tuple-element.20.left_high, bf16[512,1024]{1,0:T(8,128)(2,1)S(1)} %get-tuple-element.21.left_low, f32[512,256]{1,0:T(8,128)S(1)} %collective-permute-done.2.refs_0_, ...), custom_call_target="tpu_custom_call" | custom-call | flops 1207959552 | bytes 1048576 | tf_op jit(solution)/shard_map/small_sums/pallas_call | solution.py:226
  59.0 0.1 collective-permute-start.6
  59.1 1.7 %collective-permute-done.6 = f32[384,256]{1,0:T(8,128)S(1)} collective-permute-done((f32[384,256]{1,0:T(8,128)S(1)}, f32[384,256]{1,0:T(8,128)S(1)}, u32[]{:S(2)}, u32[]{:S(2)}) %collective-permute-start.6) | collective-permute-done | bytes 393248 | tf_op jit(solution)/shard_map/ppermute | solution.py:341
  60.9 4.6 %collective-permute-start.7 = (f32[192,256]{1,0:T(8,128)S(1)}, f32[192,256]{1,0:T(8,128)S(1)}, u32[]{:S(2)}, u32[]{:S(2)}) collective-permute-start(f32[192,256]{1,0:T(8,128)S(1)} %slice.17), channel_id=1, source_target_pairs={{0,2},{1,3},{2,0},{3,1},{4,6},{5,7},{6,4},{7,5},{8,10},{9,11},{10,... | collective-permute-start | bytes 589832 | tf_op jit(solution)/shard_map/ppermute | solution.py:341
  65.5 6.4 %band_product.1 = (f32[2,256,512]{2,1,0:T(8,128)S(1)}, f32[2,256,512]{2,1,0:T(8,128)S(1)}) custom-call(s32[50]{0:T(128)S(1)} %concatenate.6.at, f32[1024,1024]{1,0:T(8,128)S(1)} %copy-done.5, f32[512,256]{1,0:T(8,128)S(1)} %collective-permute-done.2.refs_0_, f32[512,256]{1,0:T(8,128)} %collective-permute-done.3.refs_1_, ...), custom_call_target="tpu_custom_call" | custom-call | flops 3221225472 | bytes 4194304 | tf_op jit(solution)/shard_map/band_product/pallas_call | solution.py:256
  72.0 0.1 collective-permute-start.8
  72.1 2.7 %collective-permute-start.9 = (f32[192,256]{1,0:T(8,128)S(1)}, f32[192,256]{1,0:T(8,128)S(1)}, u32[]{:S(2)}, u32[]{:S(2)}) collective-permute-start(f32[192,256]{1,0:T(8,128)S(1)} %slice_add_fusion.1), channel_id=1, source_target_pairs={{0,4},{4,0},{8,12},{12,8},{1,5},{5,1},{9,13},{13,9},{2,6},{6,2},{1... | collective-permute-start | bytes 589832 | tf_op jit(solution)/shard_map/ppermute | solution.py:341
  74.8 5.5 %collective-permute-done.9 = f32[192,256]{1,0:T(8,128)S(1)} collective-permute-done((f32[192,256]{1,0:T(8,128)S(1)}, f32[192,256]{1,0:T(8,128)S(1)}, u32[]{:S(2)}, u32[]{:S(2)}) %collective-permute-start.9) | collective-permute-done | bytes 196640 | tf_op jit(solution)/shard_map/ppermute | solution.py:341
  80.3 0.1 fusion
  80.4 1.4 %collective-permute-start.10 = (f32[256,512]{1,0:T(8,128)S(1)}, f32[256,512]{1,0:T(8,128)S(1)}, u32[]{:S(2)}, u32[]{:S(2)}) collective-permute-start(f32[256,512]{1,0:T(8,128)S(1)} %fusion), channel_id=1, source_target_pairs={{0,2},{1,3},{2,0},{3,1},{4,6},{5,7},{6,4},{7,5},{8,10},{9,11},{10,... | collective-permute-start | bytes 1572872 | tf_op jit(solution)/shard_map/ppermute | solution.py:341
  81.8 3.5 %collective-permute-start.11 = (f32[192,256]{1,0:T(8,128)S(1)}, f32[192,256]{1,0:T(8,128)S(1)}, u32[]{:S(2)}, u32[]{:S(2)}) collective-permute-start(f32[192,256]{1,0:T(8,128)S(1)} %add.22), channel_id=1, source_target_pairs={{0,8},{4,12},{8,0},{12,4},{1,9},{5,13},{9,1},{13,5},{2,10},{6,14},... | collective-permute-start | bytes 589832 | tf_op jit(solution)/shard_map/ppermute | solution.py:341
  85.3 8.7 %collective-permute-done.11 = f32[192,256]{1,0:T(8,128)S(1)} collective-permute-done((f32[192,256]{1,0:T(8,128)S(1)}, f32[192,256]{1,0:T(8,128)S(1)}, u32[]{:S(2)}, u32[]{:S(2)}) %collective-permute-start.11) | collective-permute-done | bytes 196640 | tf_op jit(solution)/shard_map/ppermute | solution.py:341
  94.0 0.8 collective-permute-start.12
  94.8 1.5 %column_rows.1 = (f32[256,256]{1,0:T(8,128)}, f32[256,256]{1,0:T(8,128)}) custom-call(s32[50]{0:T(128)S(1)} %concatenate.6.at, f32[2,256,512]{2,1,0:T(8,128)S(1)} %get-tuple-element.25.keep, f32[2,256,512]{2,1,0:T(8,128)S(1)} %collective-permute-done.8.got, f32[256,512]{1,0:T(8,128)S(1)} %collective-permute-done.10.other, f32[256,256]{1,0:T(8,128)S(1)} %copy-done), custom_call_target="tpu_custom_call" | custom-call | tf_op jit(solution)/shard_map/column_rows/pallas_call | solution.py:285
  96.3 4.2 %collective-permute-done.12 = f32[192,256]{1,0:T(8,128)S(1)} collective-permute-done((f32[192,256]{1,0:T(8,128)S(1)}, f32[192,256]{1,0:T(8,128)S(1)}, u32[]{:S(2)}, u32[]{:S(2)}) %collective-permute-start.12) | collective-permute-done | bytes 196640 | tf_op jit(solution)/shard_map/ppermute | solution.py:341
  100.5 0.1 collective-permute-start.13
  100.6 1.7 %collective-permute-done.13.second = f32[384,256]{1,0:T(8,128)S(1)} collective-permute-done((f32[384,256]{1,0:T(8,128)S(1)}, f32[384,256]{1,0:T(8,128)S(1)}, u32[]{:S(2)}, u32[]{:S(2)}) %collective-permute-start.13) | collective-permute-done | bytes 393248 | tf_op jit(solution)/shard_map/ppermute | solution.py:341
  102.3 1.9 %small_blocks.1 = (f32[256,256]{1,0:T(8,128)}, f32[256,256]{1,0:T(8,128)}, f32[256,256]{1,0:T(8,128)}) custom-call(s32[50]{0:T(128)S(1)} %concatenate.6.at, f32[256,256]{1,0:T(8,128)S(1)} %copy-done, f32[256,256]{1,0:T(8,128)S(1)} %copy-done.3, f32[256,256]{1,0:T(8,128)S(1)} %copy-done.4, f32[384,256]{1,0:T(8,128)S(1)} %constant_dynamic-update-slice_fusion.first, ...), custom_call_target="tpu_custom_call" | custom-call | tf_op jit(solution)/shard_map/small_blocks/pallas_call | solution.py:318
  (24 shorter events, 0.3 us)
Async XLA Ops:
  0.6 1.0 copy-start.1
  1.6 0.9 copy-start.2
  2.6 2.1 %collective-permute-start = (f32[512,256]{1,0:T(8,128)S(1)}, f32[512,256]{1,0:T(8,128)S(1)}, u32[]{:S(2)}, u32[]{:S(2)}) collective-permute-start(f32[512,256]{1,0:T(8,128)S(1)} %pair_rows.2.two), channel_id=1, source_target_pairs={{0,1},{1,0},{2,3},{3,2},{4,5},{5,4},{6,7},{7,6},{8,9},{9,8},{10,11... | collective-permute-start | bytes 1572872 | tf_op jit(solution)/shard_map/ppermute | solution.py:341
  4.8 43.5 %collective-permute-start.1 = (f32[1024,256]{1,0:T(8,128)S(1)}, f32[1024,256]{1,0:T(8,128)S(1)}, u32[]{:S(2)}, u32[]{:S(2)}) collective-permute-start(f32[1024,256]{1,0:T(8,128)S(1)} %pair_rows.3.refs_0_), channel_id=1, source_target_pairs={{0,2},{1,3},{2,0},{3,1},{4,6},{5,7},{6,4},{7,5},{8,10},{9,11},{10,... | collective-permute-start | bytes 3145736 | tf_op jit(solution)/shard_map/ppermute | solution.py:341
  7.7 47.9 %collective-permute-start.2 = (f32[512,256]{1,0:T(8,128)S(1)}, f32[512,256]{1,0:T(8,128)S(1)}, u32[]{:S(2)}, u32[]{:S(2)}) collective-permute-start(f32[512,256]{1,0:T(8,128)S(1)} %pair_rows.2.two), channel_id=1, source_target_pairs={{0,0},{1,4},{2,8},{3,12},{4,1},{5,5},{6,9},{7,13},{8,2},{9,6},{10,... | collective-permute-start | bytes 1572872 | tf_op jit(solution)/shard_map/ppermute | solution.py:348
  8.4 47.2 %collective-permute-start.3 = (f32[512,256]{1,0:T(8,128)S(1)}, f32[512,256]{1,0:T(8,128)}, u32[]{:S(2)}, u32[]{:S(2)}) collective-permute-start(f32[512,256]{1,0:T(8,128)S(1)} %pair_rows.2.two), channel_id=1, source_target_pairs={{0,4},{1,0},{2,12},{3,8},{4,5},{5,1},{6,13},{7,9},{8,6},{9,2},{10,... | collective-permute-start | bytes 1572872 | tf_op jit(solution)/shard_map/ppermute | solution.py:348
  11.2 44.3 %collective-permute-start.4 = (f32[512,256]{1,0:T(8,128)S(1)}, f32[512,256]{1,0:T(8,128)}, u32[]{:S(2)}, u32[]{:S(2)}) collective-permute-start(f32[512,256]{1,0:T(8,128)S(1)} %pair_rows.2.two), channel_id=1, source_target_pairs={{0,8},{1,12},{2,0},{3,4},{4,9},{5,13},{6,1},{7,5},{8,10},{9,14},{1... | collective-permute-start | bytes 1572872 | tf_op jit(solution)/shard_map/ppermute | solution.py:348
  14.6 41.0 %collective-permute-start.5 = (f32[512,256]{1,0:T(8,128)S(1)}, f32[512,256]{1,0:T(8,128)}, u32[]{:S(2)}, u32[]{:S(2)}) collective-permute-start(f32[512,256]{1,0:T(8,128)S(1)} %pair_rows.2.two), channel_id=1, source_target_pairs={{0,12},{1,8},{2,4},{3,0},{4,13},{5,9},{6,5},{7,1},{8,14},{9,10},{1... | collective-permute-start | bytes 1572872 | tf_op jit(solution)/shard_map/ppermute | solution.py:348
  48.3 2.2 %copy-start.5 = (f32[1024,1024]{1,0:T(8,128)S(1)}, f32[1024,1024]{1,0:T(8,128)}, u32[]{:S(2)}) copy-start(f32[1024,1024]{1,0:T(8,128)} %known.3) | copy-start | bytes 12582916
  59.0 1.8 %collective-permute-start.6 = (f32[384,256]{1,0:T(8,128)S(1)}, f32[384,256]{1,0:T(8,128)S(1)}, u32[]{:S(2)}, u32[]{:S(2)}) collective-permute-start(f32[384,256]{1,0:T(8,128)S(1)} %get-tuple-element.23), channel_id=1, source_target_pairs={{0,1},{1,0},{2,3},{3,2},{4,5},{5,4},{6,7},{7,6},{8,9},{9,8},{10,11... | collective-permute-start | bytes 1179656 | tf_op jit(solution)/shard_map/ppermute | solution.py:341
  60.9 33.9 %copy-start = (f32[256,256]{1,0:T(8,128)S(1)}, f32[256,256]{1,0:T(8,128)}, u32[]{:S(2)}) copy-start(f32[256,256]{1,0:T(8,128)} %top.3) | copy-start | bytes 786436
  60.9 11.1 %collective-permute-start.7 = (f32[192,256]{1,0:T(8,128)S(1)}, f32[192,256]{1,0:T(8,128)S(1)}, u32[]{:S(2)}, u32[]{:S(2)}) collective-permute-start(f32[192,256]{1,0:T(8,128)S(1)} %slice.17), channel_id=1, source_target_pairs={{0,2},{1,3},{2,0},{3,1},{4,6},{5,7},{6,4},{7,5},{8,10},{9,11},{10,... | collective-permute-start | bytes 589832 | tf_op jit(solution)/shard_map/ppermute | solution.py:341
  71.9 30.4 %copy-start.3 = (f32[256,256]{1,0:T(8,128)S(1)}, f32[256,256]{1,0:T(8,128)}, u32[]{:S(2)}) copy-start(f32[256,256]{1,0:T(8,128)} %inner_two.1) | copy-start | bytes 786436
  71.9 30.4 %copy-start.4 = (f32[256,256]{1,0:T(8,128)S(1)}, f32[256,256]{1,0:T(8,128)}, u32[]{:S(2)}) copy-start(f32[256,256]{1,0:T(8,128)} %inner_one.1) | copy-start | bytes 786436
  72.0 8.3 %collective-permute-start.8 = (f32[2,256,512]{2,1,0:T(8,128)S(1)}, f32[2,256,512]{2,1,0:T(8,128)S(1)}, u32[]{:S(2)}, u32[]{:S(2)}) collective-permute-start(f32[2,256,512]{2,1,0:T(8,128)S(1)} %get-tuple-element.27), channel_id=1, source_target_pairs={{0,1},{1,0},{2,3},{3,2},{4,5},{5,4},{6,7},{7,6},{8,9},{9,8},{10,11... | collective-permute-start | bytes 3145736 | tf_op jit(solution)/shard_map/ppermute | solution.py:341
  72.1 8.2 %collective-permute-start.9 = (f32[192,256]{1,0:T(8,128)S(1)}, f32[192,256]{1,0:T(8,128)S(1)}, u32[]{:S(2)}, u32[]{:S(2)}) collective-permute-start(f32[192,256]{1,0:T(8,128)S(1)} %slice_add_fusion.1), channel_id=1, source_target_pairs={{0,4},{4,0},{8,12},{12,8},{1,5},{5,1},{9,13},{13,9},{2,6},{6,2},{1... | collective-permute-start | bytes 589832 | tf_op jit(solution)/shard_map/ppermute | solution.py:341
  80.4 14.3 %collective-permute-start.10 = (f32[256,512]{1,0:T(8,128)S(1)}, f32[256,512]{1,0:T(8,128)S(1)}, u32[]{:S(2)}, u32[]{:S(2)}) collective-permute-start(f32[256,512]{1,0:T(8,128)S(1)} %fusion), channel_id=1, source_target_pairs={{0,2},{1,3},{2,0},{3,1},{4,6},{5,7},{6,4},{7,5},{8,10},{9,11},{10,... | collective-permute-start | bytes 1572872 | tf_op jit(solution)/shard_map/ppermute | solution.py:341
  81.8 12.1 %collective-permute-start.11 = (f32[192,256]{1,0:T(8,128)S(1)}, f32[192,256]{1,0:T(8,128)S(1)}, u32[]{:S(2)}, u32[]{:S(2)}) collective-permute-start(f32[192,256]{1,0:T(8,128)S(1)} %add.22), channel_id=1, source_target_pairs={{0,8},{4,12},{8,0},{12,4},{1,9},{5,13},{9,1},{13,5},{2,10},{6,14},... | collective-permute-start | bytes 589832 | tf_op jit(solution)/shard_map/ppermute | solution.py:341
  94.0 6.5 %collective-permute-start.12 = (f32[192,256]{1,0:T(8,128)S(1)}, f32[192,256]{1,0:T(8,128)S(1)}, u32[]{:S(2)}, u32[]{:S(2)}) collective-permute-start(f32[192,256]{1,0:T(8,128)S(1)} %add.23), channel_id=1, source_target_pairs={{0,2},{1,3},{2,0},{3,1},{4,6},{5,7},{6,4},{7,5},{8,10},{9,11},{10,... | collective-permute-start | bytes 589832 | tf_op jit(solution)/shard_map/ppermute | solution.py:341
  100.5 1.8 %collective-permute-start.13 = (f32[384,256]{1,0:T(8,128)S(1)}, f32[384,256]{1,0:T(8,128)S(1)}, u32[]{:S(2)}, u32[]{:S(2)}) collective-permute-start(f32[384,256]{1,0:T(8,128)S(1)} %constant_dynamic-update-slice_fusion.first), channel_id=1, source_target_pairs={{0,1},{1,0},{2,3},{3,2},{4,5},{5,4},{6,7},{7,6},{8,9},{9,8},{10,11... | collective-permute-start | bytes 1179656 | tf_op jit(solution)/shard_map/ppermute | solution.py:341

commit v3 on v2

--- a/solution.py
+++ b/solution.py
@@ -118,99 +118,112 @@
     )
 
 
-def tile_copies(n, col, known, tiles, sems):
-    width = tiles.shape[1]
-    copies = [
-        pltpu.make_async_copy(
-            known.at[pl.ds(pl.multiple_of((a ^ col) * width, width), width)], tiles.at[a], sems.at[a]
-        )
-        for a in range(n)
-    ]
-    for copy in copies:
-        copy.start()
-    return copies
-
-
-def pair_kernel(two, one, out, sems):
-    rows = two.shape[0]
-    copies = [
-        pltpu.make_async_copy(block, out.at[pl.ds(i * rows, rows)], sems.at[i])
-        for i, block in enumerate((two, one))
-    ]
+def tile_rows(a, col, width):
+    return pl.ds(pl.multiple_of((a ^ col) * width, width), width)
+
+
+def stack_kernel(*refs):
+    blocks, out, sems = refs[:-2], refs[-2], refs[-1]
+    copies, start = [], 0
+    for i, block in enumerate(blocks):
+        rows = block.shape[0]
+        copies.append(pltpu.make_async_copy(block, out.at[pl.ds(start, rows)], sems.at[i]))
+        start += rows
     for copy in copies:
         copy.start()
     for copy in copies:
         copy.wait()
 
 
-def pair_up(two, one):
-    rows, width = two.shape
+def stack(*blocks):
+    rows = sum(block.shape[0] for block in blocks)
+    width = blocks[0].shape[1]
     return pl.pallas_call(
-        pair_kernel,
-        out_shape=jax.ShapeDtypeStruct((2 * rows, width), F32),
-        in_specs=[HBM, HBM],
+        stack_kernel,
+        out_shape=jax.ShapeDtypeStruct((rows, width), F32),
+        in_specs=[HBM] * len(blocks),
         out_specs=VMEM,
-        scratch_shapes=[pltpu.SemaphoreType.DMA((2,))],
+        scratch_shapes=[pltpu.SemaphoreType.DMA((len(blocks),))],
         compiler_params=limits(4),
-        cost_estimate=cost(0, 16 * rows * width),
-        name="pair_rows",
-    )(two, one)
-
-
-def left_kernel(n, at, known, *refs):
-    plane, (high, low, tiles, total, sems) = refs[:2], refs[2:]
+        cost_estimate=cost(0, 8 * rows * width),
+        name="stack_rows",
+    )(*blocks)
+
+
+def left_terms(n, first, at, known, plane):
     row, col = at[0], at[1]
-    height = 2 * tiles.shape[1]
-    copies = tile_copies(n, col, known, tiles, sems)
-    for a in range(n):
-        rows = plane[a >> 1][(a & 1) * height : (a & 1) * height + height]
-        rows = halves(masked(rows, at, n, row * n + (a ^ col)))
-        copies[a].wait()
-        term = dot3(rows, halves(tiles[a]), ROWS_BY_ROWS)
-        total[...] = term if a == 0 else total[...] + term
-    high[...], low[...] = halves(total[...])
-
-
-def left_product(n, at, known, plane):
+    width = known.shape[0] // n
+    terms = []
+    for i in range(2):
+        rows = plane[2 * i * width : 2 * (i + 1) * width]
+        rows = halves(masked(rows, at, n, row * n + ((first + i) ^ col)))
+        terms.append(dot3(rows, halves(known[tile_rows(first + i, col, width)]), ROWS_BY_ROWS))
+    return terms[0] + terms[1]
+
+
+def left_first_kernel(n, at, known, plane, out):
+    out[...] = left_terms(n, 0, at, known, plane)
+
+
+def left_last_kernel(n, at, known, plane, before, high, low):
+    total = before[...] + left_terms(n, 2, at, known, plane)
+    high[...], low[...] = halves(total)
+
+
+def call(kernel, name, megabytes, estimate, out_shape, *arrays, scratch=()):
+    return pl.pallas_call(
+        kernel,
+        out_shape=out_shape,
+        in_specs=[SMEM] + [VMEM] * (len(arrays) - 1),
+        out_specs=jax.tree.map(lambda _: VMEM, out_shape),
+        scratch_shapes=scratch,
+        compiler_params=limits(megabytes),
+        cost_estimate=estimate,
+        name=name,
+    )(*arrays)
+
+
+def left_product(n, at, known, here, there):
     rows, span = known.shape
-    width = rows // n
-    half = jax.ShapeDtypeStruct((2 * width, span), BF16)
-    return pl.pallas_call(
-        functools.partial(left_kernel, n),
-        out_shape=(half, half),
-        in_specs=[SMEM, HBM, VMEM, VMEM],
-        out_specs=(VMEM, VMEM),
-        scratch_shapes=[
-            pltpu.VMEM((n, width, span), F32),
-            pltpu.VMEM((2 * width, span), F32),
-            pltpu.SemaphoreType.DMA((n,)),
-        ],
-        compiler_params=limits(24),
-        cost_estimate=cost(12 * rows * span * width, 4 * rows * span),
-        name="left_product",
-    )(at, known, *plane)
-
-
-def gathered_halves(n, at, gathered, high, low):
+    shape = (2 * rows // n, span)
+    half = jax.ShapeDtypeStruct(shape, BF16)
+    first = call(
+        functools.partial(left_first_kernel, n), "left_first", 14, cost(0, 0),
+        jax.ShapeDtypeStruct(shape, F32), at, known, here,
+    )
+    return call(
+        functools.partial(left_last_kernel, n), "left_last", 14, cost(0, 0),
+        (half, half), at, known, there, first,
+    )
+
+
+def arrived_columns(row, m, width):
+    return pl.ds(pl.multiple_of(((row >> 1) ^ m) * (2 * width), 2 * width), 2 * width)
+
+
+def sums_kernel(n, m, at, left_high, left_low, arrived, *refs):
+    before, refs = (None, refs) if m == 0 else (refs[0], refs[1:])
+    out, high, low = refs[:-2], refs[-2], refs[-1]
     row, col = at[0], at[1]
-    width = gathered[0].shape[-1]
-    for k in range(n):
-        block = row ^ k
-        h, l = halves(masked(gathered[k][...], at, n, col * n + block))
-        where = pl.ds(pl.multiple_of(block * width, width), width)
-        high[where] = h
-        low[where] = l
-
-
-def sums_kernel(n, at, left_high, left_low, *refs):
-    gathered, (keep, send, high, low, total) = refs[:n], refs[n:]
-    col = at[1]
-    width = total.shape[-1]
-    gathered_halves(n, at, gathered, high, low)
+    width = arrived.shape[-1]
+    for e in range(2):
+        block = row ^ (2 * m + e)
+        rows = arrived[2 * e * width : 2 * (e + 1) * width]
+        where = pl.ds(pl.multiple_of((block & 1) * width, width), width)
+        high[where], low[where] = halves(masked(rows, at, n, col * n + block))
+    columns = arrived_columns(row, m, width)
+    left = (left_high[:, columns], left_low[:, columns])
     two = (high[:, :width], low[:, :width])
     one = (high[:, width:], low[:, width:])
-    total[: 2 * width] = dot3((left_high[...], left_low[...]), two, ROWS_BY_COLUMNS)
-    total[2 * width :] = dot3((left_high[width:], left_low[width:]), one, ROWS_BY_COLUMNS)
+    first = dot3(left, two, ROWS_BY_COLUMNS)
+    second = dot3((left[0][width:], left[1][width:]), one, ROWS_BY_COLUMNS)
+    if m == 0:
+        out[0][: 2 * width] = first
+        out[0][2 * width :] = second
+        return
+    keep, send, total = out
+    total[: 2 * width] = before[: 2 * width] + first
+    total[2 * width :] = before[2 * width :] + second
     quarter = width // n
     for e in range(n):
         for s in range(3):
@@ -219,55 +232,48 @@
             (send if e & 1 else keep)[where] = total[pl.ds(start, quarter)]
 
 
-def small_sums(n, at, left, gathered):
-    span = left[0].shape[1]
-    width = gathered[0].shape[-1]
+def small_sums(n, at, left, arrived):
+    width = arrived[0].shape[-1]
+    part = jax.ShapeDtypeStruct((2 * width, 2 * width), BF16)
+    whole = jax.ShapeDtypeStruct((3 * width, width), F32)
     half = jax.ShapeDtypeStruct((3 * width // 2, width), F32)
-    return pl.pallas_call(
-        functools.partial(sums_kernel, n),
-        out_shape=(half, half),
-        in_specs=[SMEM] + [VMEM] * (2 + n),
-        out_specs=(VMEM, VMEM),
-        scratch_shapes=[
-            pltpu.VMEM((span, 2 * width), BF16),
-            pltpu.VMEM((span, 2 * width), BF16),
-            pltpu.VMEM((3 * width, width), F32),
-        ],
-        compiler_params=limits(16),
-        cost_estimate=cost(18 * span * width * width, 4 * span * width),
-        name="small_sums",
-    )(at, *left, *gathered)
-
-
-def band_kernel(n, at, known, *refs):
-    gathered, (keep, send, tiles, high, low, sems) = refs[:n], refs[n:]
-    copies = tile_copies(n, at[1], known, tiles, sems)
-    gathered_halves(n, at, gathered, high, low)
-    right = (high[...], low[...])
-    for a in range(n):
-        copies[a].wait()
-        (send if a & 1 else keep)[a >> 1] = dot3(halves(tiles[a]), right, ROWS_BY_COLUMNS)
-
-
-def band_product(n, at, known, gathered):
+    estimate = cost(18 * 2 * width * width * width, 0)
+    total, *first = call(
+        functools.partial(sums_kernel, n, 0), "first_sums", 8, estimate,
+        (whole, part, part), at, *left, arrived[0],
+    )
+    keep, send, _, *second = call(
+        functools.partial(sums_kernel, n, 1), "last_sums", 8, estimate,
+        (half, half, whole, part, part), at, *left, arrived[1], total,
+    )
+    return keep, send, (*first, *second)
+
+
+def band_kernel(n, first, at, known, *refs):
+    right, out = refs[:4], refs[4]
+    row, col = at[0], at[1]
+    width = right[0].shape[0] // 2
+    for i in range(n // 2):
+        tile = tile_rows(first + 2 * i, col, width)
+        terms = [
+            dot3(
+                halves(known[tile, arrived_columns(row, m, width)]),
+                (right[2 * m][...], right[2 * m + 1][...]),
+                ROWS_BY_COLUMNS,
+            )
+            for m in range(2)
+        ]
+        out[i] = terms[0] + terms[1]
+
+
+def band_product(n, first, at, known, right):
     rows, span = known.shape
     width = rows // n
-    half = jax.ShapeDtypeStruct((n // 2, width, 2 * width), F32)
-    return pl.pallas_call(
-        functools.partial(band_kernel, n),
-        out_shape=(half, half),
-        in_specs=[SMEM, HBM] + [VMEM] * n,
-        out_specs=(VMEM, VMEM),
-        scratch_shapes=[
-            pltpu.VMEM((n, width, span), F32),
-            pltpu.VMEM((span, 2 * width), BF16),
-            pltpu.VMEM((span, 2 * width), BF16),
-            pltpu.SemaphoreType.DMA((n,)),
-        ],
-        compiler_params=limits(24),
-        cost_estimate=cost(12 * rows * span * width, 4 * rows * span),
-        name="band_product",
-    )(at, known, *gathered)
+    return call(
+        functools.partial(band_kernel, n, first), "band_product", 14,
+        cost(6 * rows * span * width, 2 * rows * span),
+        jax.ShapeDtypeStruct((n // 2, width, 2 * width), F32), at, known, *right,
+    )
 
 
 def column_kernel(n, at, keep, got, other, top, two, one):
@@ -334,6 +340,7 @@
     known, lower_two, lower_one, top_one, inner_two, inner_one, heights, pattern_two, pattern_one
 ):
     n = lax.axis_size("pcol")
+    width = top_one.shape[0]
     place = jnp.stack([lax.axis_index("prow"), lax.axis_index("pcol")]).astype(jnp.int32)
     at = jnp.concatenate([place, heights, pattern_two, pattern_one])
 
@@ -347,18 +354,19 @@
         pairs = [(z * n + j, (j ^ k) * n + z) for z in range(n) for j in range(n)]
         return lax.ppermute(rows, ("prow", "pcol"), pairs)
 
-    pair = pair_up(lower_two, lower_one)
-    gathered = [direct(k, pair) for k in range(n)]
-    four = pair_up(pair, core(pair))
-    plane = [four, across(four)]
-    left = left_product(n, at, known, plane)
-
-    keep_sums, send_sums = small_sums(n, at, left, gathered)
+    four = stack(stack(lower_two, lower_one), core(lower_two), core(lower_one))
+    gathered = [direct(k, four) for k in range(0, n, 2)]
+    other = [across(lower_two), across(lower_one)]
+    there = stack(*other, *[core(rows) for rows in other])
+    left = left_product(n, at, known, four, there)
+
+    keep_sums, send_sums, right = small_sums(n, at, left, gathered)
     mine = keep_sums + core(send_sums)
     half = mine.shape[0] // 2
-    keep, send = band_product(n, after(at, mine), known, gathered)
+    send = band_product(n, 1, after(at, mine), known, right)
     mine = mine[:half] + across(mine[half:])
     got = core(after(send, mine))
+    keep = band_product(n, 0, after(at, mine, send), known, right)
     mine = mine + along("prow", 1, mine)
     other = across(after(keep[1] + got[1], mine))
     mine = mine + along("prow", 2, mine)

time: 104 us -> 100 us (0.962)
  starting transfers between devices: 25.3 us -> 15.8 us
  waiting for transfers between devices: 54.5 us -> 60 us
    ppermute x10 -> x14, starting transfers between devices: 16.7 us -> 8.56 us  [along(): return lax.ppermute(array, axis, [(i, i ^ k) for i in range(n)])]
    ppermute x10 -> x14, waiting for transfers between devices: 54.5 us -> 60 us  [along(): return lax.ppermute(array, axis, [(i, i ^ k) for i in range(n)])]
    ppermute x4 -> x2, starting transfers between devices: 8.6 us -> 7.24 us  [direct(): return lax.ppermute(rows, ('prow', 'pcol'), pairs)]
    pallas_call x5 -> x9, Pallas kernels: 15 us -> 14.8 us  [the longest x6 13.5 us: call(): pl.pallas_call(kernel, out_shape=out_shape, in_specs=[SMEM] + [VMEM] * (l...]
    unnamed x13 -> x15, local copies, waits for them, and re-layouts: 4.11 us -> 4.13 us
  transfers between devices with their start and end apart: 14 -> 16, of which waited for: 7 -> 8; matrix products, arithmetic and copies ran while one was open for 1% -> 1% of each run, Pallas kernels for 12% -> 14%
where the time goes in v3:
time: 100 us
  waiting for transfers between devices  60 us (60%)
  Pallas kernels  18.2 us (18%)
  starting transfers between devices  15.8 us (16%)
  local copies, waits for them, and re-layouts  4.92 us (5%)
    ppermute x14, waiting for transfers between devices, along(): return lax.ppermute(array, axis, [(i, i ^ k) for i in range(n)])  60 us
    pallas_call x6, Pallas kernels, call(): pl.pallas_call(kernel, out_shape=out_shape, in_specs=[SMEM] + [VMEM] * (l...  13.5 us
    ppermute x14, starting transfers between devices, along(): return lax.ppermute(array, axis, [(i, i ^ k) for i in range(n)])  8.56 us
    ppermute x2, starting transfers between devices, direct(): return lax.ppermute(rows, ('prow', 'pcol'), pairs)  7.24 us
    unnamed x15, local copies, waits for them, and re-layouts  4.13 us
  transfers between devices with their start and end apart: 16, of which 8 were waited for; matrix products, arithmetic and copies ran while one was open for 1% of the time, Pallas kernels for 14%

profile of v3, /device:TPU:0, one launch (start us, length us, event | category | flops | bytes accessed | tf_op | source)
XLA Modules:
  0.0 100.0 jit_solution(15886731606522333864)
XLA Ops:
  0.6 0.5 collective-permute-start.4
  1.2 0.9 copy-done.3
  2.2 0.9 copy-done.4
  3.2 0.1 stack_rows.5.plane
  3.3 0.7 collective-permute-start.7
  4.1 6.5 %collective-permute-start.6 = (f32[1024,256]{1,0:T(8,128)S(1)}, f32[1024,256]{1,0:T(8,128)S(1)}, u32[]{:S(2)}, u32[]{:S(2)}) collective-permute-start(f32[1024,256]{1,0:T(8,128)S(1)} %stack_rows.5.plane), channel_id=1, source_target_pairs={{0,8},{1,12},{2,0},{3,4},{4,9},{5,13},{6,1},{7,5},{8,10},{9,14},{1... | collective-permute-start | bytes 3145736 | tf_op jit(solution)/shard_map/ppermute | solution.py:355
  10.6 0.3 collective-permute-start
  10.9 1.7 %collective-permute-start.1 = (f32[256,256]{1,0:T(8,128)S(1)}, f32[256,256]{1,0:T(8,128)}, u32[]{:S(2)}, u32[]{:S(2)}) collective-permute-start(f32[256,256]{1,0:T(8,128)S(1)} %copy-done.4), channel_id=1, source_target_pairs={{0,2},{1,3},{2,0},{3,1},{4,6},{5,7},{6,4},{7,5},{8,10},{9,11},{10,... | collective-permute-start | bytes 786440 | tf_op jit(solution)/shard_map/ppermute | solution.py:348
  12.6 30.6 %collective-permute-done.refs_0_ = f32[256,256]{1,0:T(8,128)S(1)} collective-permute-done((f32[256,256]{1,0:T(8,128)S(1)}, f32[256,256]{1,0:T(8,128)S(1)}, u32[]{:S(2)}, u32[]{:S(2)}) %collective-permute-start) | collective-permute-done | bytes 262176 | tf_op jit(solution)/shard_map/ppermute | solution.py:348
  43.2 2.9 %collective-permute-done.1.refs_1_ = f32[256,256]{1,0:T(8,128)} collective-permute-done((f32[256,256]{1,0:T(8,128)S(1)}, f32[256,256]{1,0:T(8,128)}, u32[]{:S(2)}, u32[]{:S(2)}) %collective-permute-start.1) | collective-permute-done | bytes 262176 | tf_op jit(solution)/shard_map/ppermute | solution.py:348
  46.1 0.8 concatenate.6.at
  46.9 2.2 %copy-done = f32[1024,1024]{1,0:T(8,128)S(1)} copy-done((f32[1024,1024]{1,0:T(8,128)S(1)}, f32[1024,1024]{1,0:T(8,128)}, u32[]{:S(2)}) %copy-start) | copy-done | bytes 4194328
  49.1 2.4 %left_first.1.before = f32[512,1024]{1,0:T(8,128)S(1)} custom-call(s32[50]{0:T(128)S(1)} %concatenate.6.at, f32[1024,1024]{1,0:T(8,128)S(1)} %copy-done, f32[1024,256]{1,0:T(8,128)S(1)} %stack_rows.5.plane), custom_call_target="tpu_custom_call" | custom-call | tf_op jit(solution)/shard_map/left_first/pallas_call | solution.py:174
  51.6 1.2 %stack_rows.3.plane = f32[1024,256]{1,0:T(8,128)S(1)} custom-call(f32[256,256]{1,0:T(8,128)S(1)} %collective-permute-done.refs_0_, f32[256,256]{1,0:T(8,128)} %collective-permute-done.1.refs_1_, f32[256,256]{1,0:T(8,128)} %collective-permute-done.2.refs_2_, f32[256,256]{1,0:T(8,128)} %collective-permute-done.3.refs_3_), custom_call_target="tpu_custom_call" | custom-call | bytes 2097152 | tf_op jit(solution)/shard_map/stack_rows/pallas_call | solution.py:141
  52.7 2.5 %left_last.1 = (bf16[512,1024]{1,0:T(8,128)(2,1)S(1)}, bf16[512,1024]{1,0:T(8,128)(2,1)S(1)}) custom-call(s32[50]{0:T(128)S(1)} %concatenate.6.at, f32[1024,1024]{1,0:T(8,128)S(1)} %copy-done, f32[1024,256]{1,0:T(8,128)S(1)} %stack_rows.3.plane, f32[512,1024]{1,0:T(8,128)S(1)} %left_first.1.before), custom_call_target="tpu_custom_call" | custom-call | tf_op jit(solution)/shard_map/left_last/pallas_call | solution.py:174
  55.3 1.5 %first_sums.1 = (f32[768,256]{1,0:T(8,128)S(1)}, bf16[512,512]{1,0:T(8,128)(2,1)S(1)}, bf16[512,512]{1,0:T(8,128)(2,1)S(1)}) custom-call(s32[50]{0:T(128)S(1)} %concatenate.6.at, bf16[512,1024]{1,0:T(8,128)(2,1)S(1)} %get-tuple-element.24.left_high, bf16[512,1024]{1,0:T(8,128)(2,1)S(1)} %get-tuple-element.25.left_low, ...), custom_call_target="tpu_custom_call" | custom-call | flops 603979776 | tf_op jit(solution)/shard_map/first_sums/pallas_call | solution.py:174
  56.8 2.4 %last_sums.1 = (f32[384,256]{1,0:T(8,128)S(1)}, f32[384,256]{1,0:T(8,128)S(1)}, f32[768,256]{1,0:T(8,128)}, bf16[512,512]{1,0:T(8,128)(2,1)S(1)}, bf16[512,512]{1,0:T(8,128)(2,1)S(1)}) custom-call(s32[50]{0:T(128)S(1)} %concatenate.6.at, bf16[512,1024]{1,0:T(8,128)(2,1)S(1)} %get-tuple-element.24.left_high, ...), custom_call_target="tpu_custom_call" | custom-call | flops 603979776 | tf_op jit(solution)/shard_map/last_sums/pallas_call | solution.py:174
  59.1 0.5 collective-permute-start.8
  59.6 1.3 %collective-permute-done.8 = f32[384,256]{1,0:T(8,128)S(1)} collective-permute-done((f32[384,256]{1,0:T(8,128)S(1)}, f32[384,256]{1,0:T(8,128)S(1)}, u32[]{:S(2)}, u32[]{:S(2)}) %collective-permute-start.8) | collective-permute-done | bytes 393248 | tf_op jit(solution)/shard_map/ppermute | solution.py:348
  61.1 2.6 %collective-permute-start.9 = (f32[192,256]{1,0:T(8,128)S(1)}, f32[192,256]{1,0:T(8,128)S(1)}, u32[]{:S(2)}, u32[]{:S(2)}) collective-permute-start(f32[192,256]{1,0:T(8,128)S(1)} %slice.17), channel_id=1, source_target_pairs={{0,2},{1,3},{2,0},{3,1},{4,6},{5,7},{6,4},{7,5},{8,10},{9,11},{10,... | collective-permute-start | bytes 589832 | tf_op jit(solution)/shard_map/ppermute | solution.py:348
  63.7 2.3 %band_product.2 = f32[2,256,512]{2,1,0:T(8,128)S(1)} custom-call(s32[50]{0:T(128)S(1)} %concatenate.6.at, f32[1024,1024]{1,0:T(8,128)S(1)} %copy-done.1, bf16[512,512]{1,0:T(8,128)(2,1)S(1)} %get-tuple-element.30.refs_0_, bf16[512,512]{1,0:T(8,128)(2,1)S(1)} %get-tuple-element.31.refs_1_, bf16[512,512]{1,0:T(8,128)(2,1)S(1)} %get-tuple-element.32.refs_2_, ...), custom_call_target="tpu_custom_call" | custom-call | flops 1610612736 | bytes 2097152 | tf_op jit(solution)/shard_map/band_product/pallas_call | solution.py:174
  66.1 2.9 %collective-permute-done.9 = f32[192,256]{1,0:T(8,128)S(1)} collective-permute-done((f32[192,256]{1,0:T(8,128)S(1)}, f32[192,256]{1,0:T(8,128)S(1)}, u32[]{:S(2)}, u32[]{:S(2)}) %collective-permute-start.9) | collective-permute-done | bytes 196640 | tf_op jit(solution)/shard_map/ppermute | solution.py:348
  69.0 0.2 collective-permute-start.11
  69.3 2.3 %band_product.3.keep = f32[2,256,512]{2,1,0:T(8,128)S(1)} custom-call(s32[50]{0:T(128)S(1)} %concatenate.6.at, f32[1024,1024]{1,0:T(8,128)S(1)} %copy-done.1, bf16[512,512]{1,0:T(8,128)(2,1)S(1)} %get-tuple-element.30.refs_0_, bf16[512,512]{1,0:T(8,128)(2,1)S(1)} %get-tuple-element.31.refs_1_, bf16[512,512]{1,0:T(8,128)(2,1)S(1)} %get-tuple-element.32.refs_2_, ...), custom_call_target="tpu_custom_call" | custom-call | flops 1610612736 | bytes 2097152 | tf_op jit(solution)/shard_map/band_product/pallas_call | solution.py:174
  71.6 4.7 %collective-permute-done.11 = f32[192,256]{1,0:T(8,128)S(1)} collective-permute-done((f32[192,256]{1,0:T(8,128)S(1)}, f32[192,256]{1,0:T(8,128)S(1)}, u32[]{:S(2)}, u32[]{:S(2)}) %collective-permute-start.11) | collective-permute-done | bytes 196640 | tf_op jit(solution)/shard_map/ppermute | solution.py:348
  76.5 1.8 %collective-permute-start.12 = (f32[256,512]{1,0:T(8,128)S(1)}, f32[256,512]{1,0:T(8,128)S(1)}, u32[]{:S(2)}, u32[]{:S(2)}) collective-permute-start(f32[256,512]{1,0:T(8,128)S(1)} %fusion), channel_id=1, source_target_pairs={{0,2},{1,3},{2,0},{3,1},{4,6},{5,7},{6,4},{7,5},{8,10},{9,11},{10,... | collective-permute-start | bytes 1572872 | tf_op jit(solution)/shard_map/ppermute | solution.py:348
  78.3 11.1 %collective-permute-done.13 = f32[192,256]{1,0:T(8,128)S(1)} collective-permute-done((f32[192,256]{1,0:T(8,128)S(1)}, f32[192,256]{1,0:T(8,128)S(1)}, u32[]{:S(2)}, u32[]{:S(2)}) %collective-permute-start.13) | collective-permute-done | bytes 196640 | tf_op jit(solution)/shard_map/ppermute | solution.py:348
  89.4 0.6 collective-permute-start.14
  90.0 1.5 %column_rows.1 = (f32[256,256]{1,0:T(8,128)}, f32[256,256]{1,0:T(8,128)}) custom-call(s32[50]{0:T(128)S(1)} %concatenate.6.at, f32[2,256,512]{2,1,0:T(8,128)S(1)} %band_product.3.keep, f32[2,256,512]{2,1,0:T(8,128)S(1)} %collective-permute-done.10.got, f32[256,512]{1,0:T(8,128)S(1)} %collective-permute-done.12.other, f32[256,256]{1,0:T(8,128)S(1)} %copy-done.2), custom_call_target="tpu_custom_call" | custom-call | tf_op jit(solution)/shard_map/column_rows/pallas_call | solution.py:291
  91.6 4.7 %collective-permute-done.14 = f32[192,256]{1,0:T(8,128)S(1)} collective-permute-done((f32[192,256]{1,0:T(8,128)S(1)}, f32[192,256]{1,0:T(8,128)S(1)}, u32[]{:S(2)}, u32[]{:S(2)}) %collective-permute-start.14) | collective-permute-done | bytes 196640 | tf_op jit(solution)/shard_map/ppermute | solution.py:348
  96.4 1.7 %collective-permute-done.15.second = f32[384,256]{1,0:T(8,128)S(1)} collective-permute-done((f32[384,256]{1,0:T(8,128)S(1)}, f32[384,256]{1,0:T(8,128)S(1)}, u32[]{:S(2)}, u32[]{:S(2)}) %collective-permute-start.15) | collective-permute-done | bytes 393248 | tf_op jit(solution)/shard_map/ppermute | solution.py:348
  98.1 1.9 %small_blocks.1 = (f32[256,256]{1,0:T(8,128)}, f32[256,256]{1,0:T(8,128)}, f32[256,256]{1,0:T(8,128)}) custom-call(s32[50]{0:T(128)S(1)} %concatenate.6.at, f32[256,256]{1,0:T(8,128)S(1)} %copy-done.2, f32[256,256]{1,0:T(8,128)S(1)} %copy-done.5, f32[256,256]{1,0:T(8,128)S(1)} %copy-done.6, f32[384,256]{1,0:T(8,128)S(1)} %constant_dynamic-update-slice_fusion.first, ...), custom_call_target="tpu_custom_call" | custom-call | tf_op jit(solution)/shard_map/small_blocks/pallas_call | solution.py:324
  (34 shorter events, 0.6 us)
Async XLA Ops:
  0.6 2.6 %collective-permute-start.4 = (f32[256,256]{1,0:T(8,128)}, f32[256,256]{1,0:T(8,128)S(1)}, u32[]{:S(2)}, u32[]{:S(2)}) collective-permute-start(f32[256,256]{1,0:T(8,128)} %refs_0_.1), channel_id=1, source_target_pairs={{0,1},{1,0},{2,3},{3,2},{4,5},{5,4},{6,7},{7,6},{8,9},{9,8},{10,11... | collective-permute-start | bytes 786440 | tf_op jit(solution)/shard_map/ppermute | solution.py:348
  1.1 2.1 %collective-permute-start.5 = (f32[256,256]{1,0:T(8,128)}, f32[256,256]{1,0:T(8,128)S(1)}, u32[]{:S(2)}, u32[]{:S(2)}) collective-permute-start(f32[256,256]{1,0:T(8,128)} %refs_1_.1), channel_id=1, source_target_pairs={{0,1},{1,0},{2,3},{3,2},{4,5},{5,4},{6,7},{7,6},{8,9},{9,8},{10,11... | collective-permute-start | bytes 786440 | tf_op jit(solution)/shard_map/ppermute | solution.py:348
  1.2 0.9 copy-start.3
  2.2 0.9 copy-start.4
  3.3 51.9 %collective-permute-start.7 = (f32[1024,256]{1,0:T(8,128)S(1)}, f32[1024,256]{1,0:T(8,128)S(1)}, u32[]{:S(2)}, u32[]{:S(2)}) collective-permute-start(f32[1024,256]{1,0:T(8,128)S(1)} %stack_rows.5.plane), channel_id=1, source_target_pairs={{0,0},{1,4},{2,8},{3,12},{4,1},{5,5},{6,9},{7,13},{8,2},{9,6},{10,... | collective-permute-start | bytes 3145736 | tf_op jit(solution)/shard_map/ppermute | solution.py:355
  4.1 52.7 %collective-permute-start.6 = (f32[1024,256]{1,0:T(8,128)S(1)}, f32[1024,256]{1,0:T(8,128)S(1)}, u32[]{:S(2)}, u32[]{:S(2)}) collective-permute-start(f32[1024,256]{1,0:T(8,128)S(1)} %stack_rows.5.plane), channel_id=1, source_target_pairs={{0,8},{1,12},{2,0},{3,4},{4,9},{5,13},{6,1},{7,5},{8,10},{9,14},{1... | collective-permute-start | bytes 3145736 | tf_op jit(solution)/shard_map/ppermute | solution.py:355
  10.6 32.6 %collective-permute-start = (f32[256,256]{1,0:T(8,128)S(1)}, f32[256,256]{1,0:T(8,128)S(1)}, u32[]{:S(2)}, u32[]{:S(2)}) collective-permute-start(f32[256,256]{1,0:T(8,128)S(1)} %copy-done.3), channel_id=1, source_target_pairs={{0,2},{1,3},{2,0},{3,1},{4,6},{5,7},{6,4},{7,5},{8,10},{9,11},{10,... | collective-permute-start | bytes 786440 | tf_op jit(solution)/shard_map/ppermute | solution.py:348
  10.9 35.3 %collective-permute-start.1 = (f32[256,256]{1,0:T(8,128)S(1)}, f32[256,256]{1,0:T(8,128)}, u32[]{:S(2)}, u32[]{:S(2)}) collective-permute-start(f32[256,256]{1,0:T(8,128)S(1)} %copy-done.4), channel_id=1, source_target_pairs={{0,2},{1,3},{2,0},{3,1},{4,6},{5,7},{6,4},{7,5},{8,10},{9,11},{10,... | collective-permute-start | bytes 786440 | tf_op jit(solution)/shard_map/ppermute | solution.py:348
  43.2 8.3 %collective-permute-start.2 = (f32[256,256]{1,0:T(8,128)S(1)}, f32[256,256]{1,0:T(8,128)}, u32[]{:S(2)}, u32[]{:S(2)}) collective-permute-start(f32[256,256]{1,0:T(8,128)S(1)} %collective-permute-done.refs_0_), channel_id=1, source_target_pairs={{0,1},{1,0},{2,3},{3,2},{4,5},{5,4},{6,7},{7,6},{8,9},{9,8},{10,11... | collective-permute-start | bytes 786440 | tf_op jit(solution)/shard_map/ppermute | solution.py:348
  46.1 5.4 %collective-permute-start.3 = (f32[256,256]{1,0:T(8,128)}, f32[256,256]{1,0:T(8,128)}, u32[]{:S(2)}, u32[]{:S(2)}) collective-permute-start(f32[256,256]{1,0:T(8,128)} %collective-permute-done.1.refs_1_), channel_id=1, source_target_pairs={{0,1},{1,0},{2,3},{3,2},{4,5},{5,4},{6,7},{7,6},{8,9},{9,8},{10,11... | collective-permute-start | bytes 786440 | tf_op jit(solution)/shard_map/ppermute | solution.py:348
  46.9 2.2 %copy-start = (f32[1024,1024]{1,0:T(8,128)S(1)}, f32[1024,1024]{1,0:T(8,128)}, u32[]{:S(2)}) copy-start(f32[1024,1024]{1,0:T(8,128)} %known.7) | copy-start | bytes 12582916
  55.3 8.5 %copy-start.1 = (f32[1024,1024]{1,0:T(8,128)S(1)}, f32[1024,1024]{1,0:T(8,128)}, u32[]{:S(2)}) copy-start(f32[1024,1024]{1,0:T(8,128)} %known.7) | copy-start | bytes 12582916
  59.1 1.9 %collective-permute-start.8 = (f32[384,256]{1,0:T(8,128)S(1)}, f32[384,256]{1,0:T(8,128)S(1)}, u32[]{:S(2)}, u32[]{:S(2)}) collective-permute-start(f32[384,256]{1,0:T(8,128)S(1)} %get-tuple-element.28), channel_id=1, source_target_pairs={{0,1},{1,0},{2,3},{3,2},{4,5},{5,4},{6,7},{7,6},{8,9},{9,8},{10,11... | collective-permute-start | bytes 1179656 | tf_op jit(solution)/shard_map/ppermute | solution.py:348
  61.1 7.8 %collective-permute-start.9 = (f32[192,256]{1,0:T(8,128)S(1)}, f32[192,256]{1,0:T(8,128)S(1)}, u32[]{:S(2)}, u32[]{:S(2)}) collective-permute-start(f32[192,256]{1,0:T(8,128)S(1)} %slice.17), channel_id=1, source_target_pairs={{0,2},{1,3},{2,0},{3,1},{4,6},{5,7},{6,4},{7,5},{8,10},{9,11},{10,... | collective-permute-start | bytes 589832 | tf_op jit(solution)/shard_map/ppermute | solution.py:348
  68.9 21.1 %copy-start.2 = (f32[256,256]{1,0:T(8,128)S(1)}, f32[256,256]{1,0:T(8,128)}, u32[]{:S(2)}) copy-start(f32[256,256]{1,0:T(8,128)} %top.3) | copy-start | bytes 786436
  69.0 7.4 %collective-permute-start.10 = (f32[2,256,512]{2,1,0:T(8,128)S(1)}, f32[2,256,512]{2,1,0:T(8,128)S(1)}, u32[]{:S(2)}, u32[]{:S(2)}) collective-permute-start(f32[2,256,512]{2,1,0:T(8,128)S(1)} %band_product.2), channel_id=1, source_target_pairs={{0,1},{1,0},{2,3},{3,2},{4,5},{5,4},{6,7},{7,6},{8,9},{9,8},{10,11... | collective-permute-start | bytes 3145736 | tf_op jit(solution)/shard_map/ppermute | solution.py:348
  69.0 7.3 %collective-permute-start.11 = (f32[192,256]{1,0:T(8,128)S(1)}, f32[192,256]{1,0:T(8,128)S(1)}, u32[]{:S(2)}, u32[]{:S(2)}) collective-permute-start(f32[192,256]{1,0:T(8,128)S(1)} %slice_add_fusion.1), channel_id=1, source_target_pairs={{0,4},{4,0},{8,12},{12,8},{1,5},{5,1},{9,13},{13,9},{2,6},{6,2},{1... | collective-permute-start | bytes 589832 | tf_op jit(solution)/shard_map/ppermute | solution.py:348
  71.6 26.5 %copy-start.5 = (f32[256,256]{1,0:T(8,128)S(1)}, f32[256,256]{1,0:T(8,128)}, u32[]{:S(2)}) copy-start(f32[256,256]{1,0:T(8,128)} %inner_two.1) | copy-start | bytes 786436
  71.6 26.5 %copy-start.6 = (f32[256,256]{1,0:T(8,128)S(1)}, f32[256,256]{1,0:T(8,128)}, u32[]{:S(2)}) copy-start(f32[256,256]{1,0:T(8,128)} %inner_one.1) | copy-start | bytes 786436
  76.5 13.6 %collective-permute-start.12 = (f32[256,512]{1,0:T(8,128)S(1)}, f32[256,512]{1,0:T(8,128)S(1)}, u32[]{:S(2)}, u32[]{:S(2)}) collective-permute-start(f32[256,512]{1,0:T(8,128)S(1)} %fusion), channel_id=1, source_target_pairs={{0,2},{1,3},{2,0},{3,1},{4,6},{5,7},{6,4},{7,5},{8,10},{9,11},{10,... | collective-permute-start | bytes 1572872 | tf_op jit(solution)/shard_map/ppermute | solution.py:348
  78.3 11.1 %collective-permute-start.13 = (f32[192,256]{1,0:T(8,128)S(1)}, f32[192,256]{1,0:T(8,128)S(1)}, u32[]{:S(2)}, u32[]{:S(2)}) collective-permute-start(f32[192,256]{1,0:T(8,128)S(1)} %add.22), channel_id=1, source_target_pairs={{0,8},{4,12},{8,0},{12,4},{1,9},{5,13},{9,1},{13,5},{2,10},{6,14},... | collective-permute-start | bytes 589832 | tf_op jit(solution)/shard_map/ppermute | solution.py:348
  89.4 6.9 %collective-permute-start.14 = (f32[192,256]{1,0:T(8,128)S(1)}, f32[192,256]{1,0:T(8,128)S(1)}, u32[]{:S(2)}, u32[]{:S(2)}) collective-permute-start(f32[192,256]{1,0:T(8,128)S(1)} %add.23), channel_id=1, source_target_pairs={{0,2},{1,3},{2,0},{3,1},{4,6},{5,7},{6,4},{7,5},{8,10},{9,11},{10,... | collective-permute-start | bytes 589832 | tf_op jit(solution)/shard_map/ppermute | solution.py:348
  96.3 1.8 %collective-permute-start.15 = (f32[384,256]{1,0:T(8,128)S(1)}, f32[384,256]{1,0:T(8,128)S(1)}, u32[]{:S(2)}, u32[]{:S(2)}) collective-permute-start(f32[384,256]{1,0:T(8,128)S(1)} %constant_dynamic-update-slice_fusion.first), channel_id=1, source_target_pairs={{0,1},{1,0},{2,3},{3,2},{4,5},{5,4},{6,7},{7,6},{8,9},{9,8},{10,11... | collective-permute-start | bytes 1179656 | tf_op jit(solution)/shard_map/ppermute | solution.py:348

commit v4 on v3

--- a/solution.py
+++ b/solution.py
@@ -150,23 +150,23 @@
     )(*blocks)
 
 
-def left_terms(n, first, at, known, plane):
+def left_term(n, a, at, known, two, one):
     row, col = at[0], at[1]
-    width = known.shape[0] // n
-    terms = []
-    for i in range(2):
-        rows = plane[2 * i * width : 2 * (i + 1) * width]
-        rows = halves(masked(rows, at, n, row * n + ((first + i) ^ col)))
-        terms.append(dot3(rows, halves(known[tile_rows(first + i, col, width)]), ROWS_BY_ROWS))
-    return terms[0] + terms[1]
-
-
-def left_first_kernel(n, at, known, plane, out):
-    out[...] = left_terms(n, 0, at, known, plane)
-
-
-def left_last_kernel(n, at, known, plane, before, high, low):
-    total = before[...] + left_terms(n, 2, at, known, plane)
+    rows = jnp.concatenate([two, one], axis=0)
+    rows = halves(masked(rows, at, n, row * n + (a ^ col)))
+    tile = known[tile_rows(a, col, two.shape[0])]
+    return dot3(rows, halves(tile), ROWS_BY_ROWS)
+
+
+def left_first_kernel(n, at, known, here, out):
+    blocks = here[...].reshape(4, -1, here.shape[1])
+    out[...] = left_term(n, 0, at, known, blocks[0], blocks[1])
+    out[...] += left_term(n, 1, at, known, blocks[2], blocks[3])
+
+
+def left_last_kernel(n, at, known, two, one, core_two, core_one, before, high, low):
+    total = before[...] + left_term(n, 2, at, known, two[...], one[...])
+    total = total + left_term(n, 3, at, known, core_two[...], core_one[...])
     high[...], low[...] = halves(total)
 
 
@@ -183,18 +183,20 @@
     )(*arrays)
 
 
-def left_product(n, at, known, here, there):
+def left_first(n, at, known, here):
     rows, span = known.shape
-    shape = (2 * rows // n, span)
-    half = jax.ShapeDtypeStruct(shape, BF16)
-    first = call(
-        functools.partial(left_first_kernel, n), "left_first", 14, cost(0, 0),
-        jax.ShapeDtypeStruct(shape, F32), at, known, here,
-    )
-    return call(
-        functools.partial(left_last_kernel, n), "left_last", 14, cost(0, 0),
-        (half, half), at, known, there, first,
-    )
+    shape = jax.ShapeDtypeStruct((2 * rows // n, span), F32)
+    kernel = functools.partial(left_first_kernel, n)
+    return call(kernel, "left_first", 14, cost(0, 0), shape, at, known, here)
+
+
+def left_last(n, at, known, there, first):
+    half = jax.ShapeDtypeStruct(first.shape, BF16)
+    kernel = functools.partial(left_last_kernel, n)
+    return call(kernel, "left_last", 14, cost(0, 0), (half, half), at, known, *there, first)
+
+
+FIRST_ARRIVAL = 1
 
 
 def arrived_columns(row, m, width):
@@ -202,10 +204,9 @@
 
 
 def sums_kernel(n, m, at, left_high, left_low, arrived, *refs):
-    before, refs = (None, refs) if m == 0 else (refs[0], refs[1:])
-    out, high, low = refs[:-2], refs[-2], refs[-1]
     row, col = at[0], at[1]
     width = arrived.shape[-1]
+    high, low = refs[-2:] if len(refs) == 3 else refs[3:5]
     for e in range(2):
         block = row ^ (2 * m + e)
         rows = arrived[2 * e * width : 2 * (e + 1) * width]
@@ -217,11 +218,12 @@
     one = (high[:, width:], low[:, width:])
     first = dot3(left, two, ROWS_BY_COLUMNS)
     second = dot3((left[0][width:], left[1][width:]), one, ROWS_BY_COLUMNS)
-    if m == 0:
-        out[0][: 2 * width] = first
-        out[0][2 * width :] = second
+    if len(refs) == 3:
+        out = refs[0]
+        out[: 2 * width] = first
+        out[2 * width :] = second
         return
-    keep, send, total = out
+    before, keep, send, total = refs[0], refs[1], refs[2], refs[5]
     total[: 2 * width] = before[: 2 * width] + first
     total[2 * width :] = before[2 * width :] + second
     quarter = width // n
@@ -239,14 +241,15 @@
     half = jax.ShapeDtypeStruct((3 * width // 2, width), F32)
     estimate = cost(18 * 2 * width * width * width, 0)
     total, *first = call(
-        functools.partial(sums_kernel, n, 0), "first_sums", 8, estimate,
-        (whole, part, part), at, *left, arrived[0],
-    )
-    keep, send, _, *second = call(
-        functools.partial(sums_kernel, n, 1), "last_sums", 8, estimate,
-        (half, half, whole, part, part), at, *left, arrived[1], total,
-    )
-    return keep, send, (*first, *second)
+        functools.partial(sums_kernel, n, FIRST_ARRIVAL), "first_sums", 8, estimate,
+        (whole, part, part), at, *left, arrived[FIRST_ARRIVAL],
+    )
+    keep, send, *last = call(
+        functools.partial(sums_kernel, n, 1 - FIRST_ARRIVAL), "last_sums", 8, estimate,
+        (half, half, part, part), at, *left, arrived[1 - FIRST_ARRIVAL], total,
+        scratch=[pltpu.VMEM((3 * width, width), F32)],
+    )
+    return keep, send, (*first, *last) if FIRST_ARRIVAL == 0 else (*last, *first)
 
 
 def band_kernel(n, first, at, known, *refs):
@@ -356,9 +359,10 @@
 
     four = stack(stack(lower_two, lower_one), core(lower_two), core(lower_one))
     gathered = [direct(k, four) for k in range(0, n, 2)]
-    other = [across(lower_two), across(lower_one)]
-    there = stack(*other, *[core(rows) for rows in other])
-    left = left_product(n, at, known, four, there)
+    first = left_first(n, at, known, four)
+    there = [across(lower_two), across(lower_one)]
+    there += [core(after(rows, first)) for rows in there]
+    left = left_last(n, at, known, there, first)
 
     keep_sums, send_sums, right = small_sums(n, at, left, gathered)
     mine = keep_sums + core(send_sums)

time: 100 us -> 97.8 us (0.978)
  starting transfers between devices: 15.8 us -> 25.8 us
  waiting for transfers between devices: 60 us -> 50.1 us
  local copies, waits for them, and re-layouts: 4.92 us -> 3.02 us
    ppermute x14, starting transfers between devices: 8.56 us -> 21.1 us  [along(): return lax.ppermute(array, axis, [(i, i ^ k) for i in range(n)])]
    ppermute x14, waiting for transfers between devices: 60 us -> 50.1 us  [along(): return lax.ppermute(array, axis, [(i, i ^ k) for i in range(n)])]
    ppermute x2, starting transfers between devices: 7.24 us -> 4.73 us  [direct(): return lax.ppermute(rows, ('prow', 'pcol'), pairs)]
    unnamed x15 -> x11, local copies, waits for them, and re-layouts: 4.13 us -> 2.22 us
  transfers between devices with their start and end apart: 16 -> 16, of which waited for: 8 -> 11; matrix products, arithmetic and copies ran while one was open for 1% -> 1% of each run, Pallas kernels for 14% -> 14%
where the time goes in v4:
time: 97.8 us; the launch traced here: 97.6 us
  waiting for transfers between devices  50.1 us (51%)
  starting transfers between devices  25.8 us (26%)
  Pallas kernels  17.7 us (18%)
  local copies, waits for them, and re-layouts  3.02 us (3%)
    ppermute x14, waiting for transfers between devices, along(): return lax.ppermute(array, axis, [(i, i ^ k) for i in range(n)])  50.1 us
    ppermute x14, starting transfers between devices, along(): return lax.ppermute(array, axis, [(i, i ^ k) for i in range(n)])  21.1 us
    pallas_call x6, Pallas kernels, call(): pl.pallas_call(kernel, out_shape=out_shape, in_specs=[SMEM] + [VMEM] * (l...  13.1 us
    ppermute x2, starting transfers between devices, direct(): return lax.ppermute(rows, ('prow', 'pcol'), pairs)  4.73 us
    unnamed x11, local copies, waits for them, and re-layouts  2.22 us
  transfers between devices with their start and end apart: 16, of which 11 were waited for; matrix products, arithmetic and copies ran while one was open for 1% of the time, Pallas kernels for 14%

profile of v4, /device:TPU:0, one launch (start us, length us, event | category | flops | bytes accessed | tf_op | source)
XLA Modules:
  0.0 97.6 jit_solution(241132682208462448)
XLA Ops:
  0.6 0.5 collective-permute-start.2
  1.2 1.0 %stack_rows.2.refs_0_ = f32[512,256]{1,0:T(8,128)S(1)} custom-call(f32[256,256]{1,0:T(8,128)} %refs_0_.1, f32[256,256]{1,0:T(8,128)} %refs_1_.1), custom_call_target="tpu_custom_call" | custom-call | bytes 1048576 | tf_op jit(solution)/shard_map/stack_rows/pallas_call | solution.py:141
  2.3 0.2 collective-permute-done.2.refs_1_
  2.5 0.4 collective-permute-done.3.refs_2_
  3.0 4.0 %collective-permute-start.7 = (f32[1024,256]{1,0:T(8,128)S(1)}, f32[1024,256]{1,0:T(8,128)S(1)}, u32[]{:S(2)}, u32[]{:S(2)}) collective-permute-start(f32[1024,256]{1,0:T(8,128)S(1)} %stack_rows.3.here), channel_id=1, source_target_pairs={{0,8},{1,12},{2,0},{3,4},{4,9},{5,13},{6,1},{7,5},{8,10},{9,14},{1... | collective-permute-start | bytes 3145736 | tf_op jit(solution)/shard_map/ppermute | solution.py:358
  7.0 0.7 collective-permute-start.6
  7.7 4.2 %collective-permute-start = (f32[256,256]{1,0:T(8,128)}, f32[256,256]{1,0:T(8,128)S(1)}, u32[]{:S(2)}, u32[]{:S(2)}) collective-permute-start(f32[256,256]{1,0:T(8,128)} %refs_0_.1), channel_id=1, source_target_pairs={{0,2},{1,3},{2,0},{3,1},{4,6},{5,7},{6,4},{7,5},{8,10},{9,11},{10,... | collective-permute-start | bytes 786440 | tf_op jit(solution)/shard_map/ppermute | solution.py:351
  12.0 0.8 concatenate.6.at
  12.8 2.2 %copy-done = f32[1024,1024]{1,0:T(8,128)S(1)} copy-done((f32[1024,1024]{1,0:T(8,128)S(1)}, f32[1024,1024]{1,0:T(8,128)}, u32[]{:S(2)}) %copy-start) | copy-done | bytes 4194328
  15.0 2.4 %left_first.1.before = f32[512,1024]{1,0:T(8,128)S(1)} custom-call(s32[50]{0:T(128)S(1)} %concatenate.6.at, f32[1024,1024]{1,0:T(8,128)S(1)} %copy-done, f32[1024,256]{1,0:T(8,128)S(1)} %stack_rows.3.here), custom_call_target="tpu_custom_call" | custom-call | tf_op jit(solution)/shard_map/left_first/pallas_call | solution.py:174
  17.4 20.9 %collective-permute-done.two = f32[256,256]{1,0:T(8,128)S(1)} collective-permute-done((f32[256,256]{1,0:T(8,128)}, f32[256,256]{1,0:T(8,128)S(1)}, u32[]{:S(2)}, u32[]{:S(2)}) %collective-permute-start) | collective-permute-done | bytes 262176 | tf_op jit(solution)/shard_map/ppermute | solution.py:351
  38.4 2.9 %collective-permute-done.1.one = f32[256,256]{1,0:T(8,128)} collective-permute-done((f32[256,256]{1,0:T(8,128)}, f32[256,256]{1,0:T(8,128)}, u32[]{:S(2)}, u32[]{:S(2)}) %collective-permute-start.1) | collective-permute-done | bytes 262176 | tf_op jit(solution)/shard_map/ppermute | solution.py:351
  41.3 1.7 %collective-permute-done.5.core_one = f32[256,256]{1,0:T(8,128)S(1)} collective-permute-done((f32[256,256]{1,0:T(8,128)}, f32[256,256]{1,0:T(8,128)S(1)}, u32[]{:S(2)}, u32[]{:S(2)}) %collective-permute-start.5) | collective-permute-done | bytes 262176 | tf_op jit(solution)/shard_map/ppermute | solution.py:351
  43.0 3.0 %left_last.1 = (bf16[512,1024]{1,0:T(8,128)(2,1)S(1)}, bf16[512,1024]{1,0:T(8,128)(2,1)S(1)}) custom-call(s32[50]{0:T(128)S(1)} %concatenate.6.at, f32[1024,1024]{1,0:T(8,128)S(1)} %copy-done.1, f32[256,256]{1,0:T(8,128)S(1)} %collective-permute-done.two, f32[256,256]{1,0:T(8,128)} %collective-permute-done.1.one, ...), custom_call_target="tpu_custom_call" | custom-call | tf_op jit(solution)/shard_map/left_last/pallas_call | solution.py:174
  46.0 1.5 %first_sums.1 = (f32[768,256]{1,0:T(8,128)S(1)}, bf16[512,512]{1,0:T(8,128)(2,1)S(1)}, bf16[512,512]{1,0:T(8,128)(2,1)S(1)}) custom-call(s32[50]{0:T(128)S(1)} %concatenate.6.at, bf16[512,1024]{1,0:T(8,128)(2,1)S(1)} %get-tuple-element.28.left_high, bf16[512,1024]{1,0:T(8,128)(2,1)S(1)} %get-tuple-element.29.left_low, ...), custom_call_target="tpu_custom_call" | custom-call | flops 603979776 | tf_op jit(solution)/shard_map/first_sums/pallas_call | solution.py:174
  47.5 1.5 %last_sums.1 = (f32[384,256]{1,0:T(8,128)S(1)}, f32[384,256]{1,0:T(8,128)S(1)}, bf16[512,512]{1,0:T(8,128)(2,1)S(1)}, bf16[512,512]{1,0:T(8,128)(2,1)S(1)}) custom-call(s32[50]{0:T(128)S(1)} %concatenate.6.at, bf16[512,1024]{1,0:T(8,128)(2,1)S(1)} %get-tuple-element.28.left_high, bf16[512,1024]{1,0:T(8,128)(2,1)S(1)} %get-tuple-element.29.left_low, ...), custom_call_target="tpu_custom_call" | custom-call | flops 603979776 | tf_op jit(solution)/shard_map/last_sums/pallas_call | solution.py:174
  49.0 0.2 collective-permute-start.8
  49.2 1.6 %collective-permute-done.8 = f32[384,256]{1,0:T(8,128)S(1)} collective-permute-done((f32[384,256]{1,0:T(8,128)S(1)}, f32[384,256]{1,0:T(8,128)S(1)}, u32[]{:S(2)}, u32[]{:S(2)}) %collective-permute-start.8) | collective-permute-done | bytes 393248 | tf_op jit(solution)/shard_map/ppermute | solution.py:351
  50.9 10.6 %collective-permute-start.9 = (f32[192,256]{1,0:T(8,128)S(1)}, f32[192,256]{1,0:T(8,128)S(1)}, u32[]{:S(2)}, u32[]{:S(2)}) collective-permute-start(f32[192,256]{1,0:T(8,128)S(1)} %slice.17), channel_id=1, source_target_pairs={{0,2},{1,3},{2,0},{3,1},{4,6},{5,7},{6,4},{7,5},{8,10},{9,11},{10,... | collective-permute-start | bytes 589832 | tf_op jit(solution)/shard_map/ppermute | solution.py:351
  61.5 2.3 %band_product.2 = f32[2,256,512]{2,1,0:T(8,128)S(1)} custom-call(s32[50]{0:T(128)S(1)} %concatenate.6.at, f32[1024,1024]{1,0:T(8,128)S(1)} %copy-done.1, bf16[512,512]{1,0:T(8,128)(2,1)S(1)} %get-tuple-element.34.refs_0_, bf16[512,512]{1,0:T(8,128)(2,1)S(1)} %get-tuple-element.35.refs_1_, bf16[512,512]{1,0:T(8,128)(2,1)S(1)} %get-tuple-element.36.refs_2_, ...), custom_call_target="tpu_custom_call" | custom-call | flops 1610612736 | bytes 2097152 | tf_op jit(solution)/shard_map/band_product/pallas_call | solution.py:174
  63.8 2.9 %collective-permute-done.9 = f32[192,256]{1,0:T(8,128)S(1)} collective-permute-done((f32[192,256]{1,0:T(8,128)S(1)}, f32[192,256]{1,0:T(8,128)S(1)}, u32[]{:S(2)}, u32[]{:S(2)}) %collective-permute-start.9) | collective-permute-done | bytes 196640 | tf_op jit(solution)/shard_map/ppermute | solution.py:351
  66.8 1.0 collective-permute-start.11
  67.8 2.3 %band_product.3.keep = f32[2,256,512]{2,1,0:T(8,128)S(1)} custom-call(s32[50]{0:T(128)S(1)} %concatenate.6.at, f32[1024,1024]{1,0:T(8,128)S(1)} %copy-done.1, bf16[512,512]{1,0:T(8,128)(2,1)S(1)} %get-tuple-element.34.refs_0_, bf16[512,512]{1,0:T(8,128)(2,1)S(1)} %get-tuple-element.35.refs_1_, bf16[512,512]{1,0:T(8,128)(2,1)S(1)} %get-tuple-element.36.refs_2_, ...), custom_call_target="tpu_custom_call" | custom-call | flops 1610612736 | bytes 2097152 | tf_op jit(solution)/shard_map/band_product/pallas_call | solution.py:174
  70.1 4.0 %collective-permute-done.11 = f32[192,256]{1,0:T(8,128)S(1)} collective-permute-done((f32[192,256]{1,0:T(8,128)S(1)}, f32[192,256]{1,0:T(8,128)S(1)}, u32[]{:S(2)}, u32[]{:S(2)}) %collective-permute-start.11) | collective-permute-done | bytes 196640 | tf_op jit(solution)/shard_map/ppermute | solution.py:351
  74.2 1.8 %collective-permute-start.12 = (f32[256,512]{1,0:T(8,128)S(1)}, f32[256,512]{1,0:T(8,128)S(1)}, u32[]{:S(2)}, u32[]{:S(2)}) collective-permute-start(f32[256,512]{1,0:T(8,128)S(1)} %fusion), channel_id=1, source_target_pairs={{0,2},{1,3},{2,0},{3,1},{4,6},{5,7},{6,4},{7,5},{8,10},{9,11},{10,... | collective-permute-start | bytes 1572872 | tf_op jit(solution)/shard_map/ppermute | solution.py:351
  76.0 1.7 %collective-permute-start.13 = (f32[192,256]{1,0:T(8,128)S(1)}, f32[192,256]{1,0:T(8,128)S(1)}, u32[]{:S(2)}, u32[]{:S(2)}) collective-permute-start(f32[192,256]{1,0:T(8,128)S(1)} %add.22), channel_id=1, source_target_pairs={{0,8},{4,12},{8,0},{12,4},{1,9},{5,13},{9,1},{13,5},{2,10},{6,14},... | collective-permute-start | bytes 589832 | tf_op jit(solution)/shard_map/ppermute | solution.py:351
  77.7 9.6 %collective-permute-done.13 = f32[192,256]{1,0:T(8,128)S(1)} collective-permute-done((f32[192,256]{1,0:T(8,128)S(1)}, f32[192,256]{1,0:T(8,128)S(1)}, u32[]{:S(2)}, u32[]{:S(2)}) %collective-permute-start.13) | collective-permute-done | bytes 196640 | tf_op jit(solution)/shard_map/ppermute | solution.py:351
  87.4 0.8 collective-permute-start.14
  88.2 1.5 %column_rows.1 = (f32[256,256]{1,0:T(8,128)}, f32[256,256]{1,0:T(8,128)}) custom-call(s32[50]{0:T(128)S(1)} %concatenate.6.at, f32[2,256,512]{2,1,0:T(8,128)S(1)} %band_product.3.keep, f32[2,256,512]{2,1,0:T(8,128)S(1)} %collective-permute-done.10.got, f32[256,512]{1,0:T(8,128)S(1)} %collective-permute-done.12.other, f32[256,256]{1,0:T(8,128)S(1)} %copy-done.2), custom_call_target="tpu_custom_call" | custom-call | tf_op jit(solution)/shard_map/column_rows/pallas_call | solution.py:294
  89.8 4.1 %collective-permute-done.14 = f32[192,256]{1,0:T(8,128)S(1)} collective-permute-done((f32[192,256]{1,0:T(8,128)S(1)}, f32[192,256]{1,0:T(8,128)S(1)}, u32[]{:S(2)}, u32[]{:S(2)}) %collective-permute-start.14) | collective-permute-done | bytes 196640 | tf_op jit(solution)/shard_map/ppermute | solution.py:351
  93.9 1.7 %collective-permute-done.15.second = f32[384,256]{1,0:T(8,128)S(1)} collective-permute-done((f32[384,256]{1,0:T(8,128)S(1)}, f32[384,256]{1,0:T(8,128)S(1)}, u32[]{:S(2)}, u32[]{:S(2)}) %collective-permute-start.15) | collective-permute-done | bytes 393248 | tf_op jit(solution)/shard_map/ppermute | solution.py:351
  95.7 1.9 %small_blocks.1 = (f32[256,256]{1,0:T(8,128)}, f32[256,256]{1,0:T(8,128)}, f32[256,256]{1,0:T(8,128)}) custom-call(s32[50]{0:T(128)S(1)} %concatenate.6.at, f32[256,256]{1,0:T(8,128)S(1)} %copy-done.2, f32[256,256]{1,0:T(8,128)S(1)} %copy-done.3, f32[256,256]{1,0:T(8,128)S(1)} %copy-done.4, f32[384,256]{1,0:T(8,128)S(1)} %constant_dynamic-update-slice_fusion.first, ...), custom_call_target="tpu_custom_call" | custom-call | tf_op jit(solution)/shard_map/small_blocks/pallas_call | solution.py:327
  (29 shorter events, 0.7 us)
Async XLA Ops:
  0.6 1.9 %collective-permute-start.2 = (f32[256,256]{1,0:T(8,128)}, f32[256,256]{1,0:T(8,128)S(1)}, u32[]{:S(2)}, u32[]{:S(2)}) collective-permute-start(f32[256,256]{1,0:T(8,128)} %refs_0_.1), channel_id=1, source_target_pairs={{0,1},{1,0},{2,3},{3,2},{4,5},{5,4},{6,7},{7,6},{8,9},{9,8},{10,11... | collective-permute-start | bytes 786440 | tf_op jit(solution)/shard_map/ppermute | solution.py:351
  1.1 1.7 %collective-permute-start.3 = (f32[256,256]{1,0:T(8,128)}, f32[256,256]{1,0:T(8,128)S(1)}, u32[]{:S(2)}, u32[]{:S(2)}) collective-permute-start(f32[256,256]{1,0:T(8,128)} %refs_1_.1), channel_id=1, source_target_pairs={{0,1},{1,0},{2,3},{3,2},{4,5},{5,4},{6,7},{7,6},{8,9},{9,8},{10,11... | collective-permute-start | bytes 786440 | tf_op jit(solution)/shard_map/ppermute | solution.py:351
  3.0 43.0 %collective-permute-start.7 = (f32[1024,256]{1,0:T(8,128)S(1)}, f32[1024,256]{1,0:T(8,128)S(1)}, u32[]{:S(2)}, u32[]{:S(2)}) collective-permute-start(f32[1024,256]{1,0:T(8,128)S(1)} %stack_rows.3.here), channel_id=1, source_target_pairs={{0,8},{1,12},{2,0},{3,4},{4,9},{5,13},{6,1},{7,5},{8,10},{9,14},{1... | collective-permute-start | bytes 3145736 | tf_op jit(solution)/shard_map/ppermute | solution.py:358
  7.0 40.5 %collective-permute-start.6 = (f32[1024,256]{1,0:T(8,128)S(1)}, f32[1024,256]{1,0:T(8,128)S(1)}, u32[]{:S(2)}, u32[]{:S(2)}) collective-permute-start(f32[1024,256]{1,0:T(8,128)S(1)} %stack_rows.3.here), channel_id=1, source_target_pairs={{0,0},{1,4},{2,8},{3,12},{4,1},{5,5},{6,9},{7,13},{8,2},{9,6},{10,... | collective-permute-start | bytes 3145736 | tf_op jit(solution)/shard_map/ppermute | solution.py:358
  7.7 30.6 %collective-permute-start = (f32[256,256]{1,0:T(8,128)}, f32[256,256]{1,0:T(8,128)S(1)}, u32[]{:S(2)}, u32[]{:S(2)}) collective-permute-start(f32[256,256]{1,0:T(8,128)} %refs_0_.1), channel_id=1, source_target_pairs={{0,2},{1,3},{2,0},{3,1},{4,6},{5,7},{6,4},{7,5},{8,10},{9,11},{10,... | collective-permute-start | bytes 786440 | tf_op jit(solution)/shard_map/ppermute | solution.py:351
  11.9 29.3 %collective-permute-start.1 = (f32[256,256]{1,0:T(8,128)}, f32[256,256]{1,0:T(8,128)}, u32[]{:S(2)}, u32[]{:S(2)}) collective-permute-start(f32[256,256]{1,0:T(8,128)} %refs_1_.1), channel_id=1, source_target_pairs={{0,2},{1,3},{2,0},{3,1},{4,6},{5,7},{6,4},{7,5},{8,10},{9,11},{10,... | collective-permute-start | bytes 786440 | tf_op jit(solution)/shard_map/ppermute | solution.py:351
  12.8 2.2 %copy-start = (f32[1024,1024]{1,0:T(8,128)S(1)}, f32[1024,1024]{1,0:T(8,128)}, u32[]{:S(2)}) copy-start(f32[1024,1024]{1,0:T(8,128)} %known.7) | copy-start | bytes 12582916
  15.0 28.0 %copy-start.1 = (f32[1024,1024]{1,0:T(8,128)S(1)}, f32[1024,1024]{1,0:T(8,128)}, u32[]{:S(2)}) copy-start(f32[1024,1024]{1,0:T(8,128)} %known.7) | copy-start | bytes 12582916
  38.4 2.9 %collective-permute-start.4 = (f32[256,256]{1,0:T(8,128)S(1)}, f32[256,256]{1,0:T(8,128)S(1)}, u32[]{:S(2)}, u32[]{:S(2)}) collective-permute-start(f32[256,256]{1,0:T(8,128)S(1)} %collective-permute-done.two), channel_id=1, source_target_pairs={{0,1},{1,0},{2,3},{3,2},{4,5},{5,4},{6,7},{7,6},{8,9},{9,8},{10,11... | collective-permute-start | bytes 786440 | tf_op jit(solution)/shard_map/ppermute | solution.py:351
  41.3 1.7 %collective-permute-start.5 = (f32[256,256]{1,0:T(8,128)}, f32[256,256]{1,0:T(8,128)S(1)}, u32[]{:S(2)}, u32[]{:S(2)}) collective-permute-start(f32[256,256]{1,0:T(8,128)} %collective-permute-done.1.one), channel_id=1, source_target_pairs={{0,1},{1,0},{2,3},{3,2},{4,5},{5,4},{6,7},{7,6},{8,9},{9,8},{10,11... | collective-permute-start | bytes 786440 | tf_op jit(solution)/shard_map/ppermute | solution.py:351
  49.0 1.8 %collective-permute-start.8 = (f32[384,256]{1,0:T(8,128)S(1)}, f32[384,256]{1,0:T(8,128)S(1)}, u32[]{:S(2)}, u32[]{:S(2)}) collective-permute-start(f32[384,256]{1,0:T(8,128)S(1)} %get-tuple-element.32), channel_id=1, source_target_pairs={{0,1},{1,0},{2,3},{3,2},{4,5},{5,4},{6,7},{7,6},{8,9},{9,8},{10,11... | collective-permute-start | bytes 1179656 | tf_op jit(solution)/shard_map/ppermute | solution.py:351
  50.9 15.8 %collective-permute-start.9 = (f32[192,256]{1,0:T(8,128)S(1)}, f32[192,256]{1,0:T(8,128)S(1)}, u32[]{:S(2)}, u32[]{:S(2)}) collective-permute-start(f32[192,256]{1,0:T(8,128)S(1)} %slice.17), channel_id=1, source_target_pairs={{0,2},{1,3},{2,0},{3,1},{4,6},{5,7},{6,4},{7,5},{8,10},{9,11},{10,... | collective-permute-start | bytes 589832 | tf_op jit(solution)/shard_map/ppermute | solution.py:351
  66.7 21.5 %copy-start.2 = (f32[256,256]{1,0:T(8,128)S(1)}, f32[256,256]{1,0:T(8,128)}, u32[]{:S(2)}) copy-start(f32[256,256]{1,0:T(8,128)} %top.3) | copy-start | bytes 786436
  66.7 7.4 %collective-permute-start.10 = (f32[2,256,512]{2,1,0:T(8,128)S(1)}, f32[2,256,512]{2,1,0:T(8,128)S(1)}, u32[]{:S(2)}, u32[]{:S(2)}) collective-permute-start(f32[2,256,512]{2,1,0:T(8,128)S(1)} %band_product.2), channel_id=1, source_target_pairs={{0,1},{1,0},{2,3},{3,2},{4,5},{5,4},{6,7},{7,6},{8,9},{9,8},{10,11... | collective-permute-start | bytes 3145736 | tf_op jit(solution)/shard_map/ppermute | solution.py:351
  66.8 7.3 %collective-permute-start.11 = (f32[192,256]{1,0:T(8,128)S(1)}, f32[192,256]{1,0:T(8,128)S(1)}, u32[]{:S(2)}, u32[]{:S(2)}) collective-permute-start(f32[192,256]{1,0:T(8,128)S(1)} %slice_add_fusion.1), channel_id=1, source_target_pairs={{0,4},{4,0},{8,12},{12,8},{1,5},{5,1},{9,13},{13,9},{2,6},{6,2},{1... | collective-permute-start | bytes 589832 | tf_op jit(solution)/shard_map/ppermute | solution.py:351
  70.1 25.6 %copy-start.3 = (f32[256,256]{1,0:T(8,128)S(1)}, f32[256,256]{1,0:T(8,128)}, u32[]{:S(2)}) copy-start(f32[256,256]{1,0:T(8,128)} %inner_two.1) | copy-start | bytes 786436
  70.1 25.5 %copy-start.4 = (f32[256,256]{1,0:T(8,128)S(1)}, f32[256,256]{1,0:T(8,128)}, u32[]{:S(2)}) copy-start(f32[256,256]{1,0:T(8,128)} %inner_one.1) | copy-start | bytes 786436
  74.2 14.0 %collective-permute-start.12 = (f32[256,512]{1,0:T(8,128)S(1)}, f32[256,512]{1,0:T(8,128)S(1)}, u32[]{:S(2)}, u32[]{:S(2)}) collective-permute-start(f32[256,512]{1,0:T(8,128)S(1)} %fusion), channel_id=1, source_target_pairs={{0,2},{1,3},{2,0},{3,1},{4,6},{5,7},{6,4},{7,5},{8,10},{9,11},{10,... | collective-permute-start | bytes 1572872 | tf_op jit(solution)/shard_map/ppermute | solution.py:351
  76.0 11.3 %collective-permute-start.13 = (f32[192,256]{1,0:T(8,128)S(1)}, f32[192,256]{1,0:T(8,128)S(1)}, u32[]{:S(2)}, u32[]{:S(2)}) collective-permute-start(f32[192,256]{1,0:T(8,128)S(1)} %add.22), channel_id=1, source_target_pairs={{0,8},{4,12},{8,0},{12,4},{1,9},{5,13},{9,1},{13,5},{2,10},{6,14},... | collective-permute-start | bytes 589832 | tf_op jit(solution)/shard_map/ppermute | solution.py:351
  87.4 6.5 %collective-permute-start.14 = (f32[192,256]{1,0:T(8,128)S(1)}, f32[192,256]{1,0:T(8,128)S(1)}, u32[]{:S(2)}, u32[]{:S(2)}) collective-permute-start(f32[192,256]{1,0:T(8,128)S(1)} %add.23), channel_id=1, source_target_pairs={{0,2},{1,3},{2,0},{3,1},{4,6},{5,7},{6,4},{7,5},{8,10},{9,11},{10,... | collective-permute-start | bytes 589832 | tf_op jit(solution)/shard_map/ppermute | solution.py:351
  93.9 1.8 %collective-permute-start.15 = (f32[384,256]{1,0:T(8,128)S(1)}, f32[384,256]{1,0:T(8,128)S(1)}, u32[]{:S(2)}, u32[]{:S(2)}) collective-permute-start(f32[384,256]{1,0:T(8,128)S(1)} %constant_dynamic-update-slice_fusion.first), channel_id=1, source_target_pairs={{0,1},{1,0},{2,3},{3,2},{4,5},{5,4},{6,7},{7,6},{8,9},{9,8},{10,11... | collective-permute-start | bytes 1179656 | tf_op jit(solution)/shard_map/ppermute | solution.py:351

commit v5 on v4

--- a/solution.py
+++ b/solution.py
@@ -201,6 +201,11 @@
 
 def arrived_columns(row, m, width):
     return pl.ds(pl.multiple_of(((row >> 1) ^ m) * (2 * width), 2 * width), 2 * width)
+
+
+def eighth(at, e, h, width):
+    part = width // 8
+    return pl.multiple_of(((e ^ at[1]) * 2 + (h ^ (at[0] & 1))) * part, part)
 
 
 def sums_kernel(n, m, at, left_high, left_low, arrived, *refs):
@@ -226,12 +231,12 @@
     before, keep, send, total = refs[0], refs[1], refs[2], refs[5]
     total[: 2 * width] = before[: 2 * width] + first
     total[2 * width :] = before[2 * width :] + second
-    quarter = width // n
     for e in range(n):
-        for s in range(3):
-            start = pl.multiple_of(s * width + (e ^ col) * quarter, quarter)
-            where = pl.ds(((e >> 1) * 3 + s) * quarter, quarter)
-            (send if e & 1 else keep)[where] = total[pl.ds(start, quarter)]
+        for h in range(2):
+            for s in range(3):
+                start = ((e >> 1) * 6 + h * 3 + s) * (width // 8)
+                part = total[pl.ds(s * width + eighth(at, e, h, width), width // 8)]
+                (send if e & 1 else keep)[start : start + width // 8] = part
 
 
 def small_sums(n, at, left, arrived):
@@ -302,13 +307,13 @@
 
 
 def blocks_kernel(n, at, top, inner_two, inner_one, first, second, diag_two, cross, diag_one, sums):
-    col = at[1]
-    quarter = top.shape[0] // n
-    for e, (part, i) in enumerate(((first, 0), (second, 0), (first, 1), (second, 1))):
-        for s in range(3):
-            start = (i * 3 + s) * quarter
-            where = pl.ds(pl.multiple_of((e ^ col) * quarter, quarter), quarter)
-            sums[s, where] = part[start : start + quarter]
+    width = top.shape[0]
+    for e in range(n):
+        for h in range(2):
+            for s in range(3):
+                start = ((e >> 1) * 6 + h * 3 + s) * (width // 8)
+                part = (second if e & 1 else first)[start : start + width // 8]
+                sums[s, pl.ds(eighth(at, e, h, width), width // 8)] = part
     t = halves(top[...])
     d = inner_two[...] + sums[0]
     diag_two[...] = d
@@ -353,6 +358,10 @@
     core = functools.partial(along, "pcol", 1)
     across = functools.partial(along, "pcol", 2)
 
+    def opposite(rows):
+        pairs = [(r * n + c, (r ^ 1) * n + (c ^ 2)) for r in range(n) for c in range(n)]
+        return lax.ppermute(rows, ("prow", "pcol"), pairs)
+
     def direct(k, rows):
         pairs = [(z * n + j, (j ^ k) * n + z) for z in range(n) for j in range(n)]
         return lax.ppermute(rows, ("prow", "pcol"), pairs)
@@ -366,16 +375,16 @@
 
     keep_sums, send_sums, right = small_sums(n, at, left, gathered)
     mine = keep_sums + core(send_sums)
-    half = mine.shape[0] // 2
     send = band_product(n, 1, after(at, mine), known, right)
-    mine = mine[:half] + across(mine[half:])
+    keep = band_product(n, 0, after(at, send), known, right)
+    own, beyond, beside, corner = jnp.split(mine, 4)
+    mine = (own + along("prow", 1, beyond)) + (across(beside) + opposite(corner))
     got = core(after(send, mine))
-    keep = band_product(n, 0, after(at, mine, send), known, right)
-    mine = mine + along("prow", 1, mine)
-    other = across(after(keep[1] + got[1], mine))
+    other = across(keep[1] + got[1])
     mine = mine + along("prow", 2, mine)
     column_two, column_one = columns(n, at, keep, got, other, top_one)
-    both = jnp.concatenate([after(mine, column_one), across(mine)])
+    both = [mine, along("prow", 1, mine), across(mine), opposite(mine)]
+    both = jnp.concatenate([after(both[0], column_one)] + both[1:])
     both = both, core(both)
     diag_two, cross_block, diag_one = small_blocks(n, at, top_one, inner_two, inner_one, both)
     return (column_two, diag_two, column_one, cross_block, diag_one)

time: 97.8 us -> 93.3 us (0.954)
  waiting for transfers between devices: 50.1 us -> 42.3 us
  starting transfers between devices: 25.8 us -> 29.1 us
    ppermute x14 -> x15, waiting for transfers between devices: 50.1 us -> 40.3 us  [along(): return lax.ppermute(array, axis, [(i, i ^ k) for i in range(n)])]
    ppermute x0 -> x2, starting transfers between devices: none -> 3.07 us  [opposite(): return lax.ppermute(rows, ('prow', 'pcol'), pairs)]
    ppermute x0 -> x2, waiting for transfers between devices: none -> 2.02 us  [opposite(): return lax.ppermute(rows, ('prow', 'pcol'), pairs)]
    ppermute x14 -> x15, starting transfers between devices: 21.1 us -> 21.3 us  [along(): return lax.ppermute(array, axis, [(i, i ^ k) for i in range(n)])]
    unnamed x11 -> x13, local copies, waits for them, and re-layouts: 2.22 us -> 2.24 us
  transfers between devices with their start and end apart: 16 -> 19, of which waited for: 11 -> 12; matrix products, arithmetic and copies ran while one was open for 1% -> 1% of each run, Pallas kernels for 14% -> 15%
where the time goes in v5:
time: 93.3 us; the launch traced here: 93.1 us
  waiting for transfers between devices  42.3 us (45%)
  starting transfers between devices  29.1 us (31%)
  Pallas kernels  17.7 us (19%)
  local copies, waits for them, and re-layouts  3.03 us (3%)
    ppermute x15, waiting for transfers between devices, along(): return lax.ppermute(array, axis, [(i, i ^ k) for i in range(n)])  40.3 us
    ppermute x15, starting transfers between devices, along(): return lax.ppermute(array, axis, [(i, i ^ k) for i in range(n)])  21.3 us
    pallas_call x6, Pallas kernels, call(): pl.pallas_call(kernel, out_shape=out_shape, in_specs=[SMEM] + [VMEM] * (l...  13.1 us
    ppermute x2, starting transfers between devices, direct(): return lax.ppermute(rows, ('prow', 'pcol'), pairs)  4.73 us
    ppermute x2, starting transfers between devices, opposite(): return lax.ppermute(rows, ('prow', 'pcol'), pairs)  3.07 us
    unnamed x13, local copies, waits for them, and re-layouts  2.24 us
    ppermute x2, waiting for transfers between devices, opposite(): return lax.ppermute(rows, ('prow', 'pcol'), pairs)  2.02 us
    pallas_call x1, Pallas kernels, small_blocks(): pl.pallas_call(functools.partial(blocks_kernel, n), out_shape=(shape, sha...  1.89 us
  transfers between devices with their start and end apart: 19, of which 12 were waited for; matrix products, arithmetic and copies ran while one was open for 1% of the time, Pallas kernels for 15%

profile of v5, /device:TPU:0, one launch (start us, length us, event | category | flops | bytes accessed | tf_op | source)
XLA Modules:
  0.0 93.1 jit_solution(2200737082862107379)
XLA Ops:
  0.6 0.5 collective-permute-start.2
  1.2 1.0 %stack_rows.2.refs_0_ = f32[512,256]{1,0:T(8,128)S(1)} custom-call(f32[256,256]{1,0:T(8,128)} %refs_0_.1, f32[256,256]{1,0:T(8,128)} %refs_1_.1), custom_call_target="tpu_custom_call" | custom-call | bytes 1048576 | tf_op jit(solution)/shard_map/stack_rows/pallas_call | solution.py:141
  2.5 0.4 collective-permute-done.3.refs_2_
  3.0 4.0 %collective-permute-start.7 = (f32[1024,256]{1,0:T(8,128)S(1)}, f32[1024,256]{1,0:T(8,128)S(1)}, u32[]{:S(2)}, u32[]{:S(2)}) collective-permute-start(f32[1024,256]{1,0:T(8,128)S(1)} %stack_rows.3.here), channel_id=1, source_target_pairs={{0,8},{1,12},{2,0},{3,4},{4,9},{5,13},{6,1},{7,5},{8,10},{9,14},{1... | collective-permute-start | bytes 3145736 | tf_op jit(solution)/shard_map/ppermute | solution.py:367
  7.0 0.7 collective-permute-start.6
  7.7 4.2 %collective-permute-start = (f32[256,256]{1,0:T(8,128)}, f32[256,256]{1,0:T(8,128)S(1)}, u32[]{:S(2)}, u32[]{:S(2)}) collective-permute-start(f32[256,256]{1,0:T(8,128)} %refs_0_.1), channel_id=1, source_target_pairs={{0,2},{1,3},{2,0},{3,1},{4,6},{5,7},{6,4},{7,5},{8,10},{9,11},{10,... | collective-permute-start | bytes 786440 | tf_op jit(solution)/shard_map/ppermute | solution.py:356
  12.0 0.8 concatenate.6.at
  12.8 2.2 %copy-done = f32[1024,1024]{1,0:T(8,128)S(1)} copy-done((f32[1024,1024]{1,0:T(8,128)S(1)}, f32[1024,1024]{1,0:T(8,128)}, u32[]{:S(2)}) %copy-start) | copy-done | bytes 4194328
  15.0 2.4 %left_first.1.before = f32[512,1024]{1,0:T(8,128)S(1)} custom-call(s32[50]{0:T(128)S(1)} %concatenate.6.at, f32[1024,1024]{1,0:T(8,128)S(1)} %copy-done, f32[1024,256]{1,0:T(8,128)S(1)} %stack_rows.3.here), custom_call_target="tpu_custom_call" | custom-call | tf_op jit(solution)/shard_map/left_first/pallas_call | solution.py:174
  17.4 20.9 %collective-permute-done.two = f32[256,256]{1,0:T(8,128)S(1)} collective-permute-done((f32[256,256]{1,0:T(8,128)}, f32[256,256]{1,0:T(8,128)S(1)}, u32[]{:S(2)}, u32[]{:S(2)}) %collective-permute-start) | collective-permute-done | bytes 262176 | tf_op jit(solution)/shard_map/ppermute | solution.py:356
  38.4 2.9 %collective-permute-done.1.one = f32[256,256]{1,0:T(8,128)} collective-permute-done((f32[256,256]{1,0:T(8,128)}, f32[256,256]{1,0:T(8,128)}, u32[]{:S(2)}, u32[]{:S(2)}) %collective-permute-start.1) | collective-permute-done | bytes 262176 | tf_op jit(solution)/shard_map/ppermute | solution.py:356
  41.3 1.7 %collective-permute-done.5.core_one = f32[256,256]{1,0:T(8,128)S(1)} collective-permute-done((f32[256,256]{1,0:T(8,128)}, f32[256,256]{1,0:T(8,128)S(1)}, u32[]{:S(2)}, u32[]{:S(2)}) %collective-permute-start.5) | collective-permute-done | bytes 262176 | tf_op jit(solution)/shard_map/ppermute | solution.py:356
  43.0 3.0 %left_last.1 = (bf16[512,1024]{1,0:T(8,128)(2,1)S(1)}, bf16[512,1024]{1,0:T(8,128)(2,1)S(1)}) custom-call(s32[50]{0:T(128)S(1)} %concatenate.6.at, f32[1024,1024]{1,0:T(8,128)S(1)} %copy-done.1, f32[256,256]{1,0:T(8,128)S(1)} %collective-permute-done.two, f32[256,256]{1,0:T(8,128)} %collective-permute-done.1.one, ...), custom_call_target="tpu_custom_call" | custom-call | tf_op jit(solution)/shard_map/left_last/pallas_call | solution.py:174
  46.0 1.5 %first_sums.1 = (f32[768,256]{1,0:T(8,128)S(1)}, bf16[512,512]{1,0:T(8,128)(2,1)S(1)}, bf16[512,512]{1,0:T(8,128)(2,1)S(1)}) custom-call(s32[50]{0:T(128)S(1)} %concatenate.6.at, bf16[512,1024]{1,0:T(8,128)(2,1)S(1)} %get-tuple-element.27.left_high, bf16[512,1024]{1,0:T(8,128)(2,1)S(1)} %get-tuple-element.28.left_low, ...), custom_call_target="tpu_custom_call" | custom-call | flops 603979776 | tf_op jit(solution)/shard_map/first_sums/pallas_call | solution.py:174
  47.5 1.5 %last_sums.1 = (f32[384,256]{1,0:T(8,128)S(1)}, f32[384,256]{1,0:T(8,128)S(1)}, bf16[512,512]{1,0:T(8,128)(2,1)S(1)}, bf16[512,512]{1,0:T(8,128)(2,1)S(1)}) custom-call(s32[50]{0:T(128)S(1)} %concatenate.6.at, bf16[512,1024]{1,0:T(8,128)(2,1)S(1)} %get-tuple-element.27.left_high, bf16[512,1024]{1,0:T(8,128)(2,1)S(1)} %get-tuple-element.28.left_low, ...), custom_call_target="tpu_custom_call" | custom-call | flops 603979776 | tf_op jit(solution)/shard_map/last_sums/pallas_call | solution.py:174
  49.2 1.6 %collective-permute-done.8 = f32[384,256]{1,0:T(8,128)S(1)} collective-permute-done((f32[384,256]{1,0:T(8,128)S(1)}, f32[384,256]{1,0:T(8,128)S(1)}, u32[]{:S(2)}, u32[]{:S(2)}) %collective-permute-start.8) | collective-permute-done | bytes 393248 | tf_op jit(solution)/shard_map/ppermute | solution.py:356
  50.9 10.6 %collective-permute-start.10 = (f32[96,256]{1,0:T(8,128)S(1)}, f32[96,256]{1,0:T(8,128)S(1)}, u32[]{:S(2)}, u32[]{:S(2)}) collective-permute-start(f32[96,256]{1,0:T(8,128)S(1)} %get-tuple-element.46), channel_id=1, source_target_pairs={{0,2},{1,3},{2,0},{3,1},{4,6},{5,7},{6,4},{7,5},{8,10},{9,11},{10,... | collective-permute-start | bytes 294920 | tf_op jit(solution)/shard_map/ppermute | solution.py:356
  61.5 0.4 collective-permute-start.11
  61.9 1.1 %collective-permute-start.9 = (f32[96,256]{1,0:T(8,128)S(1)}, f32[96,256]{1,0:T(8,128)S(1)}, u32[]{:S(2)}, u32[]{:S(2)}) collective-permute-start(f32[96,256]{1,0:T(8,128)S(1)} %get-tuple-element.47), channel_id=1, source_target_pairs={{0,4},{4,0},{8,12},{12,8},{1,5},{5,1},{9,13},{13,9},{2,6},{6,2},{1... | collective-permute-start | bytes 294920 | tf_op jit(solution)/shard_map/ppermute | solution.py:356
  63.0 2.3 %band_product.2 = f32[2,256,512]{2,1,0:T(8,128)S(1)} custom-call(s32[50]{0:T(128)S(1)} %concatenate.6.at, f32[1024,1024]{1,0:T(8,128)S(1)} %copy-done.1, bf16[512,512]{1,0:T(8,128)(2,1)S(1)} %get-tuple-element.33.refs_0_, bf16[512,512]{1,0:T(8,128)(2,1)S(1)} %get-tuple-element.34.refs_1_, bf16[512,512]{1,0:T(8,128)(2,1)S(1)} %get-tuple-element.35.refs_2_, ...), custom_call_target="tpu_custom_call" | custom-call | flops 1610612736 | bytes 2097152 | tf_op jit(solution)/shard_map/band_product/pallas_call | solution.py:174
  65.4 0.6 collective-permute-done.10
  66.0 2.0 %collective-permute-done.11 = f32[96,256]{1,0:T(8,128)S(1)} collective-permute-done((f32[96,256]{1,0:T(8,128)S(1)}, f32[96,256]{1,0:T(8,128)S(1)}, u32[]{:S(2)}, u32[]{:S(2)}) %collective-permute-start.11) | collective-permute-done | bytes 98336 | tf_op jit(solution)/shard_map/ppermute | solution.py:363
  68.1 2.3 %band_product.3.keep = f32[2,256,512]{2,1,0:T(8,128)S(1)} custom-call(s32[50]{0:T(128)S(1)} %concatenate.6.at, f32[1024,1024]{1,0:T(8,128)S(1)} %copy-done.1, bf16[512,512]{1,0:T(8,128)(2,1)S(1)} %get-tuple-element.33.refs_0_, bf16[512,512]{1,0:T(8,128)(2,1)S(1)} %get-tuple-element.34.refs_1_, bf16[512,512]{1,0:T(8,128)(2,1)S(1)} %get-tuple-element.35.refs_2_, ...), custom_call_target="tpu_custom_call" | custom-call | flops 1610612736 | bytes 2097152 | tf_op jit(solution)/shard_map/band_product/pallas_call | solution.py:174
  70.8 1.7 %collective-permute-start.13 = (f32[256,512]{1,0:T(8,128)S(1)}, f32[256,512]{1,0:T(8,128)S(1)}, u32[]{:S(2)}, u32[]{:S(2)}) collective-permute-start(f32[256,512]{1,0:T(8,128)S(1)} %fusion), channel_id=1, source_target_pairs={{0,2},{1,3},{2,0},{3,1},{4,6},{5,7},{6,4},{7,5},{8,10},{9,11},{10,... | collective-permute-start | bytes 1572872 | tf_op jit(solution)/shard_map/ppermute | solution.py:356
  72.5 1.8 %collective-permute-start.14 = (f32[96,256]{1,0:T(8,128)S(1)}, f32[96,256]{1,0:T(8,128)S(1)}, u32[]{:S(2)}, u32[]{:S(2)}) collective-permute-start(f32[96,256]{1,0:T(8,128)S(1)} %fusion.1), channel_id=1, source_target_pairs={{0,8},{4,12},{8,0},{12,4},{1,9},{5,13},{9,1},{13,5},{2,10},{6,14},... | collective-permute-start | bytes 294920 | tf_op jit(solution)/shard_map/ppermute | solution.py:356
  74.3 5.9 %collective-permute-done.14 = f32[96,256]{1,0:T(8,128)S(1)} collective-permute-done((f32[96,256]{1,0:T(8,128)S(1)}, f32[96,256]{1,0:T(8,128)S(1)}, u32[]{:S(2)}, u32[]{:S(2)}) %collective-permute-start.14) | collective-permute-done | bytes 98336 | tf_op jit(solution)/shard_map/ppermute | solution.py:356
  80.3 0.8 collective-permute-start.16
  81.1 2.6 %collective-permute-start.17 = (f32[96,256]{1,0:T(8,128)S(1)}, f32[96,256]{1,0:T(8,128)S(1)}, u32[]{:S(2)}, u32[]{:S(2)}) collective-permute-start(f32[96,256]{1,0:T(8,128)S(1)} %add.27), channel_id=1, source_target_pairs={{0,6},{1,7},{2,4},{3,5},{4,2},{5,3},{6,0},{7,1},{8,14},{9,15},{10,... | collective-permute-start | bytes 294920 | tf_op jit(solution)/shard_map/ppermute | solution.py:363
  83.7 4.0 %collective-permute-done.13.other = f32[256,512]{1,0:T(8,128)S(1)} collective-permute-done((f32[256,512]{1,0:T(8,128)S(1)}, f32[256,512]{1,0:T(8,128)S(1)}, u32[]{:S(2)}, u32[]{:S(2)}) %collective-permute-start.13) | collective-permute-done | bytes 524320 | tf_op jit(solution)/shard_map/ppermute | solution.py:356
  87.8 1.5 %column_rows.1 = (f32[256,256]{1,0:T(8,128)}, f32[256,256]{1,0:T(8,128)}) custom-call(s32[50]{0:T(128)S(1)} %concatenate.6.at, f32[2,256,512]{2,1,0:T(8,128)S(1)} %band_product.3.keep, f32[2,256,512]{2,1,0:T(8,128)S(1)} %collective-permute-done.12.got, f32[256,512]{1,0:T(8,128)S(1)} %collective-permute-done.13.other, f32[256,256]{1,0:T(8,128)S(1)} %copy-done.2), custom_call_target="tpu_custom_call" | custom-call | tf_op jit(solution)/shard_map/column_rows/pallas_call | solution.py:299
  89.5 1.7 %collective-permute-done.18.second = f32[384,256]{1,0:T(8,128)S(1)} collective-permute-done((f32[384,256]{1,0:T(8,128)S(1)}, f32[384,256]{1,0:T(8,128)S(1)}, u32[]{:S(2)}, u32[]{:S(2)}) %collective-permute-start.18) | collective-permute-done | bytes 393248 | tf_op jit(solution)/shard_map/ppermute | solution.py:356
  91.2 1.9 %small_blocks.1 = (f32[256,256]{1,0:T(8,128)}, f32[256,256]{1,0:T(8,128)}, f32[256,256]{1,0:T(8,128)}) custom-call(s32[50]{0:T(128)S(1)} %concatenate.6.at, f32[256,256]{1,0:T(8,128)S(1)} %copy-done.2, f32[256,256]{1,0:T(8,128)S(1)} %copy-done.3, f32[256,256]{1,0:T(8,128)S(1)} %copy-done.4, f32[384,256]{1,0:T(8,128)S(1)} %constant_dynamic-update-slice_fusion.first, ...), custom_call_target="tpu_custom_call" | custom-call | tf_op jit(solution)/shard_map/small_blocks/pallas_call | solution.py:332
  (36 shorter events, 1.5 us)
Async XLA Ops:
  0.6 1.9 %collective-permute-start.2 = (f32[256,256]{1,0:T(8,128)}, f32[256,256]{1,0:T(8,128)S(1)}, u32[]{:S(2)}, u32[]{:S(2)}) collective-permute-start(f32[256,256]{1,0:T(8,128)} %refs_0_.1), channel_id=1, source_target_pairs={{0,1},{1,0},{2,3},{3,2},{4,5},{5,4},{6,7},{7,6},{8,9},{9,8},{10,11... | collective-permute-start | bytes 786440 | tf_op jit(solution)/shard_map/ppermute | solution.py:356
  1.1 1.7 %collective-permute-start.3 = (f32[256,256]{1,0:T(8,128)}, f32[256,256]{1,0:T(8,128)S(1)}, u32[]{:S(2)}, u32[]{:S(2)}) collective-permute-start(f32[256,256]{1,0:T(8,128)} %refs_1_.1), channel_id=1, source_target_pairs={{0,1},{1,0},{2,3},{3,2},{4,5},{5,4},{6,7},{7,6},{8,9},{9,8},{10,11... | collective-permute-start | bytes 786440 | tf_op jit(solution)/shard_map/ppermute | solution.py:356
  3.0 43.0 %collective-permute-start.7 = (f32[1024,256]{1,0:T(8,128)S(1)}, f32[1024,256]{1,0:T(8,128)S(1)}, u32[]{:S(2)}, u32[]{:S(2)}) collective-permute-start(f32[1024,256]{1,0:T(8,128)S(1)} %stack_rows.3.here), channel_id=1, source_target_pairs={{0,8},{1,12},{2,0},{3,4},{4,9},{5,13},{6,1},{7,5},{8,10},{9,14},{1... | collective-permute-start | bytes 3145736 | tf_op jit(solution)/shard_map/ppermute | solution.py:367
  7.0 40.5 %collective-permute-start.6 = (f32[1024,256]{1,0:T(8,128)S(1)}, f32[1024,256]{1,0:T(8,128)S(1)}, u32[]{:S(2)}, u32[]{:S(2)}) collective-permute-start(f32[1024,256]{1,0:T(8,128)S(1)} %stack_rows.3.here), channel_id=1, source_target_pairs={{0,0},{1,4},{2,8},{3,12},{4,1},{5,5},{6,9},{7,13},{8,2},{9,6},{10,... | collective-permute-start | bytes 3145736 | tf_op jit(solution)/shard_map/ppermute | solution.py:367
  7.7 30.6 %collective-permute-start = (f32[256,256]{1,0:T(8,128)}, f32[256,256]{1,0:T(8,128)S(1)}, u32[]{:S(2)}, u32[]{:S(2)}) collective-permute-start(f32[256,256]{1,0:T(8,128)} %refs_0_.1), channel_id=1, source_target_pairs={{0,2},{1,3},{2,0},{3,1},{4,6},{5,7},{6,4},{7,5},{8,10},{9,11},{10,... | collective-permute-start | bytes 786440 | tf_op jit(solution)/shard_map/ppermute | solution.py:356
  11.9 29.3 %collective-permute-start.1 = (f32[256,256]{1,0:T(8,128)}, f32[256,256]{1,0:T(8,128)}, u32[]{:S(2)}, u32[]{:S(2)}) collective-permute-start(f32[256,256]{1,0:T(8,128)} %refs_1_.1), channel_id=1, source_target_pairs={{0,2},{1,3},{2,0},{3,1},{4,6},{5,7},{6,4},{7,5},{8,10},{9,11},{10,... | collective-permute-start | bytes 786440 | tf_op jit(solution)/shard_map/ppermute | solution.py:356
  12.8 2.2 %copy-start = (f32[1024,1024]{1,0:T(8,128)S(1)}, f32[1024,1024]{1,0:T(8,128)}, u32[]{:S(2)}) copy-start(f32[1024,1024]{1,0:T(8,128)} %known.7) | copy-start | bytes 12582916
  15.0 28.0 %copy-start.1 = (f32[1024,1024]{1,0:T(8,128)S(1)}, f32[1024,1024]{1,0:T(8,128)}, u32[]{:S(2)}) copy-start(f32[1024,1024]{1,0:T(8,128)} %known.7) | copy-start | bytes 12582916
  38.4 2.9 %collective-permute-start.4 = (f32[256,256]{1,0:T(8,128)S(1)}, f32[256,256]{1,0:T(8,128)S(1)}, u32[]{:S(2)}, u32[]{:S(2)}) collective-permute-start(f32[256,256]{1,0:T(8,128)S(1)} %collective-permute-done.two), channel_id=1, source_target_pairs={{0,1},{1,0},{2,3},{3,2},{4,5},{5,4},{6,7},{7,6},{8,9},{9,8},{10,11... | collective-permute-start | bytes 786440 | tf_op jit(solution)/shard_map/ppermute | solution.py:356
  41.3 1.7 %collective-permute-start.5 = (f32[256,256]{1,0:T(8,128)}, f32[256,256]{1,0:T(8,128)S(1)}, u32[]{:S(2)}, u32[]{:S(2)}) collective-permute-start(f32[256,256]{1,0:T(8,128)} %collective-permute-done.1.one), channel_id=1, source_target_pairs={{0,1},{1,0},{2,3},{3,2},{4,5},{5,4},{6,7},{7,6},{8,9},{9,8},{10,11... | collective-permute-start | bytes 786440 | tf_op jit(solution)/shard_map/ppermute | solution.py:356
  49.0 1.8 %collective-permute-start.8 = (f32[384,256]{1,0:T(8,128)S(1)}, f32[384,256]{1,0:T(8,128)S(1)}, u32[]{:S(2)}, u32[]{:S(2)}) collective-permute-start(f32[384,256]{1,0:T(8,128)S(1)} %get-tuple-element.31), channel_id=1, source_target_pairs={{0,1},{1,0},{2,3},{3,2},{4,5},{5,4},{6,7},{7,6},{8,9},{9,8},{10,11... | collective-permute-start | bytes 1179656 | tf_op jit(solution)/shard_map/ppermute | solution.py:356
  50.9 15.1 %collective-permute-start.10 = (f32[96,256]{1,0:T(8,128)S(1)}, f32[96,256]{1,0:T(8,128)S(1)}, u32[]{:S(2)}, u32[]{:S(2)}) collective-permute-start(f32[96,256]{1,0:T(8,128)S(1)} %get-tuple-element.46), channel_id=1, source_target_pairs={{0,2},{1,3},{2,0},{3,1},{4,6},{5,7},{6,4},{7,5},{8,10},{9,11},{10,... | collective-permute-start | bytes 294920 | tf_op jit(solution)/shard_map/ppermute | solution.py:356
  61.5 6.5 %collective-permute-start.11 = (f32[96,256]{1,0:T(8,128)S(1)}, f32[96,256]{1,0:T(8,128)S(1)}, u32[]{:S(2)}, u32[]{:S(2)}) collective-permute-start(f32[96,256]{1,0:T(8,128)S(1)} %get-tuple-element.45), channel_id=1, source_target_pairs={{0,6},{1,7},{2,4},{3,5},{4,2},{5,3},{6,0},{7,1},{8,14},{9,15},{10,... | collective-permute-start | bytes 294920 | tf_op jit(solution)/shard_map/ppermute | solution.py:363
  61.9 6.1 %collective-permute-start.9 = (f32[96,256]{1,0:T(8,128)S(1)}, f32[96,256]{1,0:T(8,128)S(1)}, u32[]{:S(2)}, u32[]{:S(2)}) collective-permute-start(f32[96,256]{1,0:T(8,128)S(1)} %get-tuple-element.47), channel_id=1, source_target_pairs={{0,4},{4,0},{8,12},{12,8},{1,5},{5,1},{9,13},{13,9},{2,6},{6,2},{1... | collective-permute-start | bytes 294920 | tf_op jit(solution)/shard_map/ppermute | solution.py:356
  68.0 19.8 %copy-start.2 = (f32[256,256]{1,0:T(8,128)S(1)}, f32[256,256]{1,0:T(8,128)}, u32[]{:S(2)}) copy-start(f32[256,256]{1,0:T(8,128)} %top.3) | copy-start | bytes 786436
  68.0 2.7 %collective-permute-start.12 = (f32[2,256,512]{2,1,0:T(8,128)S(1)}, f32[2,256,512]{2,1,0:T(8,128)S(1)}, u32[]{:S(2)}, u32[]{:S(2)}) collective-permute-start(f32[2,256,512]{2,1,0:T(8,128)S(1)} %band_product.2), channel_id=1, source_target_pairs={{0,1},{1,0},{2,3},{3,2},{4,5},{5,4},{6,7},{7,6},{8,9},{9,8},{10,11... | collective-permute-start | bytes 3145736 | tf_op jit(solution)/shard_map/ppermute | solution.py:356
  70.5 20.7 %copy-start.3 = (f32[256,256]{1,0:T(8,128)S(1)}, f32[256,256]{1,0:T(8,128)}, u32[]{:S(2)}) copy-start(f32[256,256]{1,0:T(8,128)} %inner_two.1) | copy-start | bytes 786436
  70.5 20.7 %copy-start.4 = (f32[256,256]{1,0:T(8,128)S(1)}, f32[256,256]{1,0:T(8,128)}, u32[]{:S(2)}) copy-start(f32[256,256]{1,0:T(8,128)} %inner_one.1) | copy-start | bytes 786436
  70.8 16.9 %collective-permute-start.13 = (f32[256,512]{1,0:T(8,128)S(1)}, f32[256,512]{1,0:T(8,128)S(1)}, u32[]{:S(2)}, u32[]{:S(2)}) collective-permute-start(f32[256,512]{1,0:T(8,128)S(1)} %fusion), channel_id=1, source_target_pairs={{0,2},{1,3},{2,0},{3,1},{4,6},{5,7},{6,4},{7,5},{8,10},{9,11},{10,... | collective-permute-start | bytes 1572872 | tf_op jit(solution)/shard_map/ppermute | solution.py:356
  72.5 7.7 %collective-permute-start.14 = (f32[96,256]{1,0:T(8,128)S(1)}, f32[96,256]{1,0:T(8,128)S(1)}, u32[]{:S(2)}, u32[]{:S(2)}) collective-permute-start(f32[96,256]{1,0:T(8,128)S(1)} %fusion.1), channel_id=1, source_target_pairs={{0,8},{4,12},{8,0},{12,4},{1,9},{5,13},{9,1},{13,5},{2,10},{6,14},... | collective-permute-start | bytes 294920 | tf_op jit(solution)/shard_map/ppermute | solution.py:356
  80.2 9.1 %collective-permute-start.15 = (f32[96,256]{1,0:T(8,128)S(1)}, f32[96,256]{1,0:T(8,128)S(1)}, u32[]{:S(2)}, u32[]{:S(2)}) collective-permute-start(f32[96,256]{1,0:T(8,128)S(1)} %add.27), channel_id=1, source_target_pairs={{0,4},{4,0},{8,12},{12,8},{1,5},{5,1},{9,13},{13,9},{2,6},{6,2},{1... | collective-permute-start | bytes 294920 | tf_op jit(solution)/shard_map/ppermute | solution.py:356
  80.3 9.1 %collective-permute-start.16 = (f32[96,256]{1,0:T(8,128)S(1)}, f32[96,256]{1,0:T(8,128)S(1)}, u32[]{:S(2)}, u32[]{:S(2)}) collective-permute-start(f32[96,256]{1,0:T(8,128)S(1)} %add.27), channel_id=1, source_target_pairs={{0,2},{1,3},{2,0},{3,1},{4,6},{5,7},{6,4},{7,5},{8,10},{9,11},{10,... | collective-permute-start | bytes 294920 | tf_op jit(solution)/shard_map/ppermute | solution.py:356
  81.1 8.3 %collective-permute-start.17 = (f32[96,256]{1,0:T(8,128)S(1)}, f32[96,256]{1,0:T(8,128)S(1)}, u32[]{:S(2)}, u32[]{:S(2)}) collective-permute-start(f32[96,256]{1,0:T(8,128)S(1)} %add.27), channel_id=1, source_target_pairs={{0,6},{1,7},{2,4},{3,5},{4,2},{5,3},{6,0},{7,1},{8,14},{9,15},{10,... | collective-permute-start | bytes 294920 | tf_op jit(solution)/shard_map/ppermute | solution.py:363
  89.4 1.8 %collective-permute-start.18 = (f32[384,256]{1,0:T(8,128)S(1)}, f32[384,256]{1,0:T(8,128)S(1)}, u32[]{:S(2)}, u32[]{:S(2)}) collective-permute-start(f32[384,256]{1,0:T(8,128)S(1)} %constant_dynamic-update-slice_fusion.first), channel_id=1, source_target_pairs={{0,1},{1,0},{2,3},{3,2},{4,5},{5,4},{6,7},{7,6},{8,9},{9,8},{10,11... | collective-permute-start | bytes 1179656 | tf_op jit(solution)/shard_map/ppermute | solution.py:356

commit v6 on v5

--- a/solution.py
+++ b/solution.py
@@ -379,12 +379,12 @@
     keep = band_product(n, 0, after(at, send), known, right)
     own, beyond, beside, corner = jnp.split(mine, 4)
     mine = (own + along("prow", 1, beyond)) + (across(beside) + opposite(corner))
-    got = core(after(send, mine))
-    other = across(keep[1] + got[1])
+    got = core(send)
+    other = across(after(keep[1] + got[1], mine))
     mine = mine + along("prow", 2, mine)
     column_two, column_one = columns(n, at, keep, got, other, top_one)
     both = [mine, along("prow", 1, mine), across(mine), opposite(mine)]
-    both = jnp.concatenate([after(both[0], column_one)] + both[1:])
+    both = jnp.concatenate([after(both[0], other)] + both[1:])
     both = both, core(both)
     diag_two, cross_block, diag_one = small_blocks(n, at, top_one, inner_two, inner_one, both)
     return (column_two, diag_two, column_one, cross_block, diag_one)

time: 93.3 us -> 92 us (0.986)
  waiting for transfers between devices: 42.3 us -> 41.2 us
  transfers between devices with their start and end apart: 19 -> 19, of which waited for: 12 -> 12; matrix products, arithmetic and copies ran while one was open for 1% -> 1% of each run, Pallas kernels for 15% -> 13%
where the time goes in v6:
time: 92 us; the launch traced here: 91.8 us
  waiting for transfers between devices  41.2 us (45%)
  starting transfers between devices  28.9 us (31%)
  Pallas kernels  17.7 us (19%)
  local copies, waits for them, and re-layouts  3.03 us (3%)
    ppermute x15, waiting for transfers between devices, along(): return lax.ppermute(array, axis, [(i, i ^ k) for i in range(n)])  39.9 us
    ppermute x15, starting transfers between devices, along(): return lax.ppermute(array, axis, [(i, i ^ k) for i in range(n)])  21 us
    pallas_call x6, Pallas kernels, call(): pl.pallas_call(kernel, out_shape=out_shape, in_specs=[SMEM] + [VMEM] * (l...  13.1 us
    ppermute x2, starting transfers between devices, direct(): return lax.ppermute(rows, ('prow', 'pcol'), pairs)  4.73 us
    ppermute x2, starting transfers between devices, opposite(): return lax.ppermute(rows, ('prow', 'pcol'), pairs)  3.15 us
    unnamed x13, local copies, waits for them, and re-layouts  2.23 us
    pallas_call x1, Pallas kernels, small_blocks(): pl.pallas_call(functools.partial(blocks_kernel, n), out_shape=(shape, sha...  1.89 us
  transfers between devices with their start and end apart: 19, of which 12 were waited for; matrix products, arithmetic and copies ran while one was open for 1% of the time, Pallas kernels for 13%

profile of v6, /device:TPU:0, one launch (start us, length us, event | category | flops | bytes accessed | tf_op | source)
XLA Modules:
  0.0 91.8 jit_solution(8447241668226563335)
XLA Ops:
  0.6 0.5 collective-permute-start.2
  1.2 1.0 %stack_rows.2.refs_0_ = f32[512,256]{1,0:T(8,128)S(1)} custom-call(f32[256,256]{1,0:T(8,128)} %refs_0_.1, f32[256,256]{1,0:T(8,128)} %refs_1_.1), custom_call_target="tpu_custom_call" | custom-call | bytes 1048576 | tf_op jit(solution)/shard_map/stack_rows/pallas_call | solution.py:141
  2.5 0.4 collective-permute-done.3.refs_2_
  3.0 4.0 %collective-permute-start.7 = (f32[1024,256]{1,0:T(8,128)S(1)}, f32[1024,256]{1,0:T(8,128)S(1)}, u32[]{:S(2)}, u32[]{:S(2)}) collective-permute-start(f32[1024,256]{1,0:T(8,128)S(1)} %stack_rows.3.here), channel_id=1, source_target_pairs={{0,8},{1,12},{2,0},{3,4},{4,9},{5,13},{6,1},{7,5},{8,10},{9,14},{1... | collective-permute-start | bytes 3145736 | tf_op jit(solution)/shard_map/ppermute | solution.py:367
  7.0 0.7 collective-permute-start.6
  7.7 4.2 %collective-permute-start = (f32[256,256]{1,0:T(8,128)}, f32[256,256]{1,0:T(8,128)S(1)}, u32[]{:S(2)}, u32[]{:S(2)}) collective-permute-start(f32[256,256]{1,0:T(8,128)} %refs_0_.1), channel_id=1, source_target_pairs={{0,2},{1,3},{2,0},{3,1},{4,6},{5,7},{6,4},{7,5},{8,10},{9,11},{10,... | collective-permute-start | bytes 786440 | tf_op jit(solution)/shard_map/ppermute | solution.py:356
  12.0 0.8 concatenate.6.at
  12.8 2.2 %copy-done = f32[1024,1024]{1,0:T(8,128)S(1)} copy-done((f32[1024,1024]{1,0:T(8,128)S(1)}, f32[1024,1024]{1,0:T(8,128)}, u32[]{:S(2)}) %copy-start) | copy-done | bytes 4194328
  15.0 2.4 %left_first.1.before = f32[512,1024]{1,0:T(8,128)S(1)} custom-call(s32[50]{0:T(128)S(1)} %concatenate.6.at, f32[1024,1024]{1,0:T(8,128)S(1)} %copy-done, f32[1024,256]{1,0:T(8,128)S(1)} %stack_rows.3.here), custom_call_target="tpu_custom_call" | custom-call | tf_op jit(solution)/shard_map/left_first/pallas_call | solution.py:174
  17.4 20.9 %collective-permute-done.two = f32[256,256]{1,0:T(8,128)S(1)} collective-permute-done((f32[256,256]{1,0:T(8,128)}, f32[256,256]{1,0:T(8,128)S(1)}, u32[]{:S(2)}, u32[]{:S(2)}) %collective-permute-start) | collective-permute-done | bytes 262176 | tf_op jit(solution)/shard_map/ppermute | solution.py:356
  38.4 2.9 %collective-permute-done.1.one = f32[256,256]{1,0:T(8,128)} collective-permute-done((f32[256,256]{1,0:T(8,128)}, f32[256,256]{1,0:T(8,128)}, u32[]{:S(2)}, u32[]{:S(2)}) %collective-permute-start.1) | collective-permute-done | bytes 262176 | tf_op jit(solution)/shard_map/ppermute | solution.py:356
  41.3 1.7 %collective-permute-done.5.core_one = f32[256,256]{1,0:T(8,128)S(1)} collective-permute-done((f32[256,256]{1,0:T(8,128)}, f32[256,256]{1,0:T(8,128)S(1)}, u32[]{:S(2)}, u32[]{:S(2)}) %collective-permute-start.5) | collective-permute-done | bytes 262176 | tf_op jit(solution)/shard_map/ppermute | solution.py:356
  43.0 3.0 %left_last.1 = (bf16[512,1024]{1,0:T(8,128)(2,1)S(1)}, bf16[512,1024]{1,0:T(8,128)(2,1)S(1)}) custom-call(s32[50]{0:T(128)S(1)} %concatenate.6.at, f32[1024,1024]{1,0:T(8,128)S(1)} %copy-done.1, f32[256,256]{1,0:T(8,128)S(1)} %collective-permute-done.two, f32[256,256]{1,0:T(8,128)} %collective-permute-done.1.one, ...), custom_call_target="tpu_custom_call" | custom-call | tf_op jit(solution)/shard_map/left_last/pallas_call | solution.py:174
  46.0 1.5 %first_sums.1 = (f32[768,256]{1,0:T(8,128)S(1)}, bf16[512,512]{1,0:T(8,128)(2,1)S(1)}, bf16[512,512]{1,0:T(8,128)(2,1)S(1)}) custom-call(s32[50]{0:T(128)S(1)} %concatenate.6.at, bf16[512,1024]{1,0:T(8,128)(2,1)S(1)} %get-tuple-element.27.left_high, bf16[512,1024]{1,0:T(8,128)(2,1)S(1)} %get-tuple-element.28.left_low, ...), custom_call_target="tpu_custom_call" | custom-call | flops 603979776 | tf_op jit(solution)/shard_map/first_sums/pallas_call | solution.py:174
  47.5 1.5 %last_sums.1 = (f32[384,256]{1,0:T(8,128)S(1)}, f32[384,256]{1,0:T(8,128)S(1)}, bf16[512,512]{1,0:T(8,128)(2,1)S(1)}, bf16[512,512]{1,0:T(8,128)(2,1)S(1)}) custom-call(s32[50]{0:T(128)S(1)} %concatenate.6.at, bf16[512,1024]{1,0:T(8,128)(2,1)S(1)} %get-tuple-element.27.left_high, bf16[512,1024]{1,0:T(8,128)(2,1)S(1)} %get-tuple-element.28.left_low, ...), custom_call_target="tpu_custom_call" | custom-call | flops 603979776 | tf_op jit(solution)/shard_map/last_sums/pallas_call | solution.py:174
  49.2 1.6 %collective-permute-done.8 = f32[384,256]{1,0:T(8,128)S(1)} collective-permute-done((f32[384,256]{1,0:T(8,128)S(1)}, f32[384,256]{1,0:T(8,128)S(1)}, u32[]{:S(2)}, u32[]{:S(2)}) %collective-permute-start.8) | collective-permute-done | bytes 393248 | tf_op jit(solution)/shard_map/ppermute | solution.py:356
  50.9 2.3 %band_product.2 = f32[2,256,512]{2,1,0:T(8,128)S(1)} custom-call(s32[50]{0:T(128)S(1)} %concatenate.6.at, f32[1024,1024]{1,0:T(8,128)S(1)} %copy-done.1, bf16[512,512]{1,0:T(8,128)(2,1)S(1)} %get-tuple-element.33.refs_0_, bf16[512,512]{1,0:T(8,128)(2,1)S(1)} %get-tuple-element.34.refs_1_, bf16[512,512]{1,0:T(8,128)(2,1)S(1)} %get-tuple-element.35.refs_2_, ...), custom_call_target="tpu_custom_call" | custom-call | flops 1610612736 | bytes 2097152 | tf_op jit(solution)/shard_map/band_product/pallas_call | solution.py:174
  53.5 7.4 %collective-permute-start.10 = (f32[96,256]{1,0:T(8,128)S(1)}, f32[96,256]{1,0:T(8,128)S(1)}, u32[]{:S(2)}, u32[]{:S(2)}) collective-permute-start(f32[96,256]{1,0:T(8,128)S(1)} %get-tuple-element.47), channel_id=1, source_target_pairs={{0,4},{4,0},{8,12},{12,8},{1,5},{5,1},{9,13},{13,9},{2,6},{6,2},{1... | collective-permute-start | bytes 294920 | tf_op jit(solution)/shard_map/ppermute | solution.py:356
  60.8 4.1 %collective-permute-start.11 = (f32[96,256]{1,0:T(8,128)S(1)}, f32[96,256]{1,0:T(8,128)S(1)}, u32[]{:S(2)}, u32[]{:S(2)}) collective-permute-start(f32[96,256]{1,0:T(8,128)S(1)} %get-tuple-element.46), channel_id=1, source_target_pairs={{0,2},{1,3},{2,0},{3,1},{4,6},{5,7},{6,4},{7,5},{8,10},{9,11},{10,... | collective-permute-start | bytes 294920 | tf_op jit(solution)/shard_map/ppermute | solution.py:356
  64.9 0.6 collective-permute-start.12
  65.5 2.3 %band_product.3.keep = f32[2,256,512]{2,1,0:T(8,128)S(1)} custom-call(s32[50]{0:T(128)S(1)} %concatenate.6.at, f32[1024,1024]{1,0:T(8,128)S(1)} %copy-done.1, bf16[512,512]{1,0:T(8,128)(2,1)S(1)} %get-tuple-element.33.refs_0_, bf16[512,512]{1,0:T(8,128)(2,1)S(1)} %get-tuple-element.34.refs_1_, bf16[512,512]{1,0:T(8,128)(2,1)S(1)} %get-tuple-element.35.refs_2_, ...), custom_call_target="tpu_custom_call" | custom-call | flops 1610612736 | bytes 2097152 | tf_op jit(solution)/shard_map/band_product/pallas_call | solution.py:174
  67.9 1.5 %collective-permute-done.11 = f32[96,256]{1,0:T(8,128)S(1)} collective-permute-done((f32[96,256]{1,0:T(8,128)S(1)}, f32[96,256]{1,0:T(8,128)S(1)}, u32[]{:S(2)}, u32[]{:S(2)}) %collective-permute-start.11) | collective-permute-done | bytes 98336 | tf_op jit(solution)/shard_map/ppermute | solution.py:356
  69.3 1.3 %collective-permute-done.12 = f32[96,256]{1,0:T(8,128)S(1)} collective-permute-done((f32[96,256]{1,0:T(8,128)S(1)}, f32[96,256]{1,0:T(8,128)S(1)}, u32[]{:S(2)}, u32[]{:S(2)}) %collective-permute-start.12) | collective-permute-done | bytes 98336 | tf_op jit(solution)/shard_map/ppermute | solution.py:363
  70.8 1.3 %collective-permute-start.13 = (f32[256,512]{1,0:T(8,128)S(1)}, f32[256,512]{1,0:T(8,128)S(1)}, u32[]{:S(2)}, u32[]{:S(2)}) collective-permute-start(f32[256,512]{1,0:T(8,128)S(1)} %fusion), channel_id=1, source_target_pairs={{0,2},{1,3},{2,0},{3,1},{4,6},{5,7},{6,4},{7,5},{8,10},{9,11},{10,... | collective-permute-start | bytes 1572872 | tf_op jit(solution)/shard_map/ppermute | solution.py:356
  72.0 2.0 %collective-permute-start.14 = (f32[96,256]{1,0:T(8,128)S(1)}, f32[96,256]{1,0:T(8,128)S(1)}, u32[]{:S(2)}, u32[]{:S(2)}) collective-permute-start(f32[96,256]{1,0:T(8,128)S(1)} %fusion.1), channel_id=1, source_target_pairs={{0,8},{4,12},{8,0},{12,4},{1,9},{5,13},{9,1},{13,5},{2,10},{6,14},... | collective-permute-start | bytes 294920 | tf_op jit(solution)/shard_map/ppermute | solution.py:356
  74.0 4.7 %collective-permute-done.14 = f32[96,256]{1,0:T(8,128)S(1)} collective-permute-done((f32[96,256]{1,0:T(8,128)S(1)}, f32[96,256]{1,0:T(8,128)S(1)}, u32[]{:S(2)}, u32[]{:S(2)}) %collective-permute-start.14) | collective-permute-done | bytes 98336 | tf_op jit(solution)/shard_map/ppermute | solution.py:356
  78.8 0.8 collective-permute-start.16
  79.7 2.6 %collective-permute-start.17 = (f32[96,256]{1,0:T(8,128)S(1)}, f32[96,256]{1,0:T(8,128)S(1)}, u32[]{:S(2)}, u32[]{:S(2)}) collective-permute-start(f32[96,256]{1,0:T(8,128)S(1)} %add.27), channel_id=1, source_target_pairs={{0,6},{1,7},{2,4},{3,5},{4,2},{5,3},{6,0},{7,1},{8,14},{9,15},{10,... | collective-permute-start | bytes 294920 | tf_op jit(solution)/shard_map/ppermute | solution.py:363
  82.3 4.8 %collective-permute-done.13.other = f32[256,512]{1,0:T(8,128)S(1)} collective-permute-done((f32[256,512]{1,0:T(8,128)S(1)}, f32[256,512]{1,0:T(8,128)S(1)}, u32[]{:S(2)}, u32[]{:S(2)}) %collective-permute-start.13) | collective-permute-done | bytes 524320 | tf_op jit(solution)/shard_map/ppermute | solution.py:356
  87.1 1.0 %collective-permute-done.16 = f32[96,256]{1,0:T(8,128)S(1)} collective-permute-done((f32[96,256]{1,0:T(8,128)S(1)}, f32[96,256]{1,0:T(8,128)S(1)}, u32[]{:S(2)}, u32[]{:S(2)}) %collective-permute-start.16) | collective-permute-done | bytes 98336 | tf_op jit(solution)/shard_map/ppermute | solution.py:356
  88.2 1.5 %column_rows.1 = (f32[256,256]{1,0:T(8,128)}, f32[256,256]{1,0:T(8,128)}) custom-call(s32[50]{0:T(128)S(1)} %concatenate.6.at, f32[2,256,512]{2,1,0:T(8,128)S(1)} %band_product.3.keep, f32[2,256,512]{2,1,0:T(8,128)S(1)} %collective-permute-done.9.got, f32[256,512]{1,0:T(8,128)S(1)} %collective-permute-done.13.other, f32[256,256]{1,0:T(8,128)S(1)} %copy-done.2), custom_call_target="tpu_custom_call" | custom-call | tf_op jit(solution)/shard_map/column_rows/pallas_call | solution.py:299
  89.9 1.9 %small_blocks.1 = (f32[256,256]{1,0:T(8,128)}, f32[256,256]{1,0:T(8,128)}, f32[256,256]{1,0:T(8,128)}) custom-call(s32[50]{0:T(128)S(1)} %concatenate.6.at, f32[256,256]{1,0:T(8,128)S(1)} %copy-done.2, f32[256,256]{1,0:T(8,128)S(1)} %copy-done.3, f32[256,256]{1,0:T(8,128)S(1)} %copy-done.4, f32[384,256]{1,0:T(8,128)S(1)} %constant_dynamic-update-slice_fusion.first, ...), custom_call_target="tpu_custom_call" | custom-call | tf_op jit(solution)/shard_map/small_blocks/pallas_call | solution.py:332
  (36 shorter events, 1.5 us)
Async XLA Ops:
  0.6 1.9 %collective-permute-start.2 = (f32[256,256]{1,0:T(8,128)}, f32[256,256]{1,0:T(8,128)S(1)}, u32[]{:S(2)}, u32[]{:S(2)}) collective-permute-start(f32[256,256]{1,0:T(8,128)} %refs_0_.1), channel_id=1, source_target_pairs={{0,1},{1,0},{2,3},{3,2},{4,5},{5,4},{6,7},{7,6},{8,9},{9,8},{10,11... | collective-permute-start | bytes 786440 | tf_op jit(solution)/shard_map/ppermute | solution.py:356
  1.1 1.7 %collective-permute-start.3 = (f32[256,256]{1,0:T(8,128)}, f32[256,256]{1,0:T(8,128)S(1)}, u32[]{:S(2)}, u32[]{:S(2)}) collective-permute-start(f32[256,256]{1,0:T(8,128)} %refs_1_.1), channel_id=1, source_target_pairs={{0,1},{1,0},{2,3},{3,2},{4,5},{5,4},{6,7},{7,6},{8,9},{9,8},{10,11... | collective-permute-start | bytes 786440 | tf_op jit(solution)/shard_map/ppermute | solution.py:356
  3.0 43.0 %collective-permute-start.7 = (f32[1024,256]{1,0:T(8,128)S(1)}, f32[1024,256]{1,0:T(8,128)S(1)}, u32[]{:S(2)}, u32[]{:S(2)}) collective-permute-start(f32[1024,256]{1,0:T(8,128)S(1)} %stack_rows.3.here), channel_id=1, source_target_pairs={{0,8},{1,12},{2,0},{3,4},{4,9},{5,13},{6,1},{7,5},{8,10},{9,14},{1... | collective-permute-start | bytes 3145736 | tf_op jit(solution)/shard_map/ppermute | solution.py:367
  7.0 40.5 %collective-permute-start.6 = (f32[1024,256]{1,0:T(8,128)S(1)}, f32[1024,256]{1,0:T(8,128)S(1)}, u32[]{:S(2)}, u32[]{:S(2)}) collective-permute-start(f32[1024,256]{1,0:T(8,128)S(1)} %stack_rows.3.here), channel_id=1, source_target_pairs={{0,0},{1,4},{2,8},{3,12},{4,1},{5,5},{6,9},{7,13},{8,2},{9,6},{10,... | collective-permute-start | bytes 3145736 | tf_op jit(solution)/shard_map/ppermute | solution.py:367
  7.7 30.6 %collective-permute-start = (f32[256,256]{1,0:T(8,128)}, f32[256,256]{1,0:T(8,128)S(1)}, u32[]{:S(2)}, u32[]{:S(2)}) collective-permute-start(f32[256,256]{1,0:T(8,128)} %refs_0_.1), channel_id=1, source_target_pairs={{0,2},{1,3},{2,0},{3,1},{4,6},{5,7},{6,4},{7,5},{8,10},{9,11},{10,... | collective-permute-start | bytes 786440 | tf_op jit(solution)/shard_map/ppermute | solution.py:356
  11.9 29.3 %collective-permute-start.1 = (f32[256,256]{1,0:T(8,128)}, f32[256,256]{1,0:T(8,128)}, u32[]{:S(2)}, u32[]{:S(2)}) collective-permute-start(f32[256,256]{1,0:T(8,128)} %refs_1_.1), channel_id=1, source_target_pairs={{0,2},{1,3},{2,0},{3,1},{4,6},{5,7},{6,4},{7,5},{8,10},{9,11},{10,... | collective-permute-start | bytes 786440 | tf_op jit(solution)/shard_map/ppermute | solution.py:356
  12.8 2.2 %copy-start = (f32[1024,1024]{1,0:T(8,128)S(1)}, f32[1024,1024]{1,0:T(8,128)}, u32[]{:S(2)}) copy-start(f32[1024,1024]{1,0:T(8,128)} %known.7) | copy-start | bytes 12582916
  15.0 28.0 %copy-start.1 = (f32[1024,1024]{1,0:T(8,128)S(1)}, f32[1024,1024]{1,0:T(8,128)}, u32[]{:S(2)}) copy-start(f32[1024,1024]{1,0:T(8,128)} %known.7) | copy-start | bytes 12582916
  38.4 2.9 %collective-permute-start.4 = (f32[256,256]{1,0:T(8,128)S(1)}, f32[256,256]{1,0:T(8,128)S(1)}, u32[]{:S(2)}, u32[]{:S(2)}) collective-permute-start(f32[256,256]{1,0:T(8,128)S(1)} %collective-permute-done.two), channel_id=1, source_target_pairs={{0,1},{1,0},{2,3},{3,2},{4,5},{5,4},{6,7},{7,6},{8,9},{9,8},{10,11... | collective-permute-start | bytes 786440 | tf_op jit(solution)/shard_map/ppermute | solution.py:356
  41.3 1.7 %collective-permute-start.5 = (f32[256,256]{1,0:T(8,128)}, f32[256,256]{1,0:T(8,128)S(1)}, u32[]{:S(2)}, u32[]{:S(2)}) collective-permute-start(f32[256,256]{1,0:T(8,128)} %collective-permute-done.1.one), channel_id=1, source_target_pairs={{0,1},{1,0},{2,3},{3,2},{4,5},{5,4},{6,7},{7,6},{8,9},{9,8},{10,11... | collective-permute-start | bytes 786440 | tf_op jit(solution)/shard_map/ppermute | solution.py:356
  49.0 1.8 %collective-permute-start.8 = (f32[384,256]{1,0:T(8,128)S(1)}, f32[384,256]{1,0:T(8,128)S(1)}, u32[]{:S(2)}, u32[]{:S(2)}) collective-permute-start(f32[384,256]{1,0:T(8,128)S(1)} %get-tuple-element.31), channel_id=1, source_target_pairs={{0,1},{1,0},{2,3},{3,2},{4,5},{5,4},{6,7},{7,6},{8,9},{9,8},{10,11... | collective-permute-start | bytes 1179656 | tf_op jit(solution)/shard_map/ppermute | solution.py:356
  53.2 17.4 %collective-permute-start.9 = (f32[2,256,512]{2,1,0:T(8,128)S(1)}, f32[2,256,512]{2,1,0:T(8,128)S(1)}, u32[]{:S(2)}, u32[]{:S(2)}) collective-permute-start(f32[2,256,512]{2,1,0:T(8,128)S(1)} %band_product.2), channel_id=1, source_target_pairs={{0,1},{1,0},{2,3},{3,2},{4,5},{5,4},{6,7},{7,6},{8,9},{9,8},{10,11... | collective-permute-start | bytes 3145736 | tf_op jit(solution)/shard_map/ppermute | solution.py:356
  53.5 14.4 %collective-permute-start.10 = (f32[96,256]{1,0:T(8,128)S(1)}, f32[96,256]{1,0:T(8,128)S(1)}, u32[]{:S(2)}, u32[]{:S(2)}) collective-permute-start(f32[96,256]{1,0:T(8,128)S(1)} %get-tuple-element.47), channel_id=1, source_target_pairs={{0,4},{4,0},{8,12},{12,8},{1,5},{5,1},{9,13},{13,9},{2,6},{6,2},{1... | collective-permute-start | bytes 294920 | tf_op jit(solution)/shard_map/ppermute | solution.py:356
  60.8 8.5 %collective-permute-start.11 = (f32[96,256]{1,0:T(8,128)S(1)}, f32[96,256]{1,0:T(8,128)S(1)}, u32[]{:S(2)}, u32[]{:S(2)}) collective-permute-start(f32[96,256]{1,0:T(8,128)S(1)} %get-tuple-element.46), channel_id=1, source_target_pairs={{0,2},{1,3},{2,0},{3,1},{4,6},{5,7},{6,4},{7,5},{8,10},{9,11},{10,... | collective-permute-start | bytes 294920 | tf_op jit(solution)/shard_map/ppermute | solution.py:356
  64.9 23.3 %copy-start.2 = (f32[256,256]{1,0:T(8,128)S(1)}, f32[256,256]{1,0:T(8,128)}, u32[]{:S(2)}) copy-start(f32[256,256]{1,0:T(8,128)} %top.3) | copy-start | bytes 786436
  64.9 5.7 %collective-permute-start.12 = (f32[96,256]{1,0:T(8,128)S(1)}, f32[96,256]{1,0:T(8,128)S(1)}, u32[]{:S(2)}, u32[]{:S(2)}) collective-permute-start(f32[96,256]{1,0:T(8,128)S(1)} %get-tuple-element.45), channel_id=1, source_target_pairs={{0,6},{1,7},{2,4},{3,5},{4,2},{5,3},{6,0},{7,1},{8,14},{9,15},{10,... | collective-permute-start | bytes 294920 | tf_op jit(solution)/shard_map/ppermute | solution.py:363
  67.8 22.1 %copy-start.3 = (f32[256,256]{1,0:T(8,128)S(1)}, f32[256,256]{1,0:T(8,128)}, u32[]{:S(2)}) copy-start(f32[256,256]{1,0:T(8,128)} %inner_two.1) | copy-start | bytes 786436
  67.8 22.1 %copy-start.4 = (f32[256,256]{1,0:T(8,128)S(1)}, f32[256,256]{1,0:T(8,128)}, u32[]{:S(2)}) copy-start(f32[256,256]{1,0:T(8,128)} %inner_one.1) | copy-start | bytes 786436
  70.8 16.3 %collective-permute-start.13 = (f32[256,512]{1,0:T(8,128)S(1)}, f32[256,512]{1,0:T(8,128)S(1)}, u32[]{:S(2)}, u32[]{:S(2)}) collective-permute-start(f32[256,512]{1,0:T(8,128)S(1)} %fusion), channel_id=1, source_target_pairs={{0,2},{1,3},{2,0},{3,1},{4,6},{5,7},{6,4},{7,5},{8,10},{9,11},{10,... | collective-permute-start | bytes 1572872 | tf_op jit(solution)/shard_map/ppermute | solution.py:356
  72.0 6.7 %collective-permute-start.14 = (f32[96,256]{1,0:T(8,128)S(1)}, f32[96,256]{1,0:T(8,128)S(1)}, u32[]{:S(2)}, u32[]{:S(2)}) collective-permute-start(f32[96,256]{1,0:T(8,128)S(1)} %fusion.1), channel_id=1, source_target_pairs={{0,8},{4,12},{8,0},{12,4},{1,9},{5,13},{9,1},{13,5},{2,10},{6,14},... | collective-permute-start | bytes 294920 | tf_op jit(solution)/shard_map/ppermute | solution.py:356
  78.7 8.3 %collective-permute-start.15 = (f32[96,256]{1,0:T(8,128)S(1)}, f32[96,256]{1,0:T(8,128)S(1)}, u32[]{:S(2)}, u32[]{:S(2)}) collective-permute-start(f32[96,256]{1,0:T(8,128)S(1)} %add.27), channel_id=1, source_target_pairs={{0,4},{4,0},{8,12},{12,8},{1,5},{5,1},{9,13},{13,9},{2,6},{6,2},{1... | collective-permute-start | bytes 294920 | tf_op jit(solution)/shard_map/ppermute | solution.py:356
  78.8 9.2 %collective-permute-start.16 = (f32[96,256]{1,0:T(8,128)S(1)}, f32[96,256]{1,0:T(8,128)S(1)}, u32[]{:S(2)}, u32[]{:S(2)}) collective-permute-start(f32[96,256]{1,0:T(8,128)S(1)} %add.27), channel_id=1, source_target_pairs={{0,2},{1,3},{2,0},{3,1},{4,6},{5,7},{6,4},{7,5},{8,10},{9,11},{10,... | collective-permute-start | bytes 294920 | tf_op jit(solution)/shard_map/ppermute | solution.py:356
  79.7 8.4 %collective-permute-start.17 = (f32[96,256]{1,0:T(8,128)S(1)}, f32[96,256]{1,0:T(8,128)S(1)}, u32[]{:S(2)}, u32[]{:S(2)}) collective-permute-start(f32[96,256]{1,0:T(8,128)S(1)} %add.27), channel_id=1, source_target_pairs={{0,6},{1,7},{2,4},{3,5},{4,2},{5,3},{6,0},{7,1},{8,14},{9,15},{10,... | collective-permute-start | bytes 294920 | tf_op jit(solution)/shard_map/ppermute | solution.py:363
  88.1 1.8 %collective-permute-start.18 = (f32[384,256]{1,0:T(8,128)S(1)}, f32[384,256]{1,0:T(8,128)S(1)}, u32[]{:S(2)}, u32[]{:S(2)}) collective-permute-start(f32[384,256]{1,0:T(8,128)S(1)} %constant_dynamic-update-slice_fusion.first), channel_id=1, source_target_pairs={{0,1},{1,0},{2,3},{3,2},{4,5},{5,4},{6,7},{7,6},{8,9},{9,8},{10,11... | collective-permute-start | bytes 1179656 | tf_op jit(solution)/shard_map/ppermute | solution.py:356

commit v7 on v6

--- a/solution.py
+++ b/solution.py
@@ -239,26 +239,29 @@
                 (send if e & 1 else keep)[start : start + width // 8] = part
 
 
-def small_sums(n, at, left, arrived):
-    width = arrived[0].shape[-1]
+def first_sums(n, at, left, arrived):
+    width = arrived.shape[-1]
     part = jax.ShapeDtypeStruct((2 * width, 2 * width), BF16)
     whole = jax.ShapeDtypeStruct((3 * width, width), F32)
+    return call(
+        functools.partial(sums_kernel, n, FIRST_ARRIVAL), "first_sums", 8,
+        cost(36 * width * width * width, 0), (whole, part, part), at, *left, arrived,
+    )
+
+
+def last_sums(n, at, left, arrived, total):
+    width = arrived.shape[-1]
+    part = jax.ShapeDtypeStruct((2 * width, 2 * width), BF16)
     half = jax.ShapeDtypeStruct((3 * width // 2, width), F32)
-    estimate = cost(18 * 2 * width * width * width, 0)
-    total, *first = call(
-        functools.partial(sums_kernel, n, FIRST_ARRIVAL), "first_sums", 8, estimate,
-        (whole, part, part), at, *left, arrived[FIRST_ARRIVAL],
-    )
-    keep, send, *last = call(
-        functools.partial(sums_kernel, n, 1 - FIRST_ARRIVAL), "last_sums", 8, estimate,
-        (half, half, part, part), at, *left, arrived[1 - FIRST_ARRIVAL], total,
+    return call(
+        functools.partial(sums_kernel, n, 1 - FIRST_ARRIVAL), "last_sums", 8,
+        cost(36 * width * width * width, 0), (half, half, part, part), at, *left, arrived, total,
         scratch=[pltpu.VMEM((3 * width, width), F32)],
     )
-    return keep, send, (*first, *last) if FIRST_ARRIVAL == 0 else (*last, *first)
-
-
-def band_kernel(n, first, at, known, *refs):
-    right, out = refs[:4], refs[4]
+
+
+def band_kernel(n, first, arrivals, at, known, *refs):
+    right, before, out = refs[: 2 * len(arrivals)], refs[2 * len(arrivals) : -1], refs[-1]
     row, col = at[0], at[1]
     width = right[0].shape[0] // 2
     for i in range(n // 2):
@@ -266,21 +269,22 @@
         terms = [
             dot3(
                 halves(known[tile, arrived_columns(row, m, width)]),
-                (right[2 * m][...], right[2 * m + 1][...]),
+                (right[2 * k][...], right[2 * k + 1][...]),
                 ROWS_BY_COLUMNS,
             )
-            for m in range(2)
+            for k, m in enumerate(arrivals)
         ]
-        out[i] = terms[0] + terms[1]
-
-
-def band_product(n, first, at, known, right):
+        out[i] = functools.reduce(jnp.add, [ref[i] for ref in before] + terms)
+
+
+def band_product(n, first, arrivals, at, known, right, *before):
     rows, span = known.shape
     width = rows // n
+    right = [half for m in arrivals for half in right[2 * m : 2 * m + 2]]
     return call(
-        functools.partial(band_kernel, n, first), "band_product", 14,
-        cost(6 * rows * span * width, 2 * rows * span),
-        jax.ShapeDtypeStruct((n // 2, width, 2 * width), F32), at, known, *right,
+        functools.partial(band_kernel, n, first, arrivals), "band_product", 14,
+        cost(3 * len(arrivals) * rows * span * width, len(arrivals) * rows * span),
+        jax.ShapeDtypeStruct((n // 2, width, 2 * width), F32), at, known, *right, *before,
     )
 
 
@@ -373,13 +377,21 @@
     there += [core(after(rows, first)) for rows in there]
     left = left_last(n, at, known, there, first)
 
-    keep_sums, send_sums, right = small_sums(n, at, left, gathered)
+    total, *early = first_sums(n, at, left, gathered[FIRST_ARRIVAL])
+    early = {FIRST_ARRIVAL: early}
+    partial = [
+        band_product(n, 1, (FIRST_ARRIVAL,), at, known, (*early[FIRST_ARRIVAL],) * 2)
+    ]
+    keep_sums, send_sums, *late = last_sums(
+        n, after(at, *partial), left, gathered[1 - FIRST_ARRIVAL], total
+    )
+    right = [half for m in range(2) for half in early.get(m, late)]
     mine = keep_sums + core(send_sums)
-    send = band_product(n, 1, after(at, mine), known, right)
-    keep = band_product(n, 0, after(at, send), known, right)
+    send = band_product(n, 1, (1 - FIRST_ARRIVAL,), after(at, send_sums), known, right, *partial[:1])
+    keep = band_product(n, 0, (0, 1), after(at, send), known, right)
+    got = core(after(send, mine))
     own, beyond, beside, corner = jnp.split(mine, 4)
     mine = (own + along("prow", 1, beyond)) + (across(beside) + opposite(corner))
-    got = core(send)
     other = across(after(keep[1] + got[1], mine))
     mine = mine + along("prow", 2, mine)
     column_two, column_one = columns(n, at, keep, got, other, top_one)

time: 92 us -> 89.9 us (0.977)
  waiting for transfers between devices: 41.2 us -> 39.3 us
    ppermute x15, starting transfers between devices: 21 us -> 13.4 us  [along(): return lax.ppermute(array, axis, [(i, i ^ k) for i in range(n)])]
    ppermute x2, starting transfers between devices: 3.15 us -> 9.81 us  [opposite(): return lax.ppermute(rows, ('prow', 'pcol'), pairs)]
    ppermute x2, waiting for transfers between devices: 1.29 us -> 0.01 us  [opposite(): return lax.ppermute(rows, ('prow', 'pcol'), pairs)]
    pallas_call x6 -> x7, Pallas kernels: 13.1 us -> 13.8 us  [call(): pl.pallas_call(kernel, out_shape=out_shape, in_specs=[SMEM] + [VMEM] * (l...]
  transfers between devices with their start and end apart: 19 -> 19, of which waited for: 12 -> 11; matrix products, arithmetic and copies ran while one was open for 1% -> 1% of each run, Pallas kernels for 13% -> 17%
where the time goes in v7:
time: 89.9 us; the launch traced here: 89.7 us
  waiting for transfers between devices  39.3 us (44%)
  starting transfers between devices  28 us (31%)
  Pallas kernels  18.4 us (20%)
  local copies, waits for them, and re-layouts  3.03 us (3%)
    ppermute x15, waiting for transfers between devices, along(): return lax.ppermute(array, axis, [(i, i ^ k) for i in range(n)])  39.3 us
    pallas_call x7, Pallas kernels, call(): pl.pallas_call(kernel, out_shape=out_shape, in_specs=[SMEM] + [VMEM] * (l...  13.8 us
    ppermute x15, starting transfers between devices, along(): return lax.ppermute(array, axis, [(i, i ^ k) for i in range(n)])  13.4 us
    ppermute x2, starting transfers between devices, opposite(): return lax.ppermute(rows, ('prow', 'pcol'), pairs)  9.81 us
    ppermute x2, starting transfers between devices, direct(): return lax.ppermute(rows, ('prow', 'pcol'), pairs)  4.73 us
    unnamed x13, local copies, waits for them, and re-layouts  2.23 us
    pallas_call x1, Pallas kernels, small_blocks(): pl.pallas_call(functools.partial(blocks_kernel, n), out_shape=(shape, sha...  1.9 us
  transfers between devices with their start and end apart: 19, of which 11 were waited for; matrix products, arithmetic and copies ran while one was open for 1% of the time, Pallas kernels for 17%

profile of v7, /device:TPU:0, one launch (start us, length us, event | category | flops | bytes accessed | tf_op | source)
XLA Modules:
  0.0 89.7 jit_solution(17606261152890314568)
XLA Ops:
  0.6 0.5 collective-permute-start.2
  1.2 1.0 %stack_rows.2.refs_0_ = f32[512,256]{1,0:T(8,128)S(1)} custom-call(f32[256,256]{1,0:T(8,128)} %refs_0_.1, f32[256,256]{1,0:T(8,128)} %refs_1_.1), custom_call_target="tpu_custom_call" | custom-call | bytes 1048576 | tf_op jit(solution)/shard_map/stack_rows/pallas_call | solution.py:141
  3.0 4.0 %collective-permute-start.6 = (f32[1024,256]{1,0:T(8,128)S(1)}, f32[1024,256]{1,0:T(8,128)S(1)}, u32[]{:S(2)}, u32[]{:S(2)}) collective-permute-start(f32[1024,256]{1,0:T(8,128)S(1)} %stack_rows.3.here), channel_id=1, source_target_pairs={{0,8},{1,12},{2,0},{3,4},{4,9},{5,13},{6,1},{7,5},{8,10},{9,14},{1... | collective-permute-start | bytes 3145736 | tf_op jit(solution)/shard_map/ppermute | solution.py:371
  7.0 0.7 collective-permute-start.7
  7.7 4.2 %collective-permute-start.1 = (f32[256,256]{1,0:T(8,128)}, f32[256,256]{1,0:T(8,128)S(1)}, u32[]{:S(2)}, u32[]{:S(2)}) collective-permute-start(f32[256,256]{1,0:T(8,128)} %refs_1_.1), channel_id=1, source_target_pairs={{0,2},{1,3},{2,0},{3,1},{4,6},{5,7},{6,4},{7,5},{8,10},{9,11},{10,... | collective-permute-start | bytes 786440 | tf_op jit(solution)/shard_map/ppermute | solution.py:360
  12.0 0.8 concatenate.6.at
  12.8 2.2 %copy-done = f32[1024,1024]{1,0:T(8,128)S(1)} copy-done((f32[1024,1024]{1,0:T(8,128)S(1)}, f32[1024,1024]{1,0:T(8,128)}, u32[]{:S(2)}) %copy-start) | copy-done | bytes 4194328
  15.0 2.4 %left_first.1.before = f32[512,1024]{1,0:T(8,128)S(1)} custom-call(s32[50]{0:T(128)S(1)} %concatenate.6.at, f32[1024,1024]{1,0:T(8,128)S(1)} %copy-done, f32[1024,256]{1,0:T(8,128)S(1)} %stack_rows.3.here), custom_call_target="tpu_custom_call" | custom-call | tf_op jit(solution)/shard_map/left_first/pallas_call | solution.py:174
  17.4 20.9 %collective-permute-done.1.one = f32[256,256]{1,0:T(8,128)S(1)} collective-permute-done((f32[256,256]{1,0:T(8,128)}, f32[256,256]{1,0:T(8,128)S(1)}, u32[]{:S(2)}, u32[]{:S(2)}) %collective-permute-start.1) | collective-permute-done | bytes 262176 | tf_op jit(solution)/shard_map/ppermute | solution.py:360
  38.4 2.9 %collective-permute-done.two = f32[256,256]{1,0:T(8,128)} collective-permute-done((f32[256,256]{1,0:T(8,128)}, f32[256,256]{1,0:T(8,128)}, u32[]{:S(2)}, u32[]{:S(2)}) %collective-permute-start) | collective-permute-done | bytes 262176 | tf_op jit(solution)/shard_map/ppermute | solution.py:360
  41.3 0.5 collective-permute-start.5
  41.8 1.6 %collective-permute-done.4.core_two = f32[256,256]{1,0:T(8,128)S(1)} collective-permute-done((f32[256,256]{1,0:T(8,128)}, f32[256,256]{1,0:T(8,128)S(1)}, u32[]{:S(2)}, u32[]{:S(2)}) %collective-permute-start.4) | collective-permute-done | bytes 262176 | tf_op jit(solution)/shard_map/ppermute | solution.py:360
  43.4 2.9 %left_last.1 = (bf16[512,1024]{1,0:T(8,128)(2,1)S(1)}, bf16[512,1024]{1,0:T(8,128)(2,1)S(1)}) custom-call(s32[50]{0:T(128)S(1)} %concatenate.6.at, f32[1024,1024]{1,0:T(8,128)S(1)} %copy-done.1, f32[256,256]{1,0:T(8,128)} %collective-permute-done.two, f32[256,256]{1,0:T(8,128)S(1)} %collective-permute-done.1.one, ...), custom_call_target="tpu_custom_call" | custom-call | tf_op jit(solution)/shard_map/left_last/pallas_call | solution.py:174
  46.3 1.5 %first_sums.1 = (f32[768,256]{1,0:T(8,128)S(1)}, bf16[512,512]{1,0:T(8,128)(2,1)S(1)}, bf16[512,512]{1,0:T(8,128)(2,1)S(1)}) custom-call(s32[50]{0:T(128)S(1)} %concatenate.6.at, bf16[512,1024]{1,0:T(8,128)(2,1)S(1)} %get-tuple-element.29.left_high, bf16[512,1024]{1,0:T(8,128)(2,1)S(1)} %get-tuple-element.30.left_low, ...), custom_call_target="tpu_custom_call" | custom-call | flops 603979776 | tf_op jit(solution)/shard_map/first_sums/pallas_call | solution.py:174
  47.8 1.5 %band_product.3.refs_2_ = f32[2,256,512]{2,1,0:T(8,128)S(1)} custom-call(s32[50]{0:T(128)S(1)} %concatenate.6.at, f32[1024,1024]{1,0:T(8,128)S(1)} %copy-done.1, bf16[512,512]{1,0:T(8,128)(2,1)S(1)} %get-tuple-element.31.refs_0_.refs_2_, bf16[512,512]{1,0:T(8,128)(2,1)S(1)} %get-tuple-element.32.refs_1_.refs_3_), custom_call_target="tpu_custom_call" | custom-call | flops 805306368 | bytes 1048576 | tf_op jit(solution)/shard_map/band_product/pallas_call | solution.py:174
  49.3 1.5 %last_sums.1 = (f32[384,256]{1,0:T(8,128)S(1)}, f32[384,256]{1,0:T(8,128)S(1)}, bf16[512,512]{1,0:T(8,128)(2,1)S(1)}, bf16[512,512]{1,0:T(8,128)(2,1)S(1)}) custom-call(s32[50]{0:T(128)S(1)} %concatenate.6.at, bf16[512,1024]{1,0:T(8,128)(2,1)S(1)} %get-tuple-element.29.left_high, bf16[512,1024]{1,0:T(8,128)(2,1)S(1)} %get-tuple-element.30.left_low, ...), custom_call_target="tpu_custom_call" | custom-call | flops 603979776 | tf_op jit(solution)/shard_map/last_sums/pallas_call | solution.py:174
  51.1 1.5 %band_product.4 = f32[2,256,512]{2,1,0:T(8,128)S(1)} custom-call(s32[50]{0:T(128)S(1)} %concatenate.6.at, f32[1024,1024]{1,0:T(8,128)S(1)} %copy-done.1, bf16[512,512]{1,0:T(8,128)(2,1)S(1)} %get-tuple-element.37.refs_0_, bf16[512,512]{1,0:T(8,128)(2,1)S(1)} %get-tuple-element.38.refs_1_, f32[2,256,512]{2,1,0:T(8,128)S(1)} %band_product.3.refs_2_), custom_call_target="tpu_custom_call" | custom-call | flops 805306368 | bytes 1048576 | tf_op jit(solution)/shard_map/band_product/pallas_call | solution.py:174
  53.2 9.1 %collective-permute-start.12 = (f32[96,256]{1,0:T(8,128)S(1)}, f32[96,256]{1,0:T(8,128)S(1)}, u32[]{:S(2)}, u32[]{:S(2)}) collective-permute-start(f32[96,256]{1,0:T(8,128)S(1)} %get-tuple-element.49), channel_id=1, source_target_pairs={{0,6},{1,7},{2,4},{3,5},{4,2},{5,3},{6,0},{7,1},{8,14},{9,15},{10,... | collective-permute-start | bytes 294920 | tf_op jit(solution)/shard_map/ppermute | solution.py:367
  62.2 1.1 %collective-permute-start.10 = (f32[96,256]{1,0:T(8,128)S(1)}, f32[96,256]{1,0:T(8,128)S(1)}, u32[]{:S(2)}, u32[]{:S(2)}) collective-permute-start(f32[96,256]{1,0:T(8,128)S(1)} %get-tuple-element.51), channel_id=1, source_target_pairs={{0,4},{4,0},{8,12},{12,8},{1,5},{5,1},{9,13},{13,9},{2,6},{6,2},{1... | collective-permute-start | bytes 294920 | tf_op jit(solution)/shard_map/ppermute | solution.py:360
  63.3 2.3 %band_product.5.keep = f32[2,256,512]{2,1,0:T(8,128)S(1)} custom-call(s32[50]{0:T(128)S(1)} %concatenate.6.at, f32[1024,1024]{1,0:T(8,128)S(1)} %copy-done.1, bf16[512,512]{1,0:T(8,128)(2,1)S(1)} %get-tuple-element.37.refs_0_, bf16[512,512]{1,0:T(8,128)(2,1)S(1)} %get-tuple-element.38.refs_1_, bf16[512,512]{1,0:T(8,128)(2,1)S(1)} %get-tuple-element.31.refs_0_.refs_2_, ...), custom_call_target="tpu_custom_call" | custom-call | flops 1610612736 | bytes 2097152 | tf_op jit(solution)/shard_map/band_product/pallas_call | solution.py:174
  65.7 1.7 %collective-permute-done.11 = f32[96,256]{1,0:T(8,128)S(1)} collective-permute-done((f32[96,256]{1,0:T(8,128)S(1)}, f32[96,256]{1,0:T(8,128)S(1)}, u32[]{:S(2)}, u32[]{:S(2)}) %collective-permute-start.11) | collective-permute-done | bytes 98336 | tf_op jit(solution)/shard_map/ppermute | solution.py:360
  67.5 0.9 collective-permute-done.10
  68.5 0.9 %collective-permute-start.13 = (f32[256,512]{1,0:T(8,128)S(1)}, f32[256,512]{1,0:T(8,128)S(1)}, u32[]{:S(2)}, u32[]{:S(2)}) collective-permute-start(f32[256,512]{1,0:T(8,128)S(1)} %fusion), channel_id=1, source_target_pairs={{0,2},{1,3},{2,0},{3,1},{4,6},{5,7},{6,4},{7,5},{8,10},{9,11},{10,... | collective-permute-start | bytes 1572872 | tf_op jit(solution)/shard_map/ppermute | solution.py:360
  69.4 2.5 %collective-permute-start.14 = (f32[96,256]{1,0:T(8,128)S(1)}, f32[96,256]{1,0:T(8,128)S(1)}, u32[]{:S(2)}, u32[]{:S(2)}) collective-permute-start(f32[96,256]{1,0:T(8,128)S(1)} %fusion.1), channel_id=1, source_target_pairs={{0,8},{4,12},{8,0},{12,4},{1,9},{5,13},{9,1},{13,5},{2,10},{6,14},... | collective-permute-start | bytes 294920 | tf_op jit(solution)/shard_map/ppermute | solution.py:360
  71.9 4.4 %collective-permute-done.14 = f32[96,256]{1,0:T(8,128)S(1)} collective-permute-done((f32[96,256]{1,0:T(8,128)S(1)}, f32[96,256]{1,0:T(8,128)S(1)}, u32[]{:S(2)}, u32[]{:S(2)}) %collective-permute-start.14) | collective-permute-done | bytes 98336 | tf_op jit(solution)/shard_map/ppermute | solution.py:360
  76.3 0.8 collective-permute-start.17
  77.1 0.7 collective-permute-start.16
  77.8 2.1 %collective-permute-start.15 = (f32[96,256]{1,0:T(8,128)S(1)}, f32[96,256]{1,0:T(8,128)S(1)}, u32[]{:S(2)}, u32[]{:S(2)}) collective-permute-start(f32[96,256]{1,0:T(8,128)S(1)} %add.27), channel_id=1, source_target_pairs={{0,4},{4,0},{8,12},{12,8},{1,5},{5,1},{9,13},{13,9},{2,6},{6,2},{1... | collective-permute-start | bytes 294920 | tf_op jit(solution)/shard_map/ppermute | solution.py:360
  79.9 5.0 %collective-permute-done.13.other = f32[256,512]{1,0:T(8,128)S(1)} collective-permute-done((f32[256,512]{1,0:T(8,128)S(1)}, f32[256,512]{1,0:T(8,128)S(1)}, u32[]{:S(2)}, u32[]{:S(2)}) %collective-permute-start.13) | collective-permute-done | bytes 524320 | tf_op jit(solution)/shard_map/ppermute | solution.py:360
  84.9 1.0 %collective-permute-done.16 = f32[96,256]{1,0:T(8,128)S(1)} collective-permute-done((f32[96,256]{1,0:T(8,128)S(1)}, f32[96,256]{1,0:T(8,128)S(1)}, u32[]{:S(2)}, u32[]{:S(2)}) %collective-permute-start.16) | collective-permute-done | bytes 98336 | tf_op jit(solution)/shard_map/ppermute | solution.py:360
  86.0 1.5 %column_rows.1 = (f32[256,256]{1,0:T(8,128)}, f32[256,256]{1,0:T(8,128)}) custom-call(s32[50]{0:T(128)S(1)} %concatenate.6.at, f32[2,256,512]{2,1,0:T(8,128)S(1)} %band_product.5.keep, f32[2,256,512]{2,1,0:T(8,128)S(1)} %collective-permute-done.9.got, f32[256,512]{1,0:T(8,128)S(1)} %collective-permute-done.13.other, f32[256,256]{1,0:T(8,128)S(1)} %copy-done.2), custom_call_target="tpu_custom_call" | custom-call | tf_op jit(solution)/shard_map/column_rows/pallas_call | solution.py:303
  87.8 1.9 %small_blocks.1 = (f32[256,256]{1,0:T(8,128)}, f32[256,256]{1,0:T(8,128)}, f32[256,256]{1,0:T(8,128)}) custom-call(s32[50]{0:T(128)S(1)} %concatenate.6.at, f32[256,256]{1,0:T(8,128)S(1)} %copy-done.2, f32[256,256]{1,0:T(8,128)S(1)} %copy-done.3, f32[256,256]{1,0:T(8,128)S(1)} %copy-done.4, f32[384,256]{1,0:T(8,128)S(1)} %constant_dynamic-update-slice_fusion.first, ...), custom_call_target="tpu_custom_call" | custom-call | tf_op jit(solution)/shard_map/small_blocks/pallas_call | solution.py:336
  (37 shorter events, 2.0 us)
Async XLA Ops:
  0.6 1.9 %collective-permute-start.2 = (f32[256,256]{1,0:T(8,128)}, f32[256,256]{1,0:T(8,128)S(1)}, u32[]{:S(2)}, u32[]{:S(2)}) collective-permute-start(f32[256,256]{1,0:T(8,128)} %refs_0_.1), channel_id=1, source_target_pairs={{0,1},{1,0},{2,3},{3,2},{4,5},{5,4},{6,7},{7,6},{8,9},{9,8},{10,11... | collective-permute-start | bytes 786440 | tf_op jit(solution)/shard_map/ppermute | solution.py:360
  1.1 1.7 %collective-permute-start.3 = (f32[256,256]{1,0:T(8,128)}, f32[256,256]{1,0:T(8,128)S(1)}, u32[]{:S(2)}, u32[]{:S(2)}) collective-permute-start(f32[256,256]{1,0:T(8,128)} %refs_1_.1), channel_id=1, source_target_pairs={{0,1},{1,0},{2,3},{3,2},{4,5},{5,4},{6,7},{7,6},{8,9},{9,8},{10,11... | collective-permute-start | bytes 786440 | tf_op jit(solution)/shard_map/ppermute | solution.py:360
  3.0 43.3 %collective-permute-start.6 = (f32[1024,256]{1,0:T(8,128)S(1)}, f32[1024,256]{1,0:T(8,128)S(1)}, u32[]{:S(2)}, u32[]{:S(2)}) collective-permute-start(f32[1024,256]{1,0:T(8,128)S(1)} %stack_rows.3.here), channel_id=1, source_target_pairs={{0,8},{1,12},{2,0},{3,4},{4,9},{5,13},{6,1},{7,5},{8,10},{9,14},{1... | collective-permute-start | bytes 3145736 | tf_op jit(solution)/shard_map/ppermute | solution.py:371
  7.0 42.3 %collective-permute-start.7 = (f32[1024,256]{1,0:T(8,128)S(1)}, f32[1024,256]{1,0:T(8,128)S(1)}, u32[]{:S(2)}, u32[]{:S(2)}) collective-permute-start(f32[1024,256]{1,0:T(8,128)S(1)} %stack_rows.3.here), channel_id=1, source_target_pairs={{0,0},{1,4},{2,8},{3,12},{4,1},{5,5},{6,9},{7,13},{8,2},{9,6},{10,... | collective-permute-start | bytes 3145736 | tf_op jit(solution)/shard_map/ppermute | solution.py:371
  7.7 30.6 %collective-permute-start.1 = (f32[256,256]{1,0:T(8,128)}, f32[256,256]{1,0:T(8,128)S(1)}, u32[]{:S(2)}, u32[]{:S(2)}) collective-permute-start(f32[256,256]{1,0:T(8,128)} %refs_1_.1), channel_id=1, source_target_pairs={{0,2},{1,3},{2,0},{3,1},{4,6},{5,7},{6,4},{7,5},{8,10},{9,11},{10,... | collective-permute-start | bytes 786440 | tf_op jit(solution)/shard_map/ppermute | solution.py:360
  11.9 29.3 %collective-permute-start = (f32[256,256]{1,0:T(8,128)}, f32[256,256]{1,0:T(8,128)}, u32[]{:S(2)}, u32[]{:S(2)}) collective-permute-start(f32[256,256]{1,0:T(8,128)} %refs_0_.1), channel_id=1, source_target_pairs={{0,2},{1,3},{2,0},{3,1},{4,6},{5,7},{6,4},{7,5},{8,10},{9,11},{10,... | collective-permute-start | bytes 786440 | tf_op jit(solution)/shard_map/ppermute | solution.py:360
  12.8 2.2 %copy-start = (f32[1024,1024]{1,0:T(8,128)S(1)}, f32[1024,1024]{1,0:T(8,128)}, u32[]{:S(2)}) copy-start(f32[1024,1024]{1,0:T(8,128)} %known.9) | copy-start | bytes 12582916
  15.0 28.4 %copy-start.1 = (f32[1024,1024]{1,0:T(8,128)S(1)}, f32[1024,1024]{1,0:T(8,128)}, u32[]{:S(2)}) copy-start(f32[1024,1024]{1,0:T(8,128)} %known.9) | copy-start | bytes 12582916
  41.3 2.1 %collective-permute-start.4 = (f32[256,256]{1,0:T(8,128)}, f32[256,256]{1,0:T(8,128)S(1)}, u32[]{:S(2)}, u32[]{:S(2)}) collective-permute-start(f32[256,256]{1,0:T(8,128)} %collective-permute-done.two), channel_id=1, source_target_pairs={{0,1},{1,0},{2,3},{3,2},{4,5},{5,4},{6,7},{7,6},{8,9},{9,8},{10,11... | collective-permute-start | bytes 786440 | tf_op jit(solution)/shard_map/ppermute | solution.py:360
  41.3 2.1 %collective-permute-start.5 = (f32[256,256]{1,0:T(8,128)S(1)}, f32[256,256]{1,0:T(8,128)S(1)}, u32[]{:S(2)}, u32[]{:S(2)}) collective-permute-start(f32[256,256]{1,0:T(8,128)S(1)} %collective-permute-done.1.one), channel_id=1, source_target_pairs={{0,1},{1,0},{2,3},{3,2},{4,5},{5,4},{6,7},{7,6},{8,9},{9,8},{10,11... | collective-permute-start | bytes 786440 | tf_op jit(solution)/shard_map/ppermute | solution.py:360
  50.9 1.8 %collective-permute-start.8 = (f32[384,256]{1,0:T(8,128)S(1)}, f32[384,256]{1,0:T(8,128)S(1)}, u32[]{:S(2)}, u32[]{:S(2)}) collective-permute-start(f32[384,256]{1,0:T(8,128)S(1)} %get-tuple-element.35), channel_id=1, source_target_pairs={{0,1},{1,0},{2,3},{3,2},{4,5},{5,4},{6,7},{7,6},{8,9},{9,8},{10,11... | collective-permute-start | bytes 1179656 | tf_op jit(solution)/shard_map/ppermute | solution.py:360
  52.7 15.6 %collective-permute-start.9 = (f32[2,256,512]{2,1,0:T(8,128)S(1)}, f32[2,256,512]{2,1,0:T(8,128)S(1)}, u32[]{:S(2)}, u32[]{:S(2)}) collective-permute-start(f32[2,256,512]{2,1,0:T(8,128)S(1)} %band_product.4), channel_id=1, source_target_pairs={{0,1},{1,0},{2,3},{3,2},{4,5},{5,4},{6,7},{7,6},{8,9},{9,8},{10,11... | collective-permute-start | bytes 3145736 | tf_op jit(solution)/shard_map/ppermute | solution.py:360
  53.2 12.5 %collective-permute-start.12 = (f32[96,256]{1,0:T(8,128)S(1)}, f32[96,256]{1,0:T(8,128)S(1)}, u32[]{:S(2)}, u32[]{:S(2)}) collective-permute-start(f32[96,256]{1,0:T(8,128)S(1)} %get-tuple-element.49), channel_id=1, source_target_pairs={{0,6},{1,7},{2,4},{3,5},{4,2},{5,3},{6,0},{7,1},{8,14},{9,15},{10,... | collective-permute-start | bytes 294920 | tf_op jit(solution)/shard_map/ppermute | solution.py:367
  62.2 5.2 %collective-permute-start.11 = (f32[96,256]{1,0:T(8,128)S(1)}, f32[96,256]{1,0:T(8,128)S(1)}, u32[]{:S(2)}, u32[]{:S(2)}) collective-permute-start(f32[96,256]{1,0:T(8,128)S(1)} %get-tuple-element.50), channel_id=1, source_target_pairs={{0,2},{1,3},{2,0},{3,1},{4,6},{5,7},{6,4},{7,5},{8,10},{9,11},{10,... | collective-permute-start | bytes 294920 | tf_op jit(solution)/shard_map/ppermute | solution.py:360
  62.2 23.8 %copy-start.2 = (f32[256,256]{1,0:T(8,128)S(1)}, f32[256,256]{1,0:T(8,128)}, u32[]{:S(2)}) copy-start(f32[256,256]{1,0:T(8,128)} %top.3) | copy-start | bytes 786436
  62.2 6.1 %collective-permute-start.10 = (f32[96,256]{1,0:T(8,128)S(1)}, f32[96,256]{1,0:T(8,128)S(1)}, u32[]{:S(2)}, u32[]{:S(2)}) collective-permute-start(f32[96,256]{1,0:T(8,128)S(1)} %get-tuple-element.51), channel_id=1, source_target_pairs={{0,4},{4,0},{8,12},{12,8},{1,5},{5,1},{9,13},{13,9},{2,6},{6,2},{1... | collective-permute-start | bytes 294920 | tf_op jit(solution)/shard_map/ppermute | solution.py:360
  65.7 22.1 %copy-start.3 = (f32[256,256]{1,0:T(8,128)S(1)}, f32[256,256]{1,0:T(8,128)}, u32[]{:S(2)}) copy-start(f32[256,256]{1,0:T(8,128)} %inner_two.1) | copy-start | bytes 786436
  65.7 22.1 %copy-start.4 = (f32[256,256]{1,0:T(8,128)S(1)}, f32[256,256]{1,0:T(8,128)}, u32[]{:S(2)}) copy-start(f32[256,256]{1,0:T(8,128)} %inner_one.1) | copy-start | bytes 786436
  68.5 16.4 %collective-permute-start.13 = (f32[256,512]{1,0:T(8,128)S(1)}, f32[256,512]{1,0:T(8,128)S(1)}, u32[]{:S(2)}, u32[]{:S(2)}) collective-permute-start(f32[256,512]{1,0:T(8,128)S(1)} %fusion), channel_id=1, source_target_pairs={{0,2},{1,3},{2,0},{3,1},{4,6},{5,7},{6,4},{7,5},{8,10},{9,11},{10,... | collective-permute-start | bytes 1572872 | tf_op jit(solution)/shard_map/ppermute | solution.py:360
  69.4 6.9 %collective-permute-start.14 = (f32[96,256]{1,0:T(8,128)S(1)}, f32[96,256]{1,0:T(8,128)S(1)}, u32[]{:S(2)}, u32[]{:S(2)}) collective-permute-start(f32[96,256]{1,0:T(8,128)S(1)} %fusion.1), channel_id=1, source_target_pairs={{0,8},{4,12},{8,0},{12,4},{1,9},{5,13},{9,1},{13,5},{2,10},{6,14},... | collective-permute-start | bytes 294920 | tf_op jit(solution)/shard_map/ppermute | solution.py:360
  76.3 9.6 %collective-permute-start.17 = (f32[96,256]{1,0:T(8,128)S(1)}, f32[96,256]{1,0:T(8,128)S(1)}, u32[]{:S(2)}, u32[]{:S(2)}) collective-permute-start(f32[96,256]{1,0:T(8,128)S(1)} %add.27), channel_id=1, source_target_pairs={{0,6},{1,7},{2,4},{3,5},{4,2},{5,3},{6,0},{7,1},{8,14},{9,15},{10,... | collective-permute-start | bytes 294920 | tf_op jit(solution)/shard_map/ppermute | solution.py:367
  77.1 8.8 %collective-permute-start.16 = (f32[96,256]{1,0:T(8,128)S(1)}, f32[96,256]{1,0:T(8,128)S(1)}, u32[]{:S(2)}, u32[]{:S(2)}) collective-permute-start(f32[96,256]{1,0:T(8,128)S(1)} %add.27), channel_id=1, source_target_pairs={{0,2},{1,3},{2,0},{3,1},{4,6},{5,7},{6,4},{7,5},{8,10},{9,11},{10,... | collective-permute-start | bytes 294920 | tf_op jit(solution)/shard_map/ppermute | solution.py:360
  77.8 7.1 %collective-permute-start.15 = (f32[96,256]{1,0:T(8,128)S(1)}, f32[96,256]{1,0:T(8,128)S(1)}, u32[]{:S(2)}, u32[]{:S(2)}) collective-permute-start(f32[96,256]{1,0:T(8,128)S(1)} %add.27), channel_id=1, source_target_pairs={{0,4},{4,0},{8,12},{12,8},{1,5},{5,1},{9,13},{13,9},{2,6},{6,2},{1... | collective-permute-start | bytes 294920 | tf_op jit(solution)/shard_map/ppermute | solution.py:360
  86.0 1.8 %collective-permute-start.18 = (f32[384,256]{1,0:T(8,128)S(1)}, f32[384,256]{1,0:T(8,128)S(1)}, u32[]{:S(2)}, u32[]{:S(2)}) collective-permute-start(f32[384,256]{1,0:T(8,128)S(1)} %constant_dynamic-update-slice_fusion.first), channel_id=1, source_target_pairs={{0,1},{1,0},{2,3},{3,2},{4,5},{5,4},{6,7},{7,6},{8,9},{9,8},{10,11... | collective-permute-start | bytes 1179656 | tf_op jit(solution)/shard_map/ppermute | solution.py:360

commit v8 on v7

--- a/solution.py
+++ b/solution.py
@@ -391,7 +391,7 @@
     keep = band_product(n, 0, (0, 1), after(at, send), known, right)
     got = core(after(send, mine))
     own, beyond, beside, corner = jnp.split(mine, 4)
-    mine = (own + along("prow", 1, beyond)) + (across(beside) + opposite(corner))
+    mine = (own + opposite(corner)) + (across(beside) + along("prow", 1, beyond))
     other = across(after(keep[1] + got[1], mine))
     mine = mine + along("prow", 2, mine)
     column_two, column_one = columns(n, at, keep, got, other, top_one)

time: 89.9 us -> 89.3 us (level)
    ppermute x2, starting transfers between devices: 9.81 us -> 1.25 us  [opposite(): return lax.ppermute(rows, ('prow', 'pcol'), pairs)]
    ppermute x15, starting transfers between devices: 13.4 us -> 22 us  [along(): return lax.ppermute(array, axis, [(i, i ^ k) for i in range(n)])]
    ppermute x15, waiting for transfers between devices: 39.3 us -> 37.4 us  [along(): return lax.ppermute(array, axis, [(i, i ^ k) for i in range(n)])]
    ppermute x2, waiting for transfers between devices: 0.01 us -> 1.31 us  [opposite(): return lax.ppermute(rows, ('prow', 'pcol'), pairs)]
where the time goes in v8:
time: 89.3 us; the launch traced here: 89 us
  waiting for transfers between devices  38.7 us (43%)
  starting transfers between devices  28 us (31%)
  Pallas kernels  18.4 us (21%)
  local copies, waits for them, and re-layouts  3.03 us (3%)
    ppermute x15, waiting for transfers between devices, along(): return lax.ppermute(array, axis, [(i, i ^ k) for i in range(n)])  37.4 us
    ppermute x15, starting transfers between devices, along(): return lax.ppermute(array, axis, [(i, i ^ k) for i in range(n)])  22 us
    pallas_call x7, Pallas kernels, call(): pl.pallas_call(kernel, out_shape=out_shape, in_specs=[SMEM] + [VMEM] * (l...  13.8 us
    ppermute x2, starting transfers between devices, direct(): return lax.ppermute(rows, ('prow', 'pcol'), pairs)  4.73 us
    unnamed x13, local copies, waits for them, and re-layouts  2.23 us
    pallas_call x1, Pallas kernels, small_blocks(): pl.pallas_call(functools.partial(blocks_kernel, n), out_shape=(shape, sha...  1.89 us
  transfers between devices with their start and end apart: 19, of which 11 were waited for; matrix products, arithmetic and copies ran while one was open for 1% of the time, Pallas kernels for 17%

profile of v8, /device:TPU:0, one launch (start us, length us, event | category | flops | bytes accessed | tf_op | source)
XLA Modules:
  0.0 89.0 jit_solution(18186323210968157210)
XLA Ops:
  0.6 0.5 collective-permute-start.2
  1.2 1.0 %stack_rows.2.refs_0_ = f32[512,256]{1,0:T(8,128)S(1)} custom-call(f32[256,256]{1,0:T(8,128)} %refs_0_.1, f32[256,256]{1,0:T(8,128)} %refs_1_.1), custom_call_target="tpu_custom_call" | custom-call | bytes 1048576 | tf_op jit(solution)/shard_map/stack_rows/pallas_call | solution.py:141
  3.0 4.0 %collective-permute-start.6 = (f32[1024,256]{1,0:T(8,128)S(1)}, f32[1024,256]{1,0:T(8,128)S(1)}, u32[]{:S(2)}, u32[]{:S(2)}) collective-permute-start(f32[1024,256]{1,0:T(8,128)S(1)} %stack_rows.3.here), channel_id=1, source_target_pairs={{0,8},{1,12},{2,0},{3,4},{4,9},{5,13},{6,1},{7,5},{8,10},{9,14},{1... | collective-permute-start | bytes 3145736 | tf_op jit(solution)/shard_map/ppermute | solution.py:371
  7.0 0.7 collective-permute-start.7
  7.7 4.2 %collective-permute-start.1 = (f32[256,256]{1,0:T(8,128)}, f32[256,256]{1,0:T(8,128)S(1)}, u32[]{:S(2)}, u32[]{:S(2)}) collective-permute-start(f32[256,256]{1,0:T(8,128)} %refs_1_.1), channel_id=1, source_target_pairs={{0,2},{1,3},{2,0},{3,1},{4,6},{5,7},{6,4},{7,5},{8,10},{9,11},{10,... | collective-permute-start | bytes 786440 | tf_op jit(solution)/shard_map/ppermute | solution.py:360
  12.0 0.8 concatenate.6.at
  12.8 2.2 %copy-done = f32[1024,1024]{1,0:T(8,128)S(1)} copy-done((f32[1024,1024]{1,0:T(8,128)S(1)}, f32[1024,1024]{1,0:T(8,128)}, u32[]{:S(2)}) %copy-start) | copy-done | bytes 4194328
  15.0 2.4 %left_first.1.before = f32[512,1024]{1,0:T(8,128)S(1)} custom-call(s32[50]{0:T(128)S(1)} %concatenate.6.at, f32[1024,1024]{1,0:T(8,128)S(1)} %copy-done, f32[1024,256]{1,0:T(8,128)S(1)} %stack_rows.3.here), custom_call_target="tpu_custom_call" | custom-call | tf_op jit(solution)/shard_map/left_first/pallas_call | solution.py:174
  17.4 20.9 %collective-permute-done.1.one = f32[256,256]{1,0:T(8,128)S(1)} collective-permute-done((f32[256,256]{1,0:T(8,128)}, f32[256,256]{1,0:T(8,128)S(1)}, u32[]{:S(2)}, u32[]{:S(2)}) %collective-permute-start.1) | collective-permute-done | bytes 262176 | tf_op jit(solution)/shard_map/ppermute | solution.py:360
  38.4 2.9 %collective-permute-done.two = f32[256,256]{1,0:T(8,128)} collective-permute-done((f32[256,256]{1,0:T(8,128)}, f32[256,256]{1,0:T(8,128)}, u32[]{:S(2)}, u32[]{:S(2)}) %collective-permute-start) | collective-permute-done | bytes 262176 | tf_op jit(solution)/shard_map/ppermute | solution.py:360
  41.8 1.6 %collective-permute-done.4.core_two = f32[256,256]{1,0:T(8,128)S(1)} collective-permute-done((f32[256,256]{1,0:T(8,128)}, f32[256,256]{1,0:T(8,128)S(1)}, u32[]{:S(2)}, u32[]{:S(2)}) %collective-permute-start.4) | collective-permute-done | bytes 262176 | tf_op jit(solution)/shard_map/ppermute | solution.py:360
  43.4 2.9 %left_last.1 = (bf16[512,1024]{1,0:T(8,128)(2,1)S(1)}, bf16[512,1024]{1,0:T(8,128)(2,1)S(1)}) custom-call(s32[50]{0:T(128)S(1)} %concatenate.6.at, f32[1024,1024]{1,0:T(8,128)S(1)} %copy-done.1, f32[256,256]{1,0:T(8,128)} %collective-permute-done.two, f32[256,256]{1,0:T(8,128)S(1)} %collective-permute-done.1.one, ...), custom_call_target="tpu_custom_call" | custom-call | tf_op jit(solution)/shard_map/left_last/pallas_call | solution.py:174
  46.3 1.5 %first_sums.1 = (f32[768,256]{1,0:T(8,128)S(1)}, bf16[512,512]{1,0:T(8,128)(2,1)S(1)}, bf16[512,512]{1,0:T(8,128)(2,1)S(1)}) custom-call(s32[50]{0:T(128)S(1)} %concatenate.6.at, bf16[512,1024]{1,0:T(8,128)(2,1)S(1)} %get-tuple-element.29.left_high, bf16[512,1024]{1,0:T(8,128)(2,1)S(1)} %get-tuple-element.30.left_low, ...), custom_call_target="tpu_custom_call" | custom-call | flops 603979776 | tf_op jit(solution)/shard_map/first_sums/pallas_call | solution.py:174
  47.8 1.5 %band_product.3.refs_2_ = f32[2,256,512]{2,1,0:T(8,128)S(1)} custom-call(s32[50]{0:T(128)S(1)} %concatenate.6.at, f32[1024,1024]{1,0:T(8,128)S(1)} %copy-done.1, bf16[512,512]{1,0:T(8,128)(2,1)S(1)} %get-tuple-element.31.refs_0_.refs_2_, bf16[512,512]{1,0:T(8,128)(2,1)S(1)} %get-tuple-element.32.refs_1_.refs_3_), custom_call_target="tpu_custom_call" | custom-call | flops 805306368 | bytes 1048576 | tf_op jit(solution)/shard_map/band_product/pallas_call | solution.py:174
  49.3 1.5 %last_sums.1 = (f32[384,256]{1,0:T(8,128)S(1)}, f32[384,256]{1,0:T(8,128)S(1)}, bf16[512,512]{1,0:T(8,128)(2,1)S(1)}, bf16[512,512]{1,0:T(8,128)(2,1)S(1)}) custom-call(s32[50]{0:T(128)S(1)} %concatenate.6.at, bf16[512,1024]{1,0:T(8,128)(2,1)S(1)} %get-tuple-element.29.left_high, bf16[512,1024]{1,0:T(8,128)(2,1)S(1)} %get-tuple-element.30.left_low, ...), custom_call_target="tpu_custom_call" | custom-call | flops 603979776 | tf_op jit(solution)/shard_map/last_sums/pallas_call | solution.py:174
  51.1 1.5 %band_product.4 = f32[2,256,512]{2,1,0:T(8,128)S(1)} custom-call(s32[50]{0:T(128)S(1)} %concatenate.6.at, f32[1024,1024]{1,0:T(8,128)S(1)} %copy-done.1, bf16[512,512]{1,0:T(8,128)(2,1)S(1)} %get-tuple-element.37.refs_0_, bf16[512,512]{1,0:T(8,128)(2,1)S(1)} %get-tuple-element.38.refs_1_, f32[2,256,512]{2,1,0:T(8,128)S(1)} %band_product.3.refs_2_), custom_call_target="tpu_custom_call" | custom-call | flops 805306368 | bytes 1048576 | tf_op jit(solution)/shard_map/band_product/pallas_call | solution.py:174
  53.2 6.9 %collective-permute-start.12 = (f32[96,256]{1,0:T(8,128)S(1)}, f32[96,256]{1,0:T(8,128)S(1)}, u32[]{:S(2)}, u32[]{:S(2)}) collective-permute-start(f32[96,256]{1,0:T(8,128)S(1)} %get-tuple-element.49), channel_id=1, source_target_pairs={{0,4},{4,0},{8,12},{12,8},{1,5},{5,1},{9,13},{13,9},{2,6},{6,2},{1... | collective-permute-start | bytes 294920 | tf_op jit(solution)/shard_map/ppermute | solution.py:360
  60.0 2.8 %collective-permute-start.11 = (f32[96,256]{1,0:T(8,128)S(1)}, f32[96,256]{1,0:T(8,128)S(1)}, u32[]{:S(2)}, u32[]{:S(2)}) collective-permute-start(f32[96,256]{1,0:T(8,128)S(1)} %get-tuple-element.50), channel_id=1, source_target_pairs={{0,2},{1,3},{2,0},{3,1},{4,6},{5,7},{6,4},{7,5},{8,10},{9,11},{10,... | collective-permute-start | bytes 294920 | tf_op jit(solution)/shard_map/ppermute | solution.py:360
  62.8 0.6 collective-permute-start.10
  63.3 2.3 %band_product.5.keep = f32[2,256,512]{2,1,0:T(8,128)S(1)} custom-call(s32[50]{0:T(128)S(1)} %concatenate.6.at, f32[1024,1024]{1,0:T(8,128)S(1)} %copy-done.1, bf16[512,512]{1,0:T(8,128)(2,1)S(1)} %get-tuple-element.37.refs_0_, bf16[512,512]{1,0:T(8,128)(2,1)S(1)} %get-tuple-element.38.refs_1_, bf16[512,512]{1,0:T(8,128)(2,1)S(1)} %get-tuple-element.31.refs_0_.refs_2_, ...), custom_call_target="tpu_custom_call" | custom-call | flops 1610612736 | bytes 2097152 | tf_op jit(solution)/shard_map/band_product/pallas_call | solution.py:174
  65.7 1.3 %collective-permute-done.11 = f32[96,256]{1,0:T(8,128)S(1)} collective-permute-done((f32[96,256]{1,0:T(8,128)S(1)}, f32[96,256]{1,0:T(8,128)S(1)}, u32[]{:S(2)}, u32[]{:S(2)}) %collective-permute-start.11) | collective-permute-done | bytes 98336 | tf_op jit(solution)/shard_map/ppermute | solution.py:360
  67.0 1.3 %collective-permute-done.10 = f32[96,256]{1,0:T(8,128)S(1)} collective-permute-done((f32[96,256]{1,0:T(8,128)S(1)}, f32[96,256]{1,0:T(8,128)S(1)}, u32[]{:S(2)}, u32[]{:S(2)}) %collective-permute-start.10) | collective-permute-done | bytes 98336 | tf_op jit(solution)/shard_map/ppermute | solution.py:367
  68.4 1.2 %collective-permute-start.13 = (f32[256,512]{1,0:T(8,128)S(1)}, f32[256,512]{1,0:T(8,128)S(1)}, u32[]{:S(2)}, u32[]{:S(2)}) collective-permute-start(f32[256,512]{1,0:T(8,128)S(1)} %fusion), channel_id=1, source_target_pairs={{0,2},{1,3},{2,0},{3,1},{4,6},{5,7},{6,4},{7,5},{8,10},{9,11},{10,... | collective-permute-start | bytes 1572872 | tf_op jit(solution)/shard_map/ppermute | solution.py:360
  69.7 2.2 %collective-permute-start.14 = (f32[96,256]{1,0:T(8,128)S(1)}, f32[96,256]{1,0:T(8,128)S(1)}, u32[]{:S(2)}, u32[]{:S(2)}) collective-permute-start(f32[96,256]{1,0:T(8,128)S(1)} %fusion.1), channel_id=1, source_target_pairs={{0,8},{4,12},{8,0},{12,4},{1,9},{5,13},{9,1},{13,5},{2,10},{6,14},... | collective-permute-start | bytes 294920 | tf_op jit(solution)/shard_map/ppermute | solution.py:360
  71.9 4.4 %collective-permute-done.14 = f32[96,256]{1,0:T(8,128)S(1)} collective-permute-done((f32[96,256]{1,0:T(8,128)S(1)}, f32[96,256]{1,0:T(8,128)S(1)}, u32[]{:S(2)}, u32[]{:S(2)}) %collective-permute-start.14) | collective-permute-done | bytes 98336 | tf_op jit(solution)/shard_map/ppermute | solution.py:360
  76.3 0.7 collective-permute-start.17
  77.0 1.0 %collective-permute-start.16 = (f32[96,256]{1,0:T(8,128)S(1)}, f32[96,256]{1,0:T(8,128)S(1)}, u32[]{:S(2)}, u32[]{:S(2)}) collective-permute-start(f32[96,256]{1,0:T(8,128)S(1)} %add.27), channel_id=1, source_target_pairs={{0,2},{1,3},{2,0},{3,1},{4,6},{5,7},{6,4},{7,5},{8,10},{9,11},{10,... | collective-permute-start | bytes 294920 | tf_op jit(solution)/shard_map/ppermute | solution.py:360
  78.0 1.9 %collective-permute-start.15 = (f32[96,256]{1,0:T(8,128)S(1)}, f32[96,256]{1,0:T(8,128)S(1)}, u32[]{:S(2)}, u32[]{:S(2)}) collective-permute-start(f32[96,256]{1,0:T(8,128)S(1)} %add.27), channel_id=1, source_target_pairs={{0,4},{4,0},{8,12},{12,8},{1,5},{5,1},{9,13},{13,9},{2,6},{6,2},{1... | collective-permute-start | bytes 294920 | tf_op jit(solution)/shard_map/ppermute | solution.py:360
  79.8 4.4 %collective-permute-done.13.other = f32[256,512]{1,0:T(8,128)S(1)} collective-permute-done((f32[256,512]{1,0:T(8,128)S(1)}, f32[256,512]{1,0:T(8,128)S(1)}, u32[]{:S(2)}, u32[]{:S(2)}) %collective-permute-start.13) | collective-permute-done | bytes 524320 | tf_op jit(solution)/shard_map/ppermute | solution.py:360
  84.3 1.0 %collective-permute-done.16 = f32[96,256]{1,0:T(8,128)S(1)} collective-permute-done((f32[96,256]{1,0:T(8,128)S(1)}, f32[96,256]{1,0:T(8,128)S(1)}, u32[]{:S(2)}, u32[]{:S(2)}) %collective-permute-start.16) | collective-permute-done | bytes 98336 | tf_op jit(solution)/shard_map/ppermute | solution.py:360
  85.4 1.5 %column_rows.1 = (f32[256,256]{1,0:T(8,128)}, f32[256,256]{1,0:T(8,128)}) custom-call(s32[50]{0:T(128)S(1)} %concatenate.6.at, f32[2,256,512]{2,1,0:T(8,128)S(1)} %band_product.5.keep, f32[2,256,512]{2,1,0:T(8,128)S(1)} %collective-permute-done.9.got, f32[256,512]{1,0:T(8,128)S(1)} %collective-permute-done.13.other, f32[256,256]{1,0:T(8,128)S(1)} %copy-done.2), custom_call_target="tpu_custom_call" | custom-call | tf_op jit(solution)/shard_map/column_rows/pallas_call | solution.py:303
  87.1 1.9 %small_blocks.1 = (f32[256,256]{1,0:T(8,128)}, f32[256,256]{1,0:T(8,128)}, f32[256,256]{1,0:T(8,128)}) custom-call(s32[50]{0:T(128)S(1)} %concatenate.6.at, f32[256,256]{1,0:T(8,128)S(1)} %copy-done.2, f32[256,256]{1,0:T(8,128)S(1)} %copy-done.3, f32[256,256]{1,0:T(8,128)S(1)} %copy-done.4, f32[384,256]{1,0:T(8,128)S(1)} %constant_dynamic-update-slice_fusion.first, ...), custom_call_target="tpu_custom_call" | custom-call | tf_op jit(solution)/shard_map/small_blocks/pallas_call | solution.py:336
  (37 shorter events, 2.5 us)
Async XLA Ops:
  0.6 1.9 %collective-permute-start.2 = (f32[256,256]{1,0:T(8,128)}, f32[256,256]{1,0:T(8,128)S(1)}, u32[]{:S(2)}, u32[]{:S(2)}) collective-permute-start(f32[256,256]{1,0:T(8,128)} %refs_0_.1), channel_id=1, source_target_pairs={{0,1},{1,0},{2,3},{3,2},{4,5},{5,4},{6,7},{7,6},{8,9},{9,8},{10,11... | collective-permute-start | bytes 786440 | tf_op jit(solution)/shard_map/ppermute | solution.py:360
  1.1 1.7 %collective-permute-start.3 = (f32[256,256]{1,0:T(8,128)}, f32[256,256]{1,0:T(8,128)S(1)}, u32[]{:S(2)}, u32[]{:S(2)}) collective-permute-start(f32[256,256]{1,0:T(8,128)} %refs_1_.1), channel_id=1, source_target_pairs={{0,1},{1,0},{2,3},{3,2},{4,5},{5,4},{6,7},{7,6},{8,9},{9,8},{10,11... | collective-permute-start | bytes 786440 | tf_op jit(solution)/shard_map/ppermute | solution.py:360
  3.0 43.3 %collective-permute-start.6 = (f32[1024,256]{1,0:T(8,128)S(1)}, f32[1024,256]{1,0:T(8,128)S(1)}, u32[]{:S(2)}, u32[]{:S(2)}) collective-permute-start(f32[1024,256]{1,0:T(8,128)S(1)} %stack_rows.3.here), channel_id=1, source_target_pairs={{0,8},{1,12},{2,0},{3,4},{4,9},{5,13},{6,1},{7,5},{8,10},{9,14},{1... | collective-permute-start | bytes 3145736 | tf_op jit(solution)/shard_map/ppermute | solution.py:371
  7.0 42.3 %collective-permute-start.7 = (f32[1024,256]{1,0:T(8,128)S(1)}, f32[1024,256]{1,0:T(8,128)S(1)}, u32[]{:S(2)}, u32[]{:S(2)}) collective-permute-start(f32[1024,256]{1,0:T(8,128)S(1)} %stack_rows.3.here), channel_id=1, source_target_pairs={{0,0},{1,4},{2,8},{3,12},{4,1},{5,5},{6,9},{7,13},{8,2},{9,6},{10,... | collective-permute-start | bytes 3145736 | tf_op jit(solution)/shard_map/ppermute | solution.py:371
  7.7 30.6 %collective-permute-start.1 = (f32[256,256]{1,0:T(8,128)}, f32[256,256]{1,0:T(8,128)S(1)}, u32[]{:S(2)}, u32[]{:S(2)}) collective-permute-start(f32[256,256]{1,0:T(8,128)} %refs_1_.1), channel_id=1, source_target_pairs={{0,2},{1,3},{2,0},{3,1},{4,6},{5,7},{6,4},{7,5},{8,10},{9,11},{10,... | collective-permute-start | bytes 786440 | tf_op jit(solution)/shard_map/ppermute | solution.py:360
  11.9 29.3 %collective-permute-start = (f32[256,256]{1,0:T(8,128)}, f32[256,256]{1,0:T(8,128)}, u32[]{:S(2)}, u32[]{:S(2)}) collective-permute-start(f32[256,256]{1,0:T(8,128)} %refs_0_.1), channel_id=1, source_target_pairs={{0,2},{1,3},{2,0},{3,1},{4,6},{5,7},{6,4},{7,5},{8,10},{9,11},{10,... | collective-permute-start | bytes 786440 | tf_op jit(solution)/shard_map/ppermute | solution.py:360
  12.8 2.2 %copy-start = (f32[1024,1024]{1,0:T(8,128)S(1)}, f32[1024,1024]{1,0:T(8,128)}, u32[]{:S(2)}) copy-start(f32[1024,1024]{1,0:T(8,128)} %known.9) | copy-start | bytes 12582916
  15.0 28.4 %copy-start.1 = (f32[1024,1024]{1,0:T(8,128)S(1)}, f32[1024,1024]{1,0:T(8,128)}, u32[]{:S(2)}) copy-start(f32[1024,1024]{1,0:T(8,128)} %known.9) | copy-start | bytes 12582916
  41.3 2.1 %collective-permute-start.4 = (f32[256,256]{1,0:T(8,128)}, f32[256,256]{1,0:T(8,128)S(1)}, u32[]{:S(2)}, u32[]{:S(2)}) collective-permute-start(f32[256,256]{1,0:T(8,128)} %collective-permute-done.two), channel_id=1, source_target_pairs={{0,1},{1,0},{2,3},{3,2},{4,5},{5,4},{6,7},{7,6},{8,9},{9,8},{10,11... | collective-permute-start | bytes 786440 | tf_op jit(solution)/shard_map/ppermute | solution.py:360
  41.3 2.1 %collective-permute-start.5 = (f32[256,256]{1,0:T(8,128)S(1)}, f32[256,256]{1,0:T(8,128)S(1)}, u32[]{:S(2)}, u32[]{:S(2)}) collective-permute-start(f32[256,256]{1,0:T(8,128)S(1)} %collective-permute-done.1.one), channel_id=1, source_target_pairs={{0,1},{1,0},{2,3},{3,2},{4,5},{5,4},{6,7},{7,6},{8,9},{9,8},{10,11... | collective-permute-start | bytes 786440 | tf_op jit(solution)/shard_map/ppermute | solution.py:360
  50.9 1.8 %collective-permute-start.8 = (f32[384,256]{1,0:T(8,128)S(1)}, f32[384,256]{1,0:T(8,128)S(1)}, u32[]{:S(2)}, u32[]{:S(2)}) collective-permute-start(f32[384,256]{1,0:T(8,128)S(1)} %get-tuple-element.35), channel_id=1, source_target_pairs={{0,1},{1,0},{2,3},{3,2},{4,5},{5,4},{6,7},{7,6},{8,9},{9,8},{10,11... | collective-permute-start | bytes 1179656 | tf_op jit(solution)/shard_map/ppermute | solution.py:360
  52.7 15.6 %collective-permute-start.9 = (f32[2,256,512]{2,1,0:T(8,128)S(1)}, f32[2,256,512]{2,1,0:T(8,128)S(1)}, u32[]{:S(2)}, u32[]{:S(2)}) collective-permute-start(f32[2,256,512]{2,1,0:T(8,128)S(1)} %band_product.4), channel_id=1, source_target_pairs={{0,1},{1,0},{2,3},{3,2},{4,5},{5,4},{6,7},{7,6},{8,9},{9,8},{10,11... | collective-permute-start | bytes 3145736 | tf_op jit(solution)/shard_map/ppermute | solution.py:360
  53.2 12.5 %collective-permute-start.12 = (f32[96,256]{1,0:T(8,128)S(1)}, f32[96,256]{1,0:T(8,128)S(1)}, u32[]{:S(2)}, u32[]{:S(2)}) collective-permute-start(f32[96,256]{1,0:T(8,128)S(1)} %get-tuple-element.49), channel_id=1, source_target_pairs={{0,4},{4,0},{8,12},{12,8},{1,5},{5,1},{9,13},{13,9},{2,6},{6,2},{1... | collective-permute-start | bytes 294920 | tf_op jit(solution)/shard_map/ppermute | solution.py:360
  60.0 7.0 %collective-permute-start.11 = (f32[96,256]{1,0:T(8,128)S(1)}, f32[96,256]{1,0:T(8,128)S(1)}, u32[]{:S(2)}, u32[]{:S(2)}) collective-permute-start(f32[96,256]{1,0:T(8,128)S(1)} %get-tuple-element.50), channel_id=1, source_target_pairs={{0,2},{1,3},{2,0},{3,1},{4,6},{5,7},{6,4},{7,5},{8,10},{9,11},{10,... | collective-permute-start | bytes 294920 | tf_op jit(solution)/shard_map/ppermute | solution.py:360
  62.8 22.6 %copy-start.2 = (f32[256,256]{1,0:T(8,128)S(1)}, f32[256,256]{1,0:T(8,128)}, u32[]{:S(2)}) copy-start(f32[256,256]{1,0:T(8,128)} %top.3) | copy-start | bytes 786436
  62.8 5.5 %collective-permute-start.10 = (f32[96,256]{1,0:T(8,128)S(1)}, f32[96,256]{1,0:T(8,128)S(1)}, u32[]{:S(2)}, u32[]{:S(2)}) collective-permute-start(f32[96,256]{1,0:T(8,128)S(1)} %get-tuple-element.51), channel_id=1, source_target_pairs={{0,6},{1,7},{2,4},{3,5},{4,2},{5,3},{6,0},{7,1},{8,14},{9,15},{10,... | collective-permute-start | bytes 294920 | tf_op jit(solution)/shard_map/ppermute | solution.py:367
  65.7 21.4 %copy-start.3 = (f32[256,256]{1,0:T(8,128)S(1)}, f32[256,256]{1,0:T(8,128)}, u32[]{:S(2)}) copy-start(f32[256,256]{1,0:T(8,128)} %inner_two.1) | copy-start | bytes 786436
  65.7 21.4 %copy-start.4 = (f32[256,256]{1,0:T(8,128)S(1)}, f32[256,256]{1,0:T(8,128)}, u32[]{:S(2)}) copy-start(f32[256,256]{1,0:T(8,128)} %inner_one.1) | copy-start | bytes 786436
  68.4 15.8 %collective-permute-start.13 = (f32[256,512]{1,0:T(8,128)S(1)}, f32[256,512]{1,0:T(8,128)S(1)}, u32[]{:S(2)}, u32[]{:S(2)}) collective-permute-start(f32[256,512]{1,0:T(8,128)S(1)} %fusion), channel_id=1, source_target_pairs={{0,2},{1,3},{2,0},{3,1},{4,6},{5,7},{6,4},{7,5},{8,10},{9,11},{10,... | collective-permute-start | bytes 1572872 | tf_op jit(solution)/shard_map/ppermute | solution.py:360
  69.7 6.6 %collective-permute-start.14 = (f32[96,256]{1,0:T(8,128)S(1)}, f32[96,256]{1,0:T(8,128)S(1)}, u32[]{:S(2)}, u32[]{:S(2)}) collective-permute-start(f32[96,256]{1,0:T(8,128)S(1)} %fusion.1), channel_id=1, source_target_pairs={{0,8},{4,12},{8,0},{12,4},{1,9},{5,13},{9,1},{13,5},{2,10},{6,14},... | collective-permute-start | bytes 294920 | tf_op jit(solution)/shard_map/ppermute | solution.py:360
  76.3 9.0 %collective-permute-start.17 = (f32[96,256]{1,0:T(8,128)S(1)}, f32[96,256]{1,0:T(8,128)S(1)}, u32[]{:S(2)}, u32[]{:S(2)}) collective-permute-start(f32[96,256]{1,0:T(8,128)S(1)} %add.27), channel_id=1, source_target_pairs={{0,6},{1,7},{2,4},{3,5},{4,2},{5,3},{6,0},{7,1},{8,14},{9,15},{10,... | collective-permute-start | bytes 294920 | tf_op jit(solution)/shard_map/ppermute | solution.py:367
  77.0 8.3 %collective-permute-start.16 = (f32[96,256]{1,0:T(8,128)S(1)}, f32[96,256]{1,0:T(8,128)S(1)}, u32[]{:S(2)}, u32[]{:S(2)}) collective-permute-start(f32[96,256]{1,0:T(8,128)S(1)} %add.27), channel_id=1, source_target_pairs={{0,2},{1,3},{2,0},{3,1},{4,6},{5,7},{6,4},{7,5},{8,10},{9,11},{10,... | collective-permute-start | bytes 294920 | tf_op jit(solution)/shard_map/ppermute | solution.py:360
  78.0 6.3 %collective-permute-start.15 = (f32[96,256]{1,0:T(8,128)S(1)}, f32[96,256]{1,0:T(8,128)S(1)}, u32[]{:S(2)}, u32[]{:S(2)}) collective-permute-start(f32[96,256]{1,0:T(8,128)S(1)} %add.27), channel_id=1, source_target_pairs={{0,4},{4,0},{8,12},{12,8},{1,5},{5,1},{9,13},{13,9},{2,6},{6,2},{1... | collective-permute-start | bytes 294920 | tf_op jit(solution)/shard_map/ppermute | solution.py:360
  85.3 1.8 %collective-permute-start.18 = (f32[384,256]{1,0:T(8,128)S(1)}, f32[384,256]{1,0:T(8,128)S(1)}, u32[]{:S(2)}, u32[]{:S(2)}) collective-permute-start(f32[384,256]{1,0:T(8,128)S(1)} %constant_dynamic-update-slice_fusion.first), channel_id=1, source_target_pairs={{0,1},{1,0},{2,3},{3,2},{4,5},{5,4},{6,7},{7,6},{8,9},{9,8},{10,11... | collective-permute-start | bytes 1179656 | tf_op jit(solution)/shard_map/ppermute | solution.py:360

commit v9 on v8

--- a/solution.py
+++ b/solution.py
@@ -10,7 +10,6 @@
 F32 = jnp.float32
 BF16 = jnp.bfloat16
 HBM = pl.BlockSpec(memory_space=pltpu.HBM)
-SMEM = pl.BlockSpec(memory_space=pltpu.SMEM)
 VMEM = pl.BlockSpec(memory_space=pltpu.VMEM)
 
 
@@ -91,6 +90,10 @@
     return jnp.where(row < limit, block, 0.0)
 
 
+def position():
+    return lax.axis_index("prow"), lax.axis_index("pcol")
+
+
 def limits(megabytes):
     return pltpu.CompilerParams(vmem_limit_bytes=megabytes * 2**20)
 
@@ -100,11 +103,11 @@
 
 
 def live_rows(at, n, which):
-    return at[2 + which]
+    return at[pl.ds(which, 1), :]
 
 
 def kept_rows(at, n, side, which):
-    return at[2 + which] * at[2 + n * n * (1 + side) + which]
+    return at[pl.ds(n * n * (1 + side) + which, 1), :]
 
 
 def masked(block, at, n, which):
@@ -151,7 +154,7 @@
 
 
 def left_term(n, a, at, known, two, one):
-    row, col = at[0], at[1]
+    row, col = position()
     rows = jnp.concatenate([two, one], axis=0)
     rows = halves(masked(rows, at, n, row * n + (a ^ col)))
     tile = known[tile_rows(a, col, two.shape[0])]
@@ -174,7 +177,7 @@
     return pl.pallas_call(
         kernel,
         out_shape=out_shape,
-        in_specs=[SMEM] + [VMEM] * (len(arrays) - 1),
+        in_specs=[VMEM] * len(arrays),
         out_specs=jax.tree.map(lambda _: VMEM, out_shape),
         scratch_shapes=scratch,
         compiler_params=limits(megabytes),
@@ -209,7 +212,7 @@
 
 
 def sums_kernel(n, m, at, left_high, left_low, arrived, *refs):
-    row, col = at[0], at[1]
+    row, col = position()
     width = arrived.shape[-1]
     high, low = refs[-2:] if len(refs) == 3 else refs[3:5]
     for e in range(2):
@@ -235,7 +238,7 @@
         for h in range(2):
             for s in range(3):
                 start = ((e >> 1) * 6 + h * 3 + s) * (width // 8)
-                part = total[pl.ds(s * width + eighth(at, e, h, width), width // 8)]
+                part = total[pl.ds(s * width + eighth(position(), e, h, width), width // 8)]
                 (send if e & 1 else keep)[start : start + width // 8] = part
 
 
@@ -260,9 +263,9 @@
     )
 
 
-def band_kernel(n, first, arrivals, at, known, *refs):
+def band_kernel(n, first, arrivals, known, *refs):
     right, before, out = refs[: 2 * len(arrivals)], refs[2 * len(arrivals) : -1], refs[-1]
-    row, col = at[0], at[1]
+    row, col = position()
     width = right[0].shape[0] // 2
     for i in range(n // 2):
         tile = tile_rows(first + 2 * i, col, width)
@@ -277,20 +280,20 @@
         out[i] = functools.reduce(jnp.add, [ref[i] for ref in before] + terms)
 
 
-def band_product(n, first, arrivals, at, known, right, *before):
+def band_product(n, first, arrivals, known, right, *before):
     rows, span = known.shape
     width = rows // n
     right = [half for m in arrivals for half in right[2 * m : 2 * m + 2]]
     return call(
         functools.partial(band_kernel, n, first, arrivals), "band_product", 14,
         cost(3 * len(arrivals) * rows * span * width, len(arrivals) * rows * span),
-        jax.ShapeDtypeStruct((n // 2, width, 2 * width), F32), at, known, *right, *before,
+        jax.ShapeDtypeStruct((n // 2, width, 2 * width), F32), known, *right, *before,
     )
 
 
 def column_kernel(n, at, keep, got, other, top, two, one):
     width = top.shape[0]
-    limit = live_rows(at, n, at[0] * n + at[1])
+    limit = live_rows(at, n, position()[0] * n + position()[1])
     total = keep[0] + got[0] + other[...]
     column_two = keep_rows(-total[:, :width], limit)
     two[...] = column_two
@@ -303,21 +306,21 @@
     return pl.pallas_call(
         functools.partial(column_kernel, n),
         out_shape=(shape, shape),
-        in_specs=[SMEM] + [VMEM] * 4,
+        in_specs=[VMEM] * 5,
         out_specs=(VMEM, VMEM),
         compiler_params=limits(8),
         name="column_rows",
     )(at, keep, got, other, top)
 
 
-def blocks_kernel(n, at, top, inner_two, inner_one, first, second, diag_two, cross, diag_one, sums):
+def blocks_kernel(n, top, inner_two, inner_one, first, second, diag_two, cross, diag_one, sums):
     width = top.shape[0]
     for e in range(n):
         for h in range(2):
             for s in range(3):
                 start = ((e >> 1) * 6 + h * 3 + s) * (width // 8)
                 part = (second if e & 1 else first)[start : start + width // 8]
-                sums[s, pl.ds(eighth(at, e, h, width), width // 8)] = part
+                sums[s, pl.ds(eighth(position(), e, h, width), width // 8)] = part
     t = halves(top[...])
     d = inner_two[...] + sums[0]
     diag_two[...] = d
@@ -331,17 +334,17 @@
     )
 
 
-def small_blocks(n, at, top, inner_two, inner_one, parts):
+def small_blocks(n, top, inner_two, inner_one, parts):
     shape = jax.ShapeDtypeStruct(top.shape, F32)
     return pl.pallas_call(
         functools.partial(blocks_kernel, n),
         out_shape=(shape, shape, shape),
-        in_specs=[SMEM] + [VMEM] * 5,
+        in_specs=[VMEM] * 5,
         out_specs=(VMEM,) * 3,
         scratch_shapes=[pltpu.VMEM((3,) + top.shape, F32)],
         compiler_params=limits(8),
         name="small_blocks",
-    )(at, top, inner_two, inner_one, *parts)
+    )(top, inner_two, inner_one, *parts)
 
 
 def after(value, *others):
@@ -353,8 +356,8 @@
 ):
     n = lax.axis_size("pcol")
     width = top_one.shape[0]
-    place = jnp.stack([lax.axis_index("prow"), lax.axis_index("pcol")]).astype(jnp.int32)
-    at = jnp.concatenate([place, heights, pattern_two, pattern_one])
+    rows = jnp.concatenate([heights, heights * pattern_two, heights * pattern_one])
+    at = jnp.broadcast_to(rows[:, None], (rows.shape[0], top_one.shape[1]))
 
     def along(axis, k, array):
         return lax.ppermute(array, axis, [(i, i ^ k) for i in range(n)])
@@ -380,15 +383,15 @@
     total, *early = first_sums(n, at, left, gathered[FIRST_ARRIVAL])
     early = {FIRST_ARRIVAL: early}
     partial = [
-        band_product(n, 1, (FIRST_ARRIVAL,), at, known, (*early[FIRST_ARRIVAL],) * 2)
+        band_product(n, 1, (FIRST_ARRIVAL,), known, (*early[FIRST_ARRIVAL],) * 2)
     ]
     keep_sums, send_sums, *late = last_sums(
         n, after(at, *partial), left, gathered[1 - FIRST_ARRIVAL], total
     )
     right = [half for m in range(2) for half in early.get(m, late)]
     mine = keep_sums + core(send_sums)
-    send = band_product(n, 1, (1 - FIRST_ARRIVAL,), after(at, send_sums), known, right, *partial[:1])
-    keep = band_product(n, 0, (0, 1), after(at, send), known, right)
+    send = band_product(n, 1, (1 - FIRST_ARRIVAL,), after(known, send_sums), right, *partial[:1])
+    keep = band_product(n, 0, (0, 1), after(known, send), right)
     got = core(after(send, mine))
     own, beyond, beside, corner = jnp.split(mine, 4)
     mine = (own + opposite(corner)) + (across(beside) + along("prow", 1, beyond))
@@ -398,7 +401,7 @@
     both = [mine, along("prow", 1, mine), across(mine), opposite(mine)]
     both = jnp.concatenate([after(both[0], other)] + both[1:])
     both = both, core(both)
-    diag_two, cross_block, diag_one = small_blocks(n, at, top_one, inner_two, inner_one, both)
+    diag_two, cross_block, diag_one = small_blocks(n, top_one, inner_two, inner_one, both)
     return (column_two, diag_two, column_one, cross_block, diag_one)
 
 

time: 89.3 us -> 88.5 us (level)
  Pallas kernels: 18.4 us -> 12.9 us
  starting transfers between devices: 28 us -> 30 us
  waiting for transfers between devices: 38.7 us -> 40.7 us
  other arithmetic: 0.17 us -> 1.59 us
    pallas_call x7, Pallas kernels: 13.8 us -> 9.4 us  [call(): pl.pallas_call(kernel, out_shape=out_shape, in_specs=[VMEM] * len(arrays)...]
    ppermute x15, starting transfers between devices: 22 us -> 24.4 us  [along(): return lax.ppermute(array, axis, [(i, i ^ k) for i in range(n)])]
    ppermute x15, waiting for transfers between devices: 37.4 us -> 39.4 us  [along(): return lax.ppermute(array, axis, [(i, i ^ k) for i in range(n)])]
  transfers between devices with their start and end apart: 19 -> 19, of which waited for: 11 -> 12; matrix products, arithmetic and copies ran while one was open for 1% -> 2% of each run, Pallas kernels for 17% -> 12%
where the time goes in v9:
time: 88.5 us; the launch traced here: 88.3 us
  waiting for transfers between devices  40.7 us (46%)
  starting transfers between devices  30 us (34%)
  Pallas kernels  12.9 us (15%)
  local copies, waits for them, and re-layouts  2.34 us (3%)
  other arithmetic  1.59 us (2%)
    ppermute x15, waiting for transfers between devices, along(): return lax.ppermute(array, axis, [(i, i ^ k) for i in range(n)])  39.4 us
    ppermute x15, starting transfers between devices, along(): return lax.ppermute(array, axis, [(i, i ^ k) for i in range(n)])  24.4 us
    pallas_call x7, Pallas kernels, call(): pl.pallas_call(kernel, out_shape=out_shape, in_specs=[VMEM] * len(arrays)...  9.4 us
    ppermute x2, starting transfers between devices, direct(): return lax.ppermute(rows, ('prow', 'pcol'), pairs)  4.73 us
    unnamed x13, local copies, waits for them, and re-layouts  2.24 us
  transfers between devices with their start and end apart: 19, of which 12 were waited for; matrix products, arithmetic and copies ran while one was open for 2% of the time, Pallas kernels for 12%

profile of v9, /device:TPU:0, one launch (start us, length us, event | category | flops | bytes accessed | tf_op | source)
XLA Modules:
  0.0 88.3 jit_solution(7126027650036670645)
XLA Ops:
  1.2 1.0 %stack_rows.2.refs_0_ = f32[512,256]{1,0:T(8,128)S(1)} custom-call(f32[256,256]{1,0:T(8,128)} %refs_0_.1, f32[256,256]{1,0:T(8,128)} %refs_1_.1), custom_call_target="tpu_custom_call" | custom-call | bytes 1048576 | tf_op jit(solution)/shard_map/stack_rows/pallas_call | solution.py:144
  3.0 4.0 %collective-permute-start.6 = (f32[1024,256]{1,0:T(8,128)S(1)}, f32[1024,256]{1,0:T(8,128)S(1)}, u32[]{:S(2)}, u32[]{:S(2)}) collective-permute-start(f32[1024,256]{1,0:T(8,128)S(1)} %stack_rows.3.here), channel_id=1, source_target_pairs={{0,8},{1,12},{2,0},{3,4},{4,9},{5,13},{6,1},{7,5},{8,10},{9,14},{1... | collective-permute-start | bytes 3145736 | tf_op jit(solution)/shard_map/ppermute | solution.py:374
  7.0 0.7 collective-permute-start.7
  7.7 4.2 %collective-permute-start = (f32[256,256]{1,0:T(8,128)}, f32[256,256]{1,0:T(8,128)S(1)}, u32[]{:S(2)}, u32[]{:S(2)}) collective-permute-start(f32[256,256]{1,0:T(8,128)} %refs_0_.1), channel_id=1, source_target_pairs={{0,2},{1,3},{2,0},{3,1},{4,6},{5,7},{6,4},{7,5},{8,10},{9,11},{10,... | collective-permute-start | bytes 786440 | tf_op jit(solution)/shard_map/ppermute | solution.py:363
  12.0 0.7 fusion.3
  12.7 0.7 pad_add_fusion
  13.5 2.2 %copy-done = f32[1024,1024]{1,0:T(8,128)S(1)} copy-done((f32[1024,1024]{1,0:T(8,128)S(1)}, f32[1024,1024]{1,0:T(8,128)}, u32[]{:S(2)}) %copy-start) | copy-done | bytes 4194328
  15.7 1.8 %left_first.1.before = f32[512,1024]{1,0:T(8,128)S(1)} custom-call(s32[48,256]{1,0:T(8,128)S(1)} %broadcast_in_dim.2.at, f32[1024,1024]{1,0:T(8,128)S(1)} %copy-done, f32[1024,256]{1,0:T(8,128)S(1)} %stack_rows.3.here), custom_call_target="tpu_custom_call" | custom-call | tf_op jit(solution)/shard_map/left_first/pallas_call | solution.py:177
  17.6 23.6 %collective-permute-done.1.one = f32[256,256]{1,0:T(8,128)S(1)} collective-permute-done((f32[256,256]{1,0:T(8,128)}, f32[256,256]{1,0:T(8,128)S(1)}, u32[]{:S(2)}, u32[]{:S(2)}) %collective-permute-start.1) | collective-permute-done | bytes 262176 | tf_op jit(solution)/shard_map/ppermute | solution.py:363
  41.7 1.0 %collective-permute-done.4.core_two = f32[256,256]{1,0:T(8,128)S(1)} collective-permute-done((f32[256,256]{1,0:T(8,128)S(1)}, f32[256,256]{1,0:T(8,128)S(1)}, u32[]{:S(2)}, u32[]{:S(2)}) %collective-permute-start.4) | collective-permute-done | bytes 262176 | tf_op jit(solution)/shard_map/ppermute | solution.py:363
  43.1 1.9 %left_last.1 = (bf16[512,1024]{1,0:T(8,128)(2,1)S(1)}, bf16[512,1024]{1,0:T(8,128)(2,1)S(1)}) custom-call(s32[48,256]{1,0:T(8,128)S(1)} %broadcast_in_dim.2.at, f32[1024,1024]{1,0:T(8,128)S(1)} %copy-done.1, f32[256,256]{1,0:T(8,128)S(1)} %collective-permute-done.two, f32[256,256]{1,0:T(8,128)S(1)} %collective-permute-done.1.one, ...), custom_call_target="tpu_custom_call" | custom-call | tf_op jit(solution)/shard_map/left_last/pallas_call | solution.py:177
  45.0 0.9 %first_sums.1 = (f32[768,256]{1,0:T(8,128)S(1)}, bf16[512,512]{1,0:T(8,128)(2,1)S(1)}, bf16[512,512]{1,0:T(8,128)(2,1)S(1)}) custom-call(s32[48,256]{1,0:T(8,128)S(1)} %broadcast_in_dim.2.at, bf16[512,1024]{1,0:T(8,128)(2,1)S(1)} %get-tuple-element.29.left_high, bf16[512,1024]{1,0:T(8,128)(2,1)S(1)} %get-tuple-element.30.left_low, ...), custom_call_target="tpu_custom_call" | custom-call | flops 603979776 | tf_op jit(solution)/shard_map/first_sums/pallas_call | solution.py:177
  46.0 1.0 %band_product.3.refs_2_ = f32[2,256,512]{2,1,0:T(8,128)S(1)} custom-call(f32[1024,1024]{1,0:T(8,128)S(1)} %copy-done.1, bf16[512,512]{1,0:T(8,128)(2,1)S(1)} %get-tuple-element.31.refs_0_.refs_2_, bf16[512,512]{1,0:T(8,128)(2,1)S(1)} %get-tuple-element.32.refs_1_.refs_3_), custom_call_target="tpu_custom_call" | custom-call | flops 805306368 | bytes 1048576 | tf_op jit(solution)/shard_map/band_product/pallas_call | solution.py:177
  47.0 1.0 %last_sums.1 = (f32[384,256]{1,0:T(8,128)S(1)}, f32[384,256]{1,0:T(8,128)S(1)}, bf16[512,512]{1,0:T(8,128)(2,1)S(1)}, bf16[512,512]{1,0:T(8,128)(2,1)S(1)}) custom-call(s32[48,256]{1,0:T(8,128)S(1)} %broadcast_in_dim.2.at, bf16[512,1024]{1,0:T(8,128)(2,1)S(1)} %get-tuple-element.29.left_high, bf16[512,1024]{1,0:T(8,128)(2,1)S(1)} %get-tuple-element.30.left_low, ...), custom_call_target="tpu_custom_call" | custom-call | flops 603979776 | tf_op jit(solution)/shard_map/last_sums/pallas_call | solution.py:177
  48.1 1.0 %band_product.4 = f32[2,256,512]{2,1,0:T(8,128)S(1)} custom-call(f32[1024,1024]{1,0:T(8,128)S(1)} %copy-done.1, bf16[512,512]{1,0:T(8,128)(2,1)S(1)} %get-tuple-element.37.refs_0_, bf16[512,512]{1,0:T(8,128)(2,1)S(1)} %get-tuple-element.38.refs_1_, f32[2,256,512]{2,1,0:T(8,128)S(1)} %band_product.3.refs_2_), custom_call_target="tpu_custom_call" | custom-call | flops 805306368 | bytes 1048576 | tf_op jit(solution)/shard_map/band_product/pallas_call | solution.py:177
  49.1 0.6 collective-permute-done.8
  50.0 8.4 %collective-permute-start.12 = (f32[96,256]{1,0:T(8,128)S(1)}, f32[96,256]{1,0:T(8,128)S(1)}, u32[]{:S(2)}, u32[]{:S(2)}) collective-permute-start(f32[96,256]{1,0:T(8,128)S(1)} %get-tuple-element.49), channel_id=1, source_target_pairs={{0,4},{4,0},{8,12},{12,8},{1,5},{5,1},{9,13},{13,9},{2,6},{6,2},{1... | collective-permute-start | bytes 294920 | tf_op jit(solution)/shard_map/ppermute | solution.py:363
  58.4 3.7 %collective-permute-start.11 = (f32[96,256]{1,0:T(8,128)S(1)}, f32[96,256]{1,0:T(8,128)S(1)}, u32[]{:S(2)}, u32[]{:S(2)}) collective-permute-start(f32[96,256]{1,0:T(8,128)S(1)} %get-tuple-element.50), channel_id=1, source_target_pairs={{0,2},{1,3},{2,0},{3,1},{4,6},{5,7},{6,4},{7,5},{8,10},{9,11},{10,... | collective-permute-start | bytes 294920 | tf_op jit(solution)/shard_map/ppermute | solution.py:363
  62.0 0.6 collective-permute-start.10
  62.6 1.8 %band_product.5.keep = f32[2,256,512]{2,1,0:T(8,128)S(1)} custom-call(f32[1024,1024]{1,0:T(8,128)S(1)} %copy-done.1, bf16[512,512]{1,0:T(8,128)(2,1)S(1)} %get-tuple-element.37.refs_0_, bf16[512,512]{1,0:T(8,128)(2,1)S(1)} %get-tuple-element.38.refs_1_, bf16[512,512]{1,0:T(8,128)(2,1)S(1)} %get-tuple-element.31.refs_0_.refs_2_, ...), custom_call_target="tpu_custom_call" | custom-call | flops 1610612736 | bytes 2097152 | tf_op jit(solution)/shard_map/band_product/pallas_call | solution.py:177
  64.4 2.0 %collective-permute-done.11 = f32[96,256]{1,0:T(8,128)S(1)} collective-permute-done((f32[96,256]{1,0:T(8,128)S(1)}, f32[96,256]{1,0:T(8,128)S(1)}, u32[]{:S(2)}, u32[]{:S(2)}) %collective-permute-start.11) | collective-permute-done | bytes 98336 | tf_op jit(solution)/shard_map/ppermute | solution.py:363
  66.4 1.3 %collective-permute-done.10 = f32[96,256]{1,0:T(8,128)S(1)} collective-permute-done((f32[96,256]{1,0:T(8,128)S(1)}, f32[96,256]{1,0:T(8,128)S(1)}, u32[]{:S(2)}, u32[]{:S(2)}) %collective-permute-start.10) | collective-permute-done | bytes 98336 | tf_op jit(solution)/shard_map/ppermute | solution.py:370
  67.8 1.3 %collective-permute-start.13 = (f32[256,512]{1,0:T(8,128)S(1)}, f32[256,512]{1,0:T(8,128)S(1)}, u32[]{:S(2)}, u32[]{:S(2)}) collective-permute-start(f32[256,512]{1,0:T(8,128)S(1)} %fusion), channel_id=1, source_target_pairs={{0,2},{1,3},{2,0},{3,1},{4,6},{5,7},{6,4},{7,5},{8,10},{9,11},{10,... | collective-permute-start | bytes 1572872 | tf_op jit(solution)/shard_map/ppermute | solution.py:363
  69.1 2.0 %collective-permute-start.14 = (f32[96,256]{1,0:T(8,128)S(1)}, f32[96,256]{1,0:T(8,128)S(1)}, u32[]{:S(2)}, u32[]{:S(2)}) collective-permute-start(f32[96,256]{1,0:T(8,128)S(1)} %fusion.1), channel_id=1, source_target_pairs={{0,8},{4,12},{8,0},{12,4},{1,9},{5,13},{9,1},{13,5},{2,10},{6,14},... | collective-permute-start | bytes 294920 | tf_op jit(solution)/shard_map/ppermute | solution.py:363
  71.1 4.7 %collective-permute-done.14 = f32[96,256]{1,0:T(8,128)S(1)} collective-permute-done((f32[96,256]{1,0:T(8,128)S(1)}, f32[96,256]{1,0:T(8,128)S(1)}, u32[]{:S(2)}, u32[]{:S(2)}) %collective-permute-start.14) | collective-permute-done | bytes 98336 | tf_op jit(solution)/shard_map/ppermute | solution.py:363
  76.1 1.3 %collective-permute-start.16 = (f32[96,256]{1,0:T(8,128)S(1)}, f32[96,256]{1,0:T(8,128)S(1)}, u32[]{:S(2)}, u32[]{:S(2)}) collective-permute-start(f32[96,256]{1,0:T(8,128)S(1)} %add.27), channel_id=1, source_target_pairs={{0,2},{1,3},{2,0},{3,1},{4,6},{5,7},{6,4},{7,5},{8,10},{9,11},{10,... | collective-permute-start | bytes 294920 | tf_op jit(solution)/shard_map/ppermute | solution.py:363
  77.4 2.0 %collective-permute-start.15 = (f32[96,256]{1,0:T(8,128)S(1)}, f32[96,256]{1,0:T(8,128)S(1)}, u32[]{:S(2)}, u32[]{:S(2)}) collective-permute-start(f32[96,256]{1,0:T(8,128)S(1)} %add.27), channel_id=1, source_target_pairs={{0,4},{4,0},{8,12},{12,8},{1,5},{5,1},{9,13},{13,9},{2,6},{6,2},{1... | collective-permute-start | bytes 294920 | tf_op jit(solution)/shard_map/ppermute | solution.py:363
  79.3 4.8 %collective-permute-done.13.other = f32[256,512]{1,0:T(8,128)S(1)} collective-permute-done((f32[256,512]{1,0:T(8,128)S(1)}, f32[256,512]{1,0:T(8,128)S(1)}, u32[]{:S(2)}, u32[]{:S(2)}) %collective-permute-start.13) | collective-permute-done | bytes 524320 | tf_op jit(solution)/shard_map/ppermute | solution.py:363
  84.1 1.0 %collective-permute-done.16 = f32[96,256]{1,0:T(8,128)S(1)} collective-permute-done((f32[96,256]{1,0:T(8,128)S(1)}, f32[96,256]{1,0:T(8,128)S(1)}, u32[]{:S(2)}, u32[]{:S(2)}) %collective-permute-start.16) | collective-permute-done | bytes 98336 | tf_op jit(solution)/shard_map/ppermute | solution.py:363
  85.3 1.0 %column_rows.1 = (f32[256,256]{1,0:T(8,128)}, f32[256,256]{1,0:T(8,128)}) custom-call(s32[48,256]{1,0:T(8,128)S(1)} %broadcast_in_dim.2.at, f32[2,256,512]{2,1,0:T(8,128)S(1)} %band_product.5.keep, f32[2,256,512]{2,1,0:T(8,128)S(1)} %collective-permute-done.9.got, f32[256,512]{1,0:T(8,128)S(1)} %collective-permute-done.13.other, f32[256,256]{1,0:T(8,128)S(1)} %copy-done.2), custom_call_target="tpu_custom_call" | custom-call | tf_op jit(solution)/shard_map/column_rows/pallas_call | solution.py:306
  86.3 0.7 collective-permute-done.18.second
  87.0 1.4 %small_blocks.1 = (f32[256,256]{1,0:T(8,128)}, f32[256,256]{1,0:T(8,128)}, f32[256,256]{1,0:T(8,128)}) custom-call(f32[256,256]{1,0:T(8,128)S(1)} %copy-done.2, f32[256,256]{1,0:T(8,128)S(1)} %copy-done.3, f32[256,256]{1,0:T(8,128)S(1)} %copy-done.4, f32[384,256]{1,0:T(8,128)S(1)} %constant_dynamic-update-slice_fusion.first, ...), custom_call_target="tpu_custom_call" | custom-call | tf_op jit(solution)/shard_map/small_blocks/pallas_call | solution.py:339
  (39 shorter events, 3.4 us)
Async XLA Ops:
  0.6 1.9 %collective-permute-start.2 = (f32[256,256]{1,0:T(8,128)}, f32[256,256]{1,0:T(8,128)S(1)}, u32[]{:S(2)}, u32[]{:S(2)}) collective-permute-start(f32[256,256]{1,0:T(8,128)} %refs_0_.1), channel_id=1, source_target_pairs={{0,1},{1,0},{2,3},{3,2},{4,5},{5,4},{6,7},{7,6},{8,9},{9,8},{10,11... | collective-permute-start | bytes 786440 | tf_op jit(solution)/shard_map/ppermute | solution.py:363
  1.1 1.7 %collective-permute-start.3 = (f32[256,256]{1,0:T(8,128)}, f32[256,256]{1,0:T(8,128)S(1)}, u32[]{:S(2)}, u32[]{:S(2)}) collective-permute-start(f32[256,256]{1,0:T(8,128)} %refs_1_.1), channel_id=1, source_target_pairs={{0,1},{1,0},{2,3},{3,2},{4,5},{5,4},{6,7},{7,6},{8,9},{9,8},{10,11... | collective-permute-start | bytes 786440 | tf_op jit(solution)/shard_map/ppermute | solution.py:363
  3.0 42.0 %collective-permute-start.6 = (f32[1024,256]{1,0:T(8,128)S(1)}, f32[1024,256]{1,0:T(8,128)S(1)}, u32[]{:S(2)}, u32[]{:S(2)}) collective-permute-start(f32[1024,256]{1,0:T(8,128)S(1)} %stack_rows.3.here), channel_id=1, source_target_pairs={{0,8},{1,12},{2,0},{3,4},{4,9},{5,13},{6,1},{7,5},{8,10},{9,14},{1... | collective-permute-start | bytes 3145736 | tf_op jit(solution)/shard_map/ppermute | solution.py:374
  7.0 39.9 %collective-permute-start.7 = (f32[1024,256]{1,0:T(8,128)S(1)}, f32[1024,256]{1,0:T(8,128)S(1)}, u32[]{:S(2)}, u32[]{:S(2)}) collective-permute-start(f32[1024,256]{1,0:T(8,128)S(1)} %stack_rows.3.here), channel_id=1, source_target_pairs={{0,0},{1,4},{2,8},{3,12},{4,1},{5,5},{6,9},{7,13},{8,2},{9,6},{10,... | collective-permute-start | bytes 3145736 | tf_op jit(solution)/shard_map/ppermute | solution.py:374
  7.7 33.4 %collective-permute-start = (f32[256,256]{1,0:T(8,128)}, f32[256,256]{1,0:T(8,128)S(1)}, u32[]{:S(2)}, u32[]{:S(2)}) collective-permute-start(f32[256,256]{1,0:T(8,128)} %refs_0_.1), channel_id=1, source_target_pairs={{0,2},{1,3},{2,0},{3,1},{4,6},{5,7},{6,4},{7,5},{8,10},{9,11},{10,... | collective-permute-start | bytes 786440 | tf_op jit(solution)/shard_map/ppermute | solution.py:363
  11.9 29.2 %collective-permute-start.1 = (f32[256,256]{1,0:T(8,128)}, f32[256,256]{1,0:T(8,128)S(1)}, u32[]{:S(2)}, u32[]{:S(2)}) collective-permute-start(f32[256,256]{1,0:T(8,128)} %refs_1_.1), channel_id=1, source_target_pairs={{0,2},{1,3},{2,0},{3,1},{4,6},{5,7},{6,4},{7,5},{8,10},{9,11},{10,... | collective-permute-start | bytes 786440 | tf_op jit(solution)/shard_map/ppermute | solution.py:363
  13.5 2.2 %copy-start = (f32[1024,1024]{1,0:T(8,128)S(1)}, f32[1024,1024]{1,0:T(8,128)}, u32[]{:S(2)}) copy-start(f32[1024,1024]{1,0:T(8,128)} %known.7) | copy-start | bytes 12582916
  15.7 27.4 %copy-start.1 = (f32[1024,1024]{1,0:T(8,128)S(1)}, f32[1024,1024]{1,0:T(8,128)}, u32[]{:S(2)}) copy-start(f32[1024,1024]{1,0:T(8,128)} %known.7) | copy-start | bytes 12582916
  41.2 1.5 %collective-permute-start.4 = (f32[256,256]{1,0:T(8,128)S(1)}, f32[256,256]{1,0:T(8,128)S(1)}, u32[]{:S(2)}, u32[]{:S(2)}) collective-permute-start(f32[256,256]{1,0:T(8,128)S(1)} %collective-permute-done.two), channel_id=1, source_target_pairs={{0,1},{1,0},{2,3},{3,2},{4,5},{5,4},{6,7},{7,6},{8,9},{9,8},{10,11... | collective-permute-start | bytes 786440 | tf_op jit(solution)/shard_map/ppermute | solution.py:363
  41.2 1.9 %collective-permute-start.5 = (f32[256,256]{1,0:T(8,128)S(1)}, f32[256,256]{1,0:T(8,128)S(1)}, u32[]{:S(2)}, u32[]{:S(2)}) collective-permute-start(f32[256,256]{1,0:T(8,128)S(1)} %collective-permute-done.1.one), channel_id=1, source_target_pairs={{0,1},{1,0},{2,3},{3,2},{4,5},{5,4},{6,7},{7,6},{8,9},{9,8},{10,11... | collective-permute-start | bytes 786440 | tf_op jit(solution)/shard_map/ppermute | solution.py:363
  47.9 1.8 %collective-permute-start.8 = (f32[384,256]{1,0:T(8,128)S(1)}, f32[384,256]{1,0:T(8,128)S(1)}, u32[]{:S(2)}, u32[]{:S(2)}) collective-permute-start(f32[384,256]{1,0:T(8,128)S(1)} %get-tuple-element.35), channel_id=1, source_target_pairs={{0,1},{1,0},{2,3},{3,2},{4,5},{5,4},{6,7},{7,6},{8,9},{9,8},{10,11... | collective-permute-start | bytes 1179656 | tf_op jit(solution)/shard_map/ppermute | solution.py:363
  49.8 18.0 %collective-permute-start.9 = (f32[2,256,512]{2,1,0:T(8,128)S(1)}, f32[2,256,512]{2,1,0:T(8,128)S(1)}, u32[]{:S(2)}, u32[]{:S(2)}) collective-permute-start(f32[2,256,512]{2,1,0:T(8,128)S(1)} %band_product.4), channel_id=1, source_target_pairs={{0,1},{1,0},{2,3},{3,2},{4,5},{5,4},{6,7},{7,6},{8,9},{9,8},{10,11... | collective-permute-start | bytes 3145736 | tf_op jit(solution)/shard_map/ppermute | solution.py:363
  50.0 14.4 %collective-permute-start.12 = (f32[96,256]{1,0:T(8,128)S(1)}, f32[96,256]{1,0:T(8,128)S(1)}, u32[]{:S(2)}, u32[]{:S(2)}) collective-permute-start(f32[96,256]{1,0:T(8,128)S(1)} %get-tuple-element.49), channel_id=1, source_target_pairs={{0,4},{4,0},{8,12},{12,8},{1,5},{5,1},{9,13},{13,9},{2,6},{6,2},{1... | collective-permute-start | bytes 294920 | tf_op jit(solution)/shard_map/ppermute | solution.py:363
  58.4 8.1 %collective-permute-start.11 = (f32[96,256]{1,0:T(8,128)S(1)}, f32[96,256]{1,0:T(8,128)S(1)}, u32[]{:S(2)}, u32[]{:S(2)}) collective-permute-start(f32[96,256]{1,0:T(8,128)S(1)} %get-tuple-element.50), channel_id=1, source_target_pairs={{0,2},{1,3},{2,0},{3,1},{4,6},{5,7},{6,4},{7,5},{8,10},{9,11},{10,... | collective-permute-start | bytes 294920 | tf_op jit(solution)/shard_map/ppermute | solution.py:363
  62.0 23.3 %copy-start.2 = (f32[256,256]{1,0:T(8,128)S(1)}, f32[256,256]{1,0:T(8,128)}, u32[]{:S(2)}) copy-start(f32[256,256]{1,0:T(8,128)} %top.3) | copy-start | bytes 786436
  62.0 5.7 %collective-permute-start.10 = (f32[96,256]{1,0:T(8,128)S(1)}, f32[96,256]{1,0:T(8,128)S(1)}, u32[]{:S(2)}, u32[]{:S(2)}) collective-permute-start(f32[96,256]{1,0:T(8,128)S(1)} %get-tuple-element.51), channel_id=1, source_target_pairs={{0,6},{1,7},{2,4},{3,5},{4,2},{5,3},{6,0},{7,1},{8,14},{9,15},{10,... | collective-permute-start | bytes 294920 | tf_op jit(solution)/shard_map/ppermute | solution.py:370
  64.4 22.6 %copy-start.3 = (f32[256,256]{1,0:T(8,128)S(1)}, f32[256,256]{1,0:T(8,128)}, u32[]{:S(2)}) copy-start(f32[256,256]{1,0:T(8,128)} %inner_two.1) | copy-start | bytes 786436
  64.4 22.6 %copy-start.4 = (f32[256,256]{1,0:T(8,128)S(1)}, f32[256,256]{1,0:T(8,128)}, u32[]{:S(2)}) copy-start(f32[256,256]{1,0:T(8,128)} %inner_one.1) | copy-start | bytes 786436
  67.8 16.3 %collective-permute-start.13 = (f32[256,512]{1,0:T(8,128)S(1)}, f32[256,512]{1,0:T(8,128)S(1)}, u32[]{:S(2)}, u32[]{:S(2)}) collective-permute-start(f32[256,512]{1,0:T(8,128)S(1)} %fusion), channel_id=1, source_target_pairs={{0,2},{1,3},{2,0},{3,1},{4,6},{5,7},{6,4},{7,5},{8,10},{9,11},{10,... | collective-permute-start | bytes 1572872 | tf_op jit(solution)/shard_map/ppermute | solution.py:363
  69.1 6.7 %collective-permute-start.14 = (f32[96,256]{1,0:T(8,128)S(1)}, f32[96,256]{1,0:T(8,128)S(1)}, u32[]{:S(2)}, u32[]{:S(2)}) collective-permute-start(f32[96,256]{1,0:T(8,128)S(1)} %fusion.1), channel_id=1, source_target_pairs={{0,8},{4,12},{8,0},{12,4},{1,9},{5,13},{9,1},{13,5},{2,10},{6,14},... | collective-permute-start | bytes 294920 | tf_op jit(solution)/shard_map/ppermute | solution.py:363
  75.8 9.4 %collective-permute-start.17 = (f32[96,256]{1,0:T(8,128)S(1)}, f32[96,256]{1,0:T(8,128)S(1)}, u32[]{:S(2)}, u32[]{:S(2)}) collective-permute-start(f32[96,256]{1,0:T(8,128)S(1)} %add.27), channel_id=1, source_target_pairs={{0,6},{1,7},{2,4},{3,5},{4,2},{5,3},{6,0},{7,1},{8,14},{9,15},{10,... | collective-permute-start | bytes 294920 | tf_op jit(solution)/shard_map/ppermute | solution.py:370
  76.1 9.1 %collective-permute-start.16 = (f32[96,256]{1,0:T(8,128)S(1)}, f32[96,256]{1,0:T(8,128)S(1)}, u32[]{:S(2)}, u32[]{:S(2)}) collective-permute-start(f32[96,256]{1,0:T(8,128)S(1)} %add.27), channel_id=1, source_target_pairs={{0,2},{1,3},{2,0},{3,1},{4,6},{5,7},{6,4},{7,5},{8,10},{9,11},{10,... | collective-permute-start | bytes 294920 | tf_op jit(solution)/shard_map/ppermute | solution.py:363
  77.4 6.7 %collective-permute-start.15 = (f32[96,256]{1,0:T(8,128)S(1)}, f32[96,256]{1,0:T(8,128)S(1)}, u32[]{:S(2)}, u32[]{:S(2)}) collective-permute-start(f32[96,256]{1,0:T(8,128)S(1)} %add.27), channel_id=1, source_target_pairs={{0,4},{4,0},{8,12},{12,8},{1,5},{5,1},{9,13},{13,9},{2,6},{6,2},{1... | collective-permute-start | bytes 294920 | tf_op jit(solution)/shard_map/ppermute | solution.py:363
  85.2 1.8 %collective-permute-start.18 = (f32[384,256]{1,0:T(8,128)S(1)}, f32[384,256]{1,0:T(8,128)S(1)}, u32[]{:S(2)}, u32[]{:S(2)}) collective-permute-start(f32[384,256]{1,0:T(8,128)S(1)} %constant_dynamic-update-slice_fusion.first), channel_id=1, source_target_pairs={{0,1},{1,0},{2,3},{3,2},{4,5},{5,4},{6,7},{7,6},{8,9},{9,8},{10,11... | collective-permute-start | bytes 1179656 | tf_op jit(solution)/shard_map/ppermute | solution.py:363

commit v10 on v9

--- a/solution.py
+++ b/solution.py
@@ -313,7 +313,9 @@
     )(at, keep, got, other, top)
 
 
-def blocks_kernel(n, top, inner_two, inner_one, first, second, diag_two, cross, diag_one, sums):
+def blocks_kernel(n, top, inner_two, inner_one, first, second, *refs):
+    outs, (sums, blocks, sems) = refs[:3], refs[3:]
+    copies = [pltpu.make_async_copy(blocks.at[i], outs[i], sems.at[i]) for i in range(3)]
     width = top.shape[0]
     for e in range(n):
         for h in range(2):
@@ -323,15 +325,20 @@
                 sums[s, pl.ds(eighth(position(), e, h, width), width // 8)] = part
     t = halves(top[...])
     d = inner_two[...] + sums[0]
-    diag_two[...] = d
+    blocks[0] = d
+    copies[0].start()
     c = sums[1].T - dot3(halves(d), t, ROWS_BY_COLUMNS)
-    cross[...] = c
-    diag_one[...] = (
+    blocks[1] = c
+    copies[1].start()
+    blocks[2] = (
         inner_one[...]
         + sums[2]
         - dot3(halves(sums[1]), t, ROWS_BY_COLUMNS)
         - dot3(t, halves(c), ROWS_BY_ROWS)
     )
+    copies[2].start()
+    for copy in copies:
+        copy.wait()
 
 
 def small_blocks(n, top, inner_two, inner_one, parts):
@@ -340,8 +347,12 @@
         functools.partial(blocks_kernel, n),
         out_shape=(shape, shape, shape),
         in_specs=[VMEM] * 5,
-        out_specs=(VMEM,) * 3,
-        scratch_shapes=[pltpu.VMEM((3,) + top.shape, F32)],
+        out_specs=(HBM,) * 3,
+        scratch_shapes=[
+            pltpu.VMEM((3,) + top.shape, F32),
+            pltpu.VMEM((3,) + top.shape, F32),
+            pltpu.SemaphoreType.DMA((3,)),
+        ],
         compiler_params=limits(8),
         name="small_blocks",
     )(top, inner_two, inner_one, *parts)

time: 88.5 us -> 88.6 us (level)
  no operation moved by 1% of the time
where the time goes in v10:
time: 88.6 us; the launch traced here: 88.4 us
  waiting for transfers between devices  40.7 us (46%)
  starting transfers between devices  30 us (34%)
  Pallas kernels  13 us (15%)
  local copies, waits for them, and re-layouts  2.34 us (3%)
  other arithmetic  1.59 us (2%)
    ppermute x15, waiting for transfers between devices, along(): return lax.ppermute(array, axis, [(i, i ^ k) for i in range(n)])  39.4 us
    ppermute x15, starting transfers between devices, along(): return lax.ppermute(array, axis, [(i, i ^ k) for i in range(n)])  24.4 us
    pallas_call x7, Pallas kernels, call(): pl.pallas_call(kernel, out_shape=out_shape, in_specs=[VMEM] * len(arrays)...  9.4 us
    ppermute x2, starting transfers between devices, direct(): return lax.ppermute(rows, ('prow', 'pcol'), pairs)  4.73 us
    unnamed x13, local copies, waits for them, and re-layouts  2.24 us
  transfers between devices with their start and end apart: 19, of which 12 were waited for; matrix products, arithmetic and copies ran while one was open for 2% of the time, Pallas kernels for 12%

profile of v10, /device:TPU:0, one launch (start us, length us, event | category | flops | bytes accessed | tf_op | source)
XLA Modules:
  0.0 88.4 jit_solution(899947814897601810)
XLA Ops:
  1.2 1.0 %stack_rows.2.refs_0_ = f32[512,256]{1,0:T(8,128)S(1)} custom-call(f32[256,256]{1,0:T(8,128)} %refs_0_.1, f32[256,256]{1,0:T(8,128)} %refs_1_.1), custom_call_target="tpu_custom_call" | custom-call | bytes 1048576 | tf_op jit(solution)/shard_map/stack_rows/pallas_call | solution.py:144
  3.0 4.0 %collective-permute-start.6 = (f32[1024,256]{1,0:T(8,128)S(1)}, f32[1024,256]{1,0:T(8,128)S(1)}, u32[]{:S(2)}, u32[]{:S(2)}) collective-permute-start(f32[1024,256]{1,0:T(8,128)S(1)} %stack_rows.3.here), channel_id=1, source_target_pairs={{0,8},{1,12},{2,0},{3,4},{4,9},{5,13},{6,1},{7,5},{8,10},{9,14},{1... | collective-permute-start | bytes 3145736 | tf_op jit(solution)/shard_map/ppermute | solution.py:385
  7.0 0.7 collective-permute-start.7
  7.7 4.2 %collective-permute-start = (f32[256,256]{1,0:T(8,128)}, f32[256,256]{1,0:T(8,128)S(1)}, u32[]{:S(2)}, u32[]{:S(2)}) collective-permute-start(f32[256,256]{1,0:T(8,128)} %refs_0_.1), channel_id=1, source_target_pairs={{0,2},{1,3},{2,0},{3,1},{4,6},{5,7},{6,4},{7,5},{8,10},{9,11},{10,... | collective-permute-start | bytes 786440 | tf_op jit(solution)/shard_map/ppermute | solution.py:374
  12.0 0.7 fusion.3
  12.7 0.7 pad_add_fusion
  13.5 2.2 %copy-done = f32[1024,1024]{1,0:T(8,128)S(1)} copy-done((f32[1024,1024]{1,0:T(8,128)S(1)}, f32[1024,1024]{1,0:T(8,128)}, u32[]{:S(2)}) %copy-start) | copy-done | bytes 4194328
  15.7 1.8 %left_first.1.before = f32[512,1024]{1,0:T(8,128)S(1)} custom-call(s32[48,256]{1,0:T(8,128)S(1)} %broadcast_in_dim.2.at, f32[1024,1024]{1,0:T(8,128)S(1)} %copy-done, f32[1024,256]{1,0:T(8,128)S(1)} %stack_rows.3.here), custom_call_target="tpu_custom_call" | custom-call | tf_op jit(solution)/shard_map/left_first/pallas_call | solution.py:177
  17.6 23.6 %collective-permute-done.1.one = f32[256,256]{1,0:T(8,128)S(1)} collective-permute-done((f32[256,256]{1,0:T(8,128)}, f32[256,256]{1,0:T(8,128)S(1)}, u32[]{:S(2)}, u32[]{:S(2)}) %collective-permute-start.1) | collective-permute-done | bytes 262176 | tf_op jit(solution)/shard_map/ppermute | solution.py:374
  41.7 1.0 %collective-permute-done.4.core_two = f32[256,256]{1,0:T(8,128)S(1)} collective-permute-done((f32[256,256]{1,0:T(8,128)S(1)}, f32[256,256]{1,0:T(8,128)S(1)}, u32[]{:S(2)}, u32[]{:S(2)}) %collective-permute-start.4) | collective-permute-done | bytes 262176 | tf_op jit(solution)/shard_map/ppermute | solution.py:374
  43.1 1.9 %left_last.1 = (bf16[512,1024]{1,0:T(8,128)(2,1)S(1)}, bf16[512,1024]{1,0:T(8,128)(2,1)S(1)}) custom-call(s32[48,256]{1,0:T(8,128)S(1)} %broadcast_in_dim.2.at, f32[1024,1024]{1,0:T(8,128)S(1)} %copy-done.1, f32[256,256]{1,0:T(8,128)S(1)} %collective-permute-done.two, f32[256,256]{1,0:T(8,128)S(1)} %collective-permute-done.1.one, ...), custom_call_target="tpu_custom_call" | custom-call | tf_op jit(solution)/shard_map/left_last/pallas_call | solution.py:177
  45.0 0.9 %first_sums.1 = (f32[768,256]{1,0:T(8,128)S(1)}, bf16[512,512]{1,0:T(8,128)(2,1)S(1)}, bf16[512,512]{1,0:T(8,128)(2,1)S(1)}) custom-call(s32[48,256]{1,0:T(8,128)S(1)} %broadcast_in_dim.2.at, bf16[512,1024]{1,0:T(8,128)(2,1)S(1)} %get-tuple-element.29.left_high, bf16[512,1024]{1,0:T(8,128)(2,1)S(1)} %get-tuple-element.30.left_low, ...), custom_call_target="tpu_custom_call" | custom-call | flops 603979776 | tf_op jit(solution)/shard_map/first_sums/pallas_call | solution.py:177
  46.0 1.0 %band_product.3.refs_2_ = f32[2,256,512]{2,1,0:T(8,128)S(1)} custom-call(f32[1024,1024]{1,0:T(8,128)S(1)} %copy-done.1, bf16[512,512]{1,0:T(8,128)(2,1)S(1)} %get-tuple-element.31.refs_0_.refs_2_, bf16[512,512]{1,0:T(8,128)(2,1)S(1)} %get-tuple-element.32.refs_1_.refs_3_), custom_call_target="tpu_custom_call" | custom-call | flops 805306368 | bytes 1048576 | tf_op jit(solution)/shard_map/band_product/pallas_call | solution.py:177
  47.0 1.0 %last_sums.1 = (f32[384,256]{1,0:T(8,128)S(1)}, f32[384,256]{1,0:T(8,128)S(1)}, bf16[512,512]{1,0:T(8,128)(2,1)S(1)}, bf16[512,512]{1,0:T(8,128)(2,1)S(1)}) custom-call(s32[48,256]{1,0:T(8,128)S(1)} %broadcast_in_dim.2.at, bf16[512,1024]{1,0:T(8,128)(2,1)S(1)} %get-tuple-element.29.left_high, bf16[512,1024]{1,0:T(8,128)(2,1)S(1)} %get-tuple-element.30.left_low, ...), custom_call_target="tpu_custom_call" | custom-call | flops 603979776 | tf_op jit(solution)/shard_map/last_sums/pallas_call | solution.py:177
  48.1 1.0 %band_product.4 = f32[2,256,512]{2,1,0:T(8,128)S(1)} custom-call(f32[1024,1024]{1,0:T(8,128)S(1)} %copy-done.1, bf16[512,512]{1,0:T(8,128)(2,1)S(1)} %get-tuple-element.37.refs_0_, bf16[512,512]{1,0:T(8,128)(2,1)S(1)} %get-tuple-element.38.refs_1_, f32[2,256,512]{2,1,0:T(8,128)S(1)} %band_product.3.refs_2_), custom_call_target="tpu_custom_call" | custom-call | flops 805306368 | bytes 1048576 | tf_op jit(solution)/shard_map/band_product/pallas_call | solution.py:177
  49.1 0.6 collective-permute-done.8
  50.0 8.4 %collective-permute-start.12 = (f32[96,256]{1,0:T(8,128)S(1)}, f32[96,256]{1,0:T(8,128)S(1)}, u32[]{:S(2)}, u32[]{:S(2)}) collective-permute-start(f32[96,256]{1,0:T(8,128)S(1)} %get-tuple-element.49), channel_id=1, source_target_pairs={{0,4},{4,0},{8,12},{12,8},{1,5},{5,1},{9,13},{13,9},{2,6},{6,2},{1... | collective-permute-start | bytes 294920 | tf_op jit(solution)/shard_map/ppermute | solution.py:374
  58.4 3.7 %collective-permute-start.11 = (f32[96,256]{1,0:T(8,128)S(1)}, f32[96,256]{1,0:T(8,128)S(1)}, u32[]{:S(2)}, u32[]{:S(2)}) collective-permute-start(f32[96,256]{1,0:T(8,128)S(1)} %get-tuple-element.50), channel_id=1, source_target_pairs={{0,2},{1,3},{2,0},{3,1},{4,6},{5,7},{6,4},{7,5},{8,10},{9,11},{10,... | collective-permute-start | bytes 294920 | tf_op jit(solution)/shard_map/ppermute | solution.py:374
  62.0 0.6 collective-permute-start.10
  62.6 1.8 %band_product.5.keep = f32[2,256,512]{2,1,0:T(8,128)S(1)} custom-call(f32[1024,1024]{1,0:T(8,128)S(1)} %copy-done.1, bf16[512,512]{1,0:T(8,128)(2,1)S(1)} %get-tuple-element.37.refs_0_, bf16[512,512]{1,0:T(8,128)(2,1)S(1)} %get-tuple-element.38.refs_1_, bf16[512,512]{1,0:T(8,128)(2,1)S(1)} %get-tuple-element.31.refs_0_.refs_2_, ...), custom_call_target="tpu_custom_call" | custom-call | flops 1610612736 | bytes 2097152 | tf_op jit(solution)/shard_map/band_product/pallas_call | solution.py:177
  64.4 2.0 %collective-permute-done.11 = f32[96,256]{1,0:T(8,128)S(1)} collective-permute-done((f32[96,256]{1,0:T(8,128)S(1)}, f32[96,256]{1,0:T(8,128)S(1)}, u32[]{:S(2)}, u32[]{:S(2)}) %collective-permute-start.11) | collective-permute-done | bytes 98336 | tf_op jit(solution)/shard_map/ppermute | solution.py:374
  66.4 1.3 %collective-permute-done.10 = f32[96,256]{1,0:T(8,128)S(1)} collective-permute-done((f32[96,256]{1,0:T(8,128)S(1)}, f32[96,256]{1,0:T(8,128)S(1)}, u32[]{:S(2)}, u32[]{:S(2)}) %collective-permute-start.10) | collective-permute-done | bytes 98336 | tf_op jit(solution)/shard_map/ppermute | solution.py:381
  67.8 1.3 %collective-permute-start.13 = (f32[256,512]{1,0:T(8,128)S(1)}, f32[256,512]{1,0:T(8,128)S(1)}, u32[]{:S(2)}, u32[]{:S(2)}) collective-permute-start(f32[256,512]{1,0:T(8,128)S(1)} %fusion), channel_id=1, source_target_pairs={{0,2},{1,3},{2,0},{3,1},{4,6},{5,7},{6,4},{7,5},{8,10},{9,11},{10,... | collective-permute-start | bytes 1572872 | tf_op jit(solution)/shard_map/ppermute | solution.py:374
  69.1 2.0 %collective-permute-start.14 = (f32[96,256]{1,0:T(8,128)S(1)}, f32[96,256]{1,0:T(8,128)S(1)}, u32[]{:S(2)}, u32[]{:S(2)}) collective-permute-start(f32[96,256]{1,0:T(8,128)S(1)} %fusion.1), channel_id=1, source_target_pairs={{0,8},{4,12},{8,0},{12,4},{1,9},{5,13},{9,1},{13,5},{2,10},{6,14},... | collective-permute-start | bytes 294920 | tf_op jit(solution)/shard_map/ppermute | solution.py:374
  71.1 4.7 %collective-permute-done.14 = f32[96,256]{1,0:T(8,128)S(1)} collective-permute-done((f32[96,256]{1,0:T(8,128)S(1)}, f32[96,256]{1,0:T(8,128)S(1)}, u32[]{:S(2)}, u32[]{:S(2)}) %collective-permute-start.14) | collective-permute-done | bytes 98336 | tf_op jit(solution)/shard_map/ppermute | solution.py:374
  76.1 1.3 %collective-permute-start.16 = (f32[96,256]{1,0:T(8,128)S(1)}, f32[96,256]{1,0:T(8,128)S(1)}, u32[]{:S(2)}, u32[]{:S(2)}) collective-permute-start(f32[96,256]{1,0:T(8,128)S(1)} %add.27), channel_id=1, source_target_pairs={{0,2},{1,3},{2,0},{3,1},{4,6},{5,7},{6,4},{7,5},{8,10},{9,11},{10,... | collective-permute-start | bytes 294920 | tf_op jit(solution)/shard_map/ppermute | solution.py:374
  77.4 2.0 %collective-permute-start.15 = (f32[96,256]{1,0:T(8,128)S(1)}, f32[96,256]{1,0:T(8,128)S(1)}, u32[]{:S(2)}, u32[]{:S(2)}) collective-permute-start(f32[96,256]{1,0:T(8,128)S(1)} %add.27), channel_id=1, source_target_pairs={{0,4},{4,0},{8,12},{12,8},{1,5},{5,1},{9,13},{13,9},{2,6},{6,2},{1... | collective-permute-start | bytes 294920 | tf_op jit(solution)/shard_map/ppermute | solution.py:374
  79.3 4.8 %collective-permute-done.13.other = f32[256,512]{1,0:T(8,128)S(1)} collective-permute-done((f32[256,512]{1,0:T(8,128)S(1)}, f32[256,512]{1,0:T(8,128)S(1)}, u32[]{:S(2)}, u32[]{:S(2)}) %collective-permute-start.13) | collective-permute-done | bytes 524320 | tf_op jit(solution)/shard_map/ppermute | solution.py:374
  84.1 1.0 %collective-permute-done.16 = f32[96,256]{1,0:T(8,128)S(1)} collective-permute-done((f32[96,256]{1,0:T(8,128)S(1)}, f32[96,256]{1,0:T(8,128)S(1)}, u32[]{:S(2)}, u32[]{:S(2)}) %collective-permute-start.16) | collective-permute-done | bytes 98336 | tf_op jit(solution)/shard_map/ppermute | solution.py:374
  85.3 1.0 %column_rows.1 = (f32[256,256]{1,0:T(8,128)}, f32[256,256]{1,0:T(8,128)}) custom-call(s32[48,256]{1,0:T(8,128)S(1)} %broadcast_in_dim.2.at, f32[2,256,512]{2,1,0:T(8,128)S(1)} %band_product.5.keep, f32[2,256,512]{2,1,0:T(8,128)S(1)} %collective-permute-done.9.got, f32[256,512]{1,0:T(8,128)S(1)} %collective-permute-done.13.other, f32[256,256]{1,0:T(8,128)S(1)} %copy-done.2), custom_call_target="tpu_custom_call" | custom-call | tf_op jit(solution)/shard_map/column_rows/pallas_call | solution.py:306
  86.3 0.7 collective-permute-done.18.second
  87.0 1.4 %small_blocks.1 = (f32[256,256]{1,0:T(8,128)}, f32[256,256]{1,0:T(8,128)}, f32[256,256]{1,0:T(8,128)}) custom-call(f32[256,256]{1,0:T(8,128)S(1)} %copy-done.2, f32[256,256]{1,0:T(8,128)S(1)} %copy-done.3, f32[256,256]{1,0:T(8,128)S(1)} %copy-done.4, f32[384,256]{1,0:T(8,128)S(1)} %constant_dynamic-update-slice_fusion.first, ...), custom_call_target="tpu_custom_call" | custom-call | tf_op jit(solution)/shard_map/small_blocks/pallas_call | solution.py:346
  (39 shorter events, 3.4 us)
Async XLA Ops:
  0.6 1.9 %collective-permute-start.2 = (f32[256,256]{1,0:T(8,128)}, f32[256,256]{1,0:T(8,128)S(1)}, u32[]{:S(2)}, u32[]{:S(2)}) collective-permute-start(f32[256,256]{1,0:T(8,128)} %refs_0_.1), channel_id=1, source_target_pairs={{0,1},{1,0},{2,3},{3,2},{4,5},{5,4},{6,7},{7,6},{8,9},{9,8},{10,11... | collective-permute-start | bytes 786440 | tf_op jit(solution)/shard_map/ppermute | solution.py:374
  1.1 1.7 %collective-permute-start.3 = (f32[256,256]{1,0:T(8,128)}, f32[256,256]{1,0:T(8,128)S(1)}, u32[]{:S(2)}, u32[]{:S(2)}) collective-permute-start(f32[256,256]{1,0:T(8,128)} %refs_1_.1), channel_id=1, source_target_pairs={{0,1},{1,0},{2,3},{3,2},{4,5},{5,4},{6,7},{7,6},{8,9},{9,8},{10,11... | collective-permute-start | bytes 786440 | tf_op jit(solution)/shard_map/ppermute | solution.py:374
  3.0 42.0 %collective-permute-start.6 = (f32[1024,256]{1,0:T(8,128)S(1)}, f32[1024,256]{1,0:T(8,128)S(1)}, u32[]{:S(2)}, u32[]{:S(2)}) collective-permute-start(f32[1024,256]{1,0:T(8,128)S(1)} %stack_rows.3.here), channel_id=1, source_target_pairs={{0,8},{1,12},{2,0},{3,4},{4,9},{5,13},{6,1},{7,5},{8,10},{9,14},{1... | collective-permute-start | bytes 3145736 | tf_op jit(solution)/shard_map/ppermute | solution.py:385
  7.0 39.9 %collective-permute-start.7 = (f32[1024,256]{1,0:T(8,128)S(1)}, f32[1024,256]{1,0:T(8,128)S(1)}, u32[]{:S(2)}, u32[]{:S(2)}) collective-permute-start(f32[1024,256]{1,0:T(8,128)S(1)} %stack_rows.3.here), channel_id=1, source_target_pairs={{0,0},{1,4},{2,8},{3,12},{4,1},{5,5},{6,9},{7,13},{8,2},{9,6},{10,... | collective-permute-start | bytes 3145736 | tf_op jit(solution)/shard_map/ppermute | solution.py:385
  7.7 33.4 %collective-permute-start = (f32[256,256]{1,0:T(8,128)}, f32[256,256]{1,0:T(8,128)S(1)}, u32[]{:S(2)}, u32[]{:S(2)}) collective-permute-start(f32[256,256]{1,0:T(8,128)} %refs_0_.1), channel_id=1, source_target_pairs={{0,2},{1,3},{2,0},{3,1},{4,6},{5,7},{6,4},{7,5},{8,10},{9,11},{10,... | collective-permute-start | bytes 786440 | tf_op jit(solution)/shard_map/ppermute | solution.py:374
  11.9 29.2 %collective-permute-start.1 = (f32[256,256]{1,0:T(8,128)}, f32[256,256]{1,0:T(8,128)S(1)}, u32[]{:S(2)}, u32[]{:S(2)}) collective-permute-start(f32[256,256]{1,0:T(8,128)} %refs_1_.1), channel_id=1, source_target_pairs={{0,2},{1,3},{2,0},{3,1},{4,6},{5,7},{6,4},{7,5},{8,10},{9,11},{10,... | collective-permute-start | bytes 786440 | tf_op jit(solution)/shard_map/ppermute | solution.py:374
  13.5 2.2 %copy-start = (f32[1024,1024]{1,0:T(8,128)S(1)}, f32[1024,1024]{1,0:T(8,128)}, u32[]{:S(2)}) copy-start(f32[1024,1024]{1,0:T(8,128)} %known.7) | copy-start | bytes 12582916
  15.7 27.4 %copy-start.1 = (f32[1024,1024]{1,0:T(8,128)S(1)}, f32[1024,1024]{1,0:T(8,128)}, u32[]{:S(2)}) copy-start(f32[1024,1024]{1,0:T(8,128)} %known.7) | copy-start | bytes 12582916
  41.2 1.5 %collective-permute-start.4 = (f32[256,256]{1,0:T(8,128)S(1)}, f32[256,256]{1,0:T(8,128)S(1)}, u32[]{:S(2)}, u32[]{:S(2)}) collective-permute-start(f32[256,256]{1,0:T(8,128)S(1)} %collective-permute-done.two), channel_id=1, source_target_pairs={{0,1},{1,0},{2,3},{3,2},{4,5},{5,4},{6,7},{7,6},{8,9},{9,8},{10,11... | collective-permute-start | bytes 786440 | tf_op jit(solution)/shard_map/ppermute | solution.py:374
  41.2 1.9 %collective-permute-start.5 = (f32[256,256]{1,0:T(8,128)S(1)}, f32[256,256]{1,0:T(8,128)S(1)}, u32[]{:S(2)}, u32[]{:S(2)}) collective-permute-start(f32[256,256]{1,0:T(8,128)S(1)} %collective-permute-done.1.one), channel_id=1, source_target_pairs={{0,1},{1,0},{2,3},{3,2},{4,5},{5,4},{6,7},{7,6},{8,9},{9,8},{10,11... | collective-permute-start | bytes 786440 | tf_op jit(solution)/shard_map/ppermute | solution.py:374
  47.9 1.8 %collective-permute-start.8 = (f32[384,256]{1,0:T(8,128)S(1)}, f32[384,256]{1,0:T(8,128)S(1)}, u32[]{:S(2)}, u32[]{:S(2)}) collective-permute-start(f32[384,256]{1,0:T(8,128)S(1)} %get-tuple-element.35), channel_id=1, source_target_pairs={{0,1},{1,0},{2,3},{3,2},{4,5},{5,4},{6,7},{7,6},{8,9},{9,8},{10,11... | collective-permute-start | bytes 1179656 | tf_op jit(solution)/shard_map/ppermute | solution.py:374
  49.8 18.0 %collective-permute-start.9 = (f32[2,256,512]{2,1,0:T(8,128)S(1)}, f32[2,256,512]{2,1,0:T(8,128)S(1)}, u32[]{:S(2)}, u32[]{:S(2)}) collective-permute-start(f32[2,256,512]{2,1,0:T(8,128)S(1)} %band_product.4), channel_id=1, source_target_pairs={{0,1},{1,0},{2,3},{3,2},{4,5},{5,4},{6,7},{7,6},{8,9},{9,8},{10,11... | collective-permute-start | bytes 3145736 | tf_op jit(solution)/shard_map/ppermute | solution.py:374
  50.0 14.4 %collective-permute-start.12 = (f32[96,256]{1,0:T(8,128)S(1)}, f32[96,256]{1,0:T(8,128)S(1)}, u32[]{:S(2)}, u32[]{:S(2)}) collective-permute-start(f32[96,256]{1,0:T(8,128)S(1)} %get-tuple-element.49), channel_id=1, source_target_pairs={{0,4},{4,0},{8,12},{12,8},{1,5},{5,1},{9,13},{13,9},{2,6},{6,2},{1... | collective-permute-start | bytes 294920 | tf_op jit(solution)/shard_map/ppermute | solution.py:374
  58.4 8.1 %collective-permute-start.11 = (f32[96,256]{1,0:T(8,128)S(1)}, f32[96,256]{1,0:T(8,128)S(1)}, u32[]{:S(2)}, u32[]{:S(2)}) collective-permute-start(f32[96,256]{1,0:T(8,128)S(1)} %get-tuple-element.50), channel_id=1, source_target_pairs={{0,2},{1,3},{2,0},{3,1},{4,6},{5,7},{6,4},{7,5},{8,10},{9,11},{10,... | collective-permute-start | bytes 294920 | tf_op jit(solution)/shard_map/ppermute | solution.py:374
  62.0 23.3 %copy-start.2 = (f32[256,256]{1,0:T(8,128)S(1)}, f32[256,256]{1,0:T(8,128)}, u32[]{:S(2)}) copy-start(f32[256,256]{1,0:T(8,128)} %top.3) | copy-start | bytes 786436
  62.0 5.7 %collective-permute-start.10 = (f32[96,256]{1,0:T(8,128)S(1)}, f32[96,256]{1,0:T(8,128)S(1)}, u32[]{:S(2)}, u32[]{:S(2)}) collective-permute-start(f32[96,256]{1,0:T(8,128)S(1)} %get-tuple-element.51), channel_id=1, source_target_pairs={{0,6},{1,7},{2,4},{3,5},{4,2},{5,3},{6,0},{7,1},{8,14},{9,15},{10,... | collective-permute-start | bytes 294920 | tf_op jit(solution)/shard_map/ppermute | solution.py:381
  64.4 22.6 %copy-start.3 = (f32[256,256]{1,0:T(8,128)S(1)}, f32[256,256]{1,0:T(8,128)}, u32[]{:S(2)}) copy-start(f32[256,256]{1,0:T(8,128)} %inner_two.1) | copy-start | bytes 786436
  64.4 22.6 %copy-start.4 = (f32[256,256]{1,0:T(8,128)S(1)}, f32[256,256]{1,0:T(8,128)}, u32[]{:S(2)}) copy-start(f32[256,256]{1,0:T(8,128)} %inner_one.1) | copy-start | bytes 786436
  67.8 16.3 %collective-permute-start.13 = (f32[256,512]{1,0:T(8,128)S(1)}, f32[256,512]{1,0:T(8,128)S(1)}, u32[]{:S(2)}, u32[]{:S(2)}) collective-permute-start(f32[256,512]{1,0:T(8,128)S(1)} %fusion), channel_id=1, source_target_pairs={{0,2},{1,3},{2,0},{3,1},{4,6},{5,7},{6,4},{7,5},{8,10},{9,11},{10,... | collective-permute-start | bytes 1572872 | tf_op jit(solution)/shard_map/ppermute | solution.py:374
  69.1 6.7 %collective-permute-start.14 = (f32[96,256]{1,0:T(8,128)S(1)}, f32[96,256]{1,0:T(8,128)S(1)}, u32[]{:S(2)}, u32[]{:S(2)}) collective-permute-start(f32[96,256]{1,0:T(8,128)S(1)} %fusion.1), channel_id=1, source_target_pairs={{0,8},{4,12},{8,0},{12,4},{1,9},{5,13},{9,1},{13,5},{2,10},{6,14},... | collective-permute-start | bytes 294920 | tf_op jit(solution)/shard_map/ppermute | solution.py:374
  75.8 9.4 %collective-permute-start.17 = (f32[96,256]{1,0:T(8,128)S(1)}, f32[96,256]{1,0:T(8,128)S(1)}, u32[]{:S(2)}, u32[]{:S(2)}) collective-permute-start(f32[96,256]{1,0:T(8,128)S(1)} %add.27), channel_id=1, source_target_pairs={{0,6},{1,7},{2,4},{3,5},{4,2},{5,3},{6,0},{7,1},{8,14},{9,15},{10,... | collective-permute-start | bytes 294920 | tf_op jit(solution)/shard_map/ppermute | solution.py:381
  76.1 9.1 %collective-permute-start.16 = (f32[96,256]{1,0:T(8,128)S(1)}, f32[96,256]{1,0:T(8,128)S(1)}, u32[]{:S(2)}, u32[]{:S(2)}) collective-permute-start(f32[96,256]{1,0:T(8,128)S(1)} %add.27), channel_id=1, source_target_pairs={{0,2},{1,3},{2,0},{3,1},{4,6},{5,7},{6,4},{7,5},{8,10},{9,11},{10,... | collective-permute-start | bytes 294920 | tf_op jit(solution)/shard_map/ppermute | solution.py:374
  77.4 6.7 %collective-permute-start.15 = (f32[96,256]{1,0:T(8,128)S(1)}, f32[96,256]{1,0:T(8,128)S(1)}, u32[]{:S(2)}, u32[]{:S(2)}) collective-permute-start(f32[96,256]{1,0:T(8,128)S(1)} %add.27), channel_id=1, source_target_pairs={{0,4},{4,0},{8,12},{12,8},{1,5},{5,1},{9,13},{13,9},{2,6},{6,2},{1... | collective-permute-start | bytes 294920 | tf_op jit(solution)/shard_map/ppermute | solution.py:374
  85.2 1.8 %collective-permute-start.18 = (f32[384,256]{1,0:T(8,128)S(1)}, f32[384,256]{1,0:T(8,128)S(1)}, u32[]{:S(2)}, u32[]{:S(2)}) collective-permute-start(f32[384,256]{1,0:T(8,128)S(1)} %constant_dynamic-update-slice_fusion.first), channel_id=1, source_target_pairs={{0,1},{1,0},{2,3},{3,2},{4,5},{5,4},{6,7},{7,6},{8,9},{9,8},{10,11... | collective-permute-start | bytes 1179656 | tf_op jit(solution)/shard_map/ppermute | solution.py:374
